TPU v7x, 256 devices: a whole 4x4x8 slice. The times are simulated.
256 devices in a mesh: blk: 64 (over x_lo, z, y), rep: 4 (over x_hi, core).
Axes of the slice: x: 4 (x_hi: 2, x_lo: 2; x = x_hi * 2 + x_lo), y: 4, z: 8, core: 2. Of those that a mesh axis runs over, the one named last changes fastest.
Arguments:
- image_emb: bfloat16 [65536, 1024], P(('blk', 'rep')), may hold values from -640 to 640
- text_emb: bfloat16 [65536, 1024], P('blk'), may hold values from -9 to 9
- logit_scale: float32 [1], replicated, may hold values from 0.04 to 0.08
Outputs:
- grad_image: float32 [65536, 1024], P(('blk', 'rep'))
- grad_text: float32 [65536, 1024], P(('blk', 'rep'))
- loss: float32 [1], replicated
All inputs are finite; a program needn't handle non-finite values.
Results may differ from a plain program's by a relative error of at most 0.002.
Values may be sent and summed in bfloat16 or wider, within the bound.
No kernel may reach another device: no remote copies, remote signals or barrier semaphores. Data moves between devices by JAX's collectives and lax.ppermute only.
A program may use at most 64 MiB of HBM per device.

v0:
```python
import jax
import jax.numpy as jnp
from jax import lax
from jax.sharding import PartitionSpec as P

STEPS = 4


def from_behind(block, axis, distance):
    devices = range(lax.axis_size(axis))
    route = [((i - distance) % len(devices), i) for i in devices]
    return lax.ppermute(block, axis, route)


def joined(part, axis, combine):
    gathered = jax.tree.map(lambda a: lax.all_gather(a, axis), part)

    def take(source):
        return jax.tree.map(lambda a: lax.dynamic_index_in_dim(a, source, 0, False), gathered)

    return lax.fori_loop(
        1, lax.axis_size(axis), lambda source, state: combine(state, take(source)), take(0)
    )


def pair_logits(images, captions, multiplier):
    product = lax.dot_general(
        images, captions, (((1,), (1,)), ((), ())), preferred_element_type=jnp.float32
    )
    return multiplier * product


def reduce_stats(logits, along):
    highest = jnp.max(logits, axis=along)
    summed = jnp.sum(jnp.exp(logits - jnp.expand_dims(highest, along)), axis=along)
    return (highest, summed)


def join_stats(former, latter):
    highest = jnp.maximum(former[0], latter[0])
    summed = former[1] * jnp.exp(former[0] - highest) + latter[1] * jnp.exp(latter[0] - highest)
    return (highest, summed)


def beside_all(values, offset):
    return from_behind(values, "blk", offset)


def carried(former, latter, offset):
    return from_behind((former, latter), "blk", offset)


def send_home(values, offset):
    return from_behind(values, "blk", offset)


def per_device(image_emb, text_emb, logit_scale):
    row_count = image_emb.shape[0]
    block_rows = text_emb.shape[0]
    multiplier = logit_scale[0]
    rep_index = lax.axis_index("rep")
    pair_count = row_count * lax.axis_size("blk") * lax.axis_size("rep")
    step_by = 1
    moving = text_emb
    moving_stats = None
    staying_stats = None
    for position in range(STEPS):
        if position > 0:
            moving = beside_all(moving, step_by)
            moving_stats = carried(moving_stats[0], moving_stats[1], step_by)
        images = image_emb
        captions = moving
        logits = pair_logits(images, captions, multiplier)
        row_part = reduce_stats(logits, 1)
        column_part = reduce_stats(logits, 0)
        if position == 0:
            moving_stats = column_part
            staying_stats = row_part
        else:
            moving_stats = join_stats(moving_stats, column_part)
            staying_stats = join_stats(staying_stats, row_part)
    column_high, column_sum = joined((moving_stats[0], moving_stats[1]), "rep", join_stats)
    column_lse = column_high + jnp.log(column_sum)
    row_lse = staying_stats[0] + jnp.log(staying_stats[1])
    own_captions = lax.dynamic_slice_in_dim(text_emb, rep_index * row_count, row_count, 0)
    matched = multiplier * jnp.einsum(
        "nd,nd->n", image_emb, own_captions, preferred_element_type=jnp.float32
    )
    column_share = lax.dynamic_slice_in_dim(column_lse, rep_index * row_count, row_count, 0)
    local_loss = jnp.sum(row_lse) + jnp.sum(column_share) - 2.0 * jnp.sum(matched)
    loss_sum = lax.psum(local_loss, ("blk", "rep"))
    loss_value = jnp.reshape(loss_sum / (2.0 * pair_count), (1,))
    moving_lse = column_lse
    moving_lse = send_home(moving_lse, -(STEPS - 1) * step_by)
    moving = text_emb
    offsets = list(range(STEPS))
    moving_grad = jnp.zeros(moving.shape, jnp.float32)
    staying_grad = jnp.zeros(image_emb.shape, jnp.float32)
    column_ids = lax.broadcasted_iota(jnp.int32, (row_count, block_rows), 1)
    row_ids = lax.broadcasted_iota(jnp.int32, (row_count, block_rows), 0) + rep_index * row_count
    for position, offset in enumerate(offsets):
        if position > 0:
            moving = beside_all(moving, step_by)
            moving_lse, moving_grad = carried(moving_lse, moving_grad, step_by)
        images = image_emb
        captions = moving
        logits = pair_logits(images, captions, multiplier)
        averaged = 0.5 * (
            jnp.exp(logits - row_lse[:, None]) + jnp.exp(logits - moving_lse[None, :])
        )
        if offset == 0:
            averaged = averaged - (column_ids == row_ids).astype(jnp.float32)
        weights = averaged.astype(jnp.bfloat16)
        image_term = multiplier * jnp.dot(weights, captions, preferred_element_type=jnp.float32)
        text_term = multiplier * lax.dot_general(
            weights, images, (((0,), (0,)), ((), ())), preferred_element_type=jnp.float32
        )
        moving_grad = moving_grad + text_term
        staying_grad = staying_grad + image_term
    moving_grad = send_home(moving_grad, -(STEPS - 1) * step_by)
    text_grad = lax.psum_scatter(moving_grad, "rep", scatter_dimension=0, tiled=True)
    return (staying_grad, text_grad, loss_value)


def solution(mesh):
    placed = (P(("blk", "rep"), None), P("blk", None), P())
    return jax.shard_map(
        per_device,
        mesh=mesh,
        in_specs=placed,
        out_specs=(P(("blk", "rep"), None), P(("blk", "rep"), None), P()),
        check_vma=False,
    )
```

profile of v0, /device:TPU:16, one launch (start us, length us, event | category | flops | bytes accessed | tf_op | source)
XLA Modules:
  0.0 673.8 jit_solution(9149401139867334695)
XLA Ops:
  7.2 1.4 collective-permute-start
  8.6 46.3 %collective-permute-done = bf16[1024,1024]{1,0:T(8,128)(2,1)S(1)} collective-permute-done((bf16[1024,1024]{1,0:T(8,128)(2,1)}, bf16[1024,1024]{1,0:T(8,128)(2,1)S(1)}, u32[]{:S(2)}, u32[]{:S(2)}) %collective-permute-start) | collective-permute-done | bytes 2097184 | tf_op jit(solution)/shard_map/ppermute | solution.py:12
  54.9 1.3 collective-permute-start.1
  56.2 45.3 %collective-permute-done.1 = bf16[1024,1024]{1,0:T(8,128)(2,1)} collective-permute-done((bf16[1024,1024]{1,0:T(8,128)(2,1)S(1)}, bf16[1024,1024]{1,0:T(8,128)(2,1)}, u32[]{:S(2)}, u32[]{:S(2)}) %collective-permute-start.1) | collective-permute-done | bytes 2097184 | tf_op jit(solution)/shard_map/ppermute | solution.py:12
  101.5 2.4 collective-permute-start.2
  104.5 2.6 fusion.11
  107.2 4.8 collective-permute-start.3
  112.4 2.4 fusion.12
  115.3 38.0 %collective-permute-done.6 = f32[1024]{0:T(1024)S(1)} collective-permute-done((f32[1024]{0:T(1024)S(1)}, f32[1024]{0:T(1024)S(1)}, u32[]{:S(2)}, u32[]{:S(2)}) %collective-permute-start.6) | collective-permute-done | bytes 4128 | tf_op jit(solution)/shard_map/ppermute | solution.py:12
  153.4 3.3 collective-permute-start.4
  156.7 2.4 fusion.13
  159.6 1.1 collective-permute-done.7
  160.8 1.8 collective-permute-start.5
  162.6 2.4 fusion.14
  166.4 1.9 collective-permute-done.8
  168.5 6.7 all-gather.1
  175.2 6.7 all-gather
  182.1 12.4 %collective-permute-start.9 = (f32[1024]{0:T(1024)S(1)}, f32[1024]{0:T(1024)S(1)}, u32[]{:S(2)}, u32[]{:S(2)}) collective-permute-start(f32[1024]{0:T(1024)S(1)} %log_add_fusion), channel_id=1, source_target_pairs={{12,0},{16,4},{20,8},{24,12},{28,16},{32,20},{36,24},{40,28},{44,3... | collective-permute-start | bytes 12296 | tf_op jit(solution)/shard_map/ppermute | solution.py:12
  195.7 1.1 convolution_multiply_fusion
  196.8 1.1 collective-permute-start.13
  198.0 91.1 %collective-permute-done.10 = f32[1024]{0:T(1024)S(1)} collective-permute-done((f32[1024]{0:T(1024)S(1)}, f32[1024]{0:T(1024)S(1)}, u32[]{:S(2)}, u32[]{:S(2)}) %collective-permute-start.10) | collective-permute-done | bytes 4128 | tf_op jit(solution)/shard_map/ppermute | solution.py:12
  290.9 2.4 collective-permute-start.11
  293.3 88.1 %collective-permute-done.11 = f32[1024]{0:T(1024)S(1)} collective-permute-done((f32[1024]{0:T(1024)S(1)}, f32[1024]{0:T(1024)S(1)}, u32[]{:S(2)}, u32[]{:S(2)}) %collective-permute-start.11) | collective-permute-done | bytes 4128 | tf_op jit(solution)/shard_map/ppermute | solution.py:12
  383.3 4.6 collective-permute-start.12
  387.9 88.4 %collective-permute-done.12 = f32[1024]{0:T(1024)S(1)} collective-permute-done((f32[1024]{0:T(1024)S(1)}, f32[1024]{0:T(1024)S(1)}, u32[]{:S(2)}, u32[]{:S(2)}) %collective-permute-start.12) | collective-permute-done | bytes 4128 | tf_op jit(solution)/shard_map/ppermute | solution.py:12
  477.2 8.6 %collective-permute-start.16 = (f32[1024,1024]{1,0:T(8,128)S(1)}, f32[1024,1024]{1,0:T(8,128)}, u32[]{:S(2)}, u32[]{:S(2)}) collective-permute-start(f32[1024,1024]{1,0:T(8,128)S(1)} %multiply_add_fusion.1), channel_id=1, source_target_pairs={{12,0},{16,4},{20,8},{24,12},{28,16},{32,20},{36,24},{40,28},{44,3... | collective-permute-start | bytes 12582920 | tf_op jit(solution)/shard_map/ppermute | solution.py:12
  485.8 86.4 %collective-permute-done.16 = f32[1024,1024]{1,0:T(8,128)} collective-permute-done((f32[1024,1024]{1,0:T(8,128)S(1)}, f32[1024,1024]{1,0:T(8,128)}, u32[]{:S(2)}, u32[]{:S(2)}) %collective-permute-start.16) | collective-permute-done | bytes 4194336 | tf_op jit(solution)/shard_map/ppermute | solution.py:12
  572.2 1.3 fusion.1
  576.9 78.2 %psum.7 = f32[]{:T(128)} all-reduce(f32[]{:T(128)S(6)} %sub.250), channel_id=1, replica_groups=mesh['blk'=64,'rep'=4] {'blk','rep'}, use_global_device_ids=true, to_apply=%region_22.23 | all-reduce | flops 1 | bytes 8 | tf_op jit(solution)/shard_map/psum | solution.py:91
  655.7 2.7 fusion.10
  659.7 2.6 convolution_add_fusion.1
  662.3 3.5 fusion
  (62 shorter events, 12.0 us)
Async XLA Ops:
  7.2 658.6 %reduce-scatter.2.cloned.1.call-start = ((), (), s32[]{:S(2)}) async-start(), calls=%async_computation.1 | async-start | bytes 5242880 | tf_op jit(solution)/shard_map/reduce_scatter | solution.py:121
  7.2 47.7 %collective-permute-start = (bf16[1024,1024]{1,0:T(8,128)(2,1)}, bf16[1024,1024]{1,0:T(8,128)(2,1)S(1)}, u32[]{:S(2)}, u32[]{:S(2)}) collective-permute-start(bf16[1024,1024]{1,0:T(8,128)(2,1)} %param.6), channel_id=1, source_target_pairs={{252,0},{0,4},{4,8},{8,12},{12,16},{16,20},{20,24},{24,28},{28,32}... | collective-permute-start | bytes 6291464 | tf_op jit(solution)/shard_map/ppermute | solution.py:12
  54.9 49.6 %copy-start.7 = (bf16[1024,1024]{1,0:T(8,128)(2,1)}, bf16[1024,1024]{1,0:T(8,128)(2,1)S(1)}, u32[]{:S(2)}) copy-start(bf16[1024,1024]{1,0:T(8,128)(2,1)S(1)} %collective-permute-done) | copy-start | bytes 6291460
  54.9 46.6 %collective-permute-start.1 = (bf16[1024,1024]{1,0:T(8,128)(2,1)S(1)}, bf16[1024,1024]{1,0:T(8,128)(2,1)}, u32[]{:S(2)}, u32[]{:S(2)}) collective-permute-start(bf16[1024,1024]{1,0:T(8,128)(2,1)S(1)} %collective-permute-done), channel_id=1, source_target_pairs={{252,0},{0,4},{4,8},{8,12},{12,16},{16,20},{20,24},{24,28},{28,32}... | collective-permute-start | bytes 6291464 | tf_op jit(solution)/shard_map/ppermute | solution.py:12
  101.5 61.2 %collective-permute-start.2 = (bf16[1024,1024]{1,0:T(8,128)(2,1)}, bf16[1024,1024]{1,0:T(8,128)(2,1)}, u32[]{:S(2)}, u32[]{:S(2)}) collective-permute-start(bf16[1024,1024]{1,0:T(8,128)(2,1)} %collective-permute-done.1), channel_id=1, source_target_pairs={{252,0},{0,4},{4,8},{8,12},{12,16},{16,20},{20,24},{24,28},{28,32}... | collective-permute-start | bytes 6291464 | tf_op jit(solution)/shard_map/ppermute | solution.py:12
  104.5 7.9 %copy-start = (bf16[256,1024]{1,0:T(8,128)(2,1)S(1)}, bf16[256,1024]{1,0:T(8,128)(2,1)}, u32[]{:S(2)}) copy-start(bf16[256,1024]{1,0:T(8,128)(2,1)} %param.5) | copy-start | bytes 1572868
  107.2 46.1 %collective-permute-start.3 = (f32[1024]{0:T(1024)S(1)}, f32[1024]{0:T(1024)S(1)}, u32[]{:S(2)}, u32[]{:S(2)}) collective-permute-start(f32[1024]{0:T(1024)S(1)} %get-tuple-element.141), channel_id=1, source_target_pairs={{252,0},{0,4},{4,8},{8,12},{12,16},{16,20},{20,24},{24,28},{28,32}... | collective-permute-start | bytes 12296 | tf_op jit(solution)/shard_map/ppermute | solution.py:12
  112.3 41.0 %collective-permute-start.6 = (f32[1024]{0:T(1024)S(1)}, f32[1024]{0:T(1024)S(1)}, u32[]{:S(2)}, u32[]{:S(2)}) collective-permute-start(f32[1024]{0:T(1024)S(1)} %get-tuple-element.139), channel_id=1, source_target_pairs={{252,0},{0,4},{4,8},{8,12},{12,16},{16,20},{20,24},{24,28},{28,32}... | collective-permute-start | bytes 12296 | tf_op jit(solution)/shard_map/ppermute | solution.py:12
  153.3 7.3 %collective-permute-start.7 = (f32[1024]{0:T(1024)S(1)}, f32[1024]{0:T(1024)S(1)}, u32[]{:S(2)}, u32[]{:S(2)}) collective-permute-start(f32[1024]{0:T(1024)S(1)} %get-tuple-element.172), channel_id=1, source_target_pairs={{252,0},{0,4},{4,8},{8,12},{12,16},{16,20},{20,24},{24,28},{28,32}... | collective-permute-start | bytes 12296 | tf_op jit(solution)/shard_map/ppermute | solution.py:12
  153.4 7.3 %collective-permute-start.4 = (f32[1024]{0:T(1024)S(1)}, f32[1024]{0:T(1024)S(1)}, u32[]{:S(2)}, u32[]{:S(2)}) collective-permute-start(f32[1024]{0:T(1024)S(1)} %get-tuple-element.173), channel_id=1, source_target_pairs={{252,0},{0,4},{4,8},{8,12},{12,16},{16,20},{20,24},{24,28},{28,32}... | collective-permute-start | bytes 12296 | tf_op jit(solution)/shard_map/ppermute | solution.py:12
  159.2 5.9 copy-start.1
  160.7 7.6 %collective-permute-start.8 = (f32[1024]{0:T(1024)S(1)}, f32[1024]{0:T(1024)S(1)}, u32[]{:S(2)}, u32[]{:S(2)}) collective-permute-start(f32[1024]{0:T(1024)S(1)} %get-tuple-element.170), channel_id=1, source_target_pairs={{252,0},{0,4},{4,8},{8,12},{12,16},{16,20},{20,24},{24,28},{28,32}... | collective-permute-start | bytes 12296 | tf_op jit(solution)/shard_map/ppermute | solution.py:12
  160.8 7.6 %collective-permute-start.5 = (f32[1024]{0:T(1024)S(1)}, f32[1024]{0:T(1024)S(1)}, u32[]{:S(2)}, u32[]{:S(2)}) collective-permute-start(f32[1024]{0:T(1024)S(1)} %get-tuple-element.171), channel_id=1, source_target_pairs={{252,0},{0,4},{4,8},{8,12},{12,16},{16,20},{20,24},{24,28},{28,32}... | collective-permute-start | bytes 12296 | tf_op jit(solution)/shard_map/ppermute | solution.py:12
  165.1 1.0 copy-start.4
  182.1 13.7 %collective-permute-start.9 = (f32[1024]{0:T(1024)S(1)}, f32[1024]{0:T(1024)S(1)}, u32[]{:S(2)}, u32[]{:S(2)}) collective-permute-start(f32[1024]{0:T(1024)S(1)} %log_add_fusion), channel_id=1, source_target_pairs={{12,0},{16,4},{20,8},{24,12},{28,16},{32,20},{36,24},{40,28},{44,3... | collective-permute-start | bytes 12296 | tf_op jit(solution)/shard_map/ppermute | solution.py:12
  196.8 92.3 %collective-permute-start.13 = (f32[1024,1024]{1,0:T(8,128)S(1)}, f32[1024,1024]{1,0:T(8,128)S(1)}, u32[]{:S(2)}, u32[]{:S(2)}) collective-permute-start(f32[1024,1024]{1,0:T(8,128)S(1)} %convolution_multiply_fusion), channel_id=1, source_target_pairs={{252,0},{0,4},{4,8},{8,12},{12,16},{16,20},{20,24},{24,28},{28,32}... | collective-permute-start | bytes 12582920 | tf_op jit(solution)/shard_map/ppermute | solution.py:12
  197.9 91.2 %collective-permute-start.10 = (f32[1024]{0:T(1024)S(1)}, f32[1024]{0:T(1024)S(1)}, u32[]{:S(2)}, u32[]{:S(2)}) collective-permute-start(f32[1024]{0:T(1024)S(1)} %collective-permute-done.9), channel_id=1, source_target_pairs={{252,0},{0,4},{4,8},{8,12},{12,16},{16,20},{20,24},{24,28},{28,32}... | collective-permute-start | bytes 12296 | tf_op jit(solution)/shard_map/ppermute | solution.py:12
  289.1 92.3 %copy-start.2 = (f32[256,1024]{1,0:T(8,128)S(1)}, f32[256,1024]{1,0:T(8,128)}, u32[]{:S(2)}) copy-start(f32[256,1024]{1,0:T(8,128)} %copy-done.1) | copy-start | bytes 3145732
  290.1 91.4 %collective-permute-start.14 = (f32[1024,1024]{1,0:T(8,128)S(1)}, f32[1024,1024]{1,0:T(8,128)S(1)}, u32[]{:S(2)}, u32[]{:S(2)}) collective-permute-start(f32[1024,1024]{1,0:T(8,128)S(1)} %multiply_add_fusion.3), channel_id=1, source_target_pairs={{252,0},{0,4},{4,8},{8,12},{12,16},{16,20},{20,24},{24,28},{28,32}... | collective-permute-start | bytes 12582920 | tf_op jit(solution)/shard_map/ppermute | solution.py:12
  290.9 90.5 %collective-permute-start.11 = (f32[1024]{0:T(1024)S(1)}, f32[1024]{0:T(1024)S(1)}, u32[]{:S(2)}, u32[]{:S(2)}) collective-permute-start(f32[1024]{0:T(1024)S(1)} %collective-permute-done.10), channel_id=1, source_target_pairs={{252,0},{0,4},{4,8},{8,12},{12,16},{16,20},{20,24},{24,28},{28,32}... | collective-permute-start | bytes 12296 | tf_op jit(solution)/shard_map/ppermute | solution.py:12
  381.4 94.8 %copy-start.5 = (f32[256,1024]{1,0:T(8,128)S(1)}, f32[256,1024]{1,0:T(8,128)}, u32[]{:S(2)}) copy-start(f32[256,1024]{1,0:T(8,128)} %copy-done.4) | copy-start | bytes 3145732
  382.4 93.8 %collective-permute-start.15 = (f32[1024,1024]{1,0:T(8,128)S(1)}, f32[1024,1024]{1,0:T(8,128)S(1)}, u32[]{:S(2)}, u32[]{:S(2)}) collective-permute-start(f32[1024,1024]{1,0:T(8,128)S(1)} %multiply_add_fusion.2), channel_id=1, source_target_pairs={{252,0},{0,4},{4,8},{8,12},{12,16},{16,20},{20,24},{24,28},{28,32}... | collective-permute-start | bytes 12582920 | tf_op jit(solution)/shard_map/ppermute | solution.py:12
  383.3 93.0 %collective-permute-start.12 = (f32[1024]{0:T(1024)S(1)}, f32[1024]{0:T(1024)S(1)}, u32[]{:S(2)}, u32[]{:S(2)}) collective-permute-start(f32[1024]{0:T(1024)S(1)} %collective-permute-done.11), channel_id=1, source_target_pairs={{252,0},{0,4},{4,8},{8,12},{12,16},{16,20},{20,24},{24,28},{28,32}... | collective-permute-start | bytes 12296 | tf_op jit(solution)/shard_map/ppermute | solution.py:12
  477.2 95.0 %collective-permute-start.16 = (f32[1024,1024]{1,0:T(8,128)S(1)}, f32[1024,1024]{1,0:T(8,128)}, u32[]{:S(2)}, u32[]{:S(2)}) collective-permute-start(f32[1024,1024]{1,0:T(8,128)S(1)} %multiply_add_fusion.1), channel_id=1, source_target_pairs={{12,0},{16,4},{20,8},{24,12},{28,16},{32,20},{36,24},{40,28},{44,3... | collective-permute-start | bytes 12582920 | tf_op jit(solution)/shard_map/ppermute | solution.py:12
  655.7 2.7 copy-start.8
  658.4 1.2 copy-start.3
  659.7 2.6 copy-start.6
Sparse Core Ops, SparseCore 0:
  572.3 56.7 reduce-scatter.1
where the time goes:
time: 677 us; the launch traced here: 674 us
  waiting for transfers between devices  488 us (72%)
  blocking collectives  91.5 us (14%)
  starting transfers between devices  46.1 us (7%)
  matrix products  23.6 us (3%)
  between operations  18.7 us (3%)
    ppermute x17, waiting for transfers between devices, from_behind(): return lax.ppermute(block, axis, route)  488 us
    psum x1, blocking collectives, per_device(): loss_sum = lax.psum(local_loss, ('blk', 'rep'))  78.2 us
    ppermute x17, starting transfers between devices, from_behind(): return lax.ppermute(block, axis, route)  46 us
  transfers between devices with their start and end apart: 18, of which 12 were waited for; matrix products, arithmetic and copies ran while one was open for 4% of the time, Pallas kernels for 0%

commit v1 on v0

v1 whole, which is shorter than its diff:
```python
import math

import jax
import jax.numpy as jnp
from jax import lax
from jax.experimental import pallas as pl
from jax.experimental.pallas import tpu as pltpu
from jax.sharding import PartitionSpec as P

LOG2E = math.log2(math.e)
LN2 = math.log(2.0)
ORDER = (0, 2, 1, 3)
PLACE = (0, 2, 1, 3)
NT = (((1,), (1,)), ((), ()))
TN = (((0,), (0,)), ((), ()))
F32 = jnp.float32
BF16 = jnp.bfloat16
LIMIT = 48 * 1024 * 1024


def params(**kw):
    return pltpu.CompilerParams(vmem_limit_bytes=LIMIT, **kw)


def stats_of(s, k, col_ref, row_ref, m_scr, l_scr):
    top = jnp.max(s, axis=0, keepdims=True)
    col_ref[...] = top + jnp.log2(jnp.sum(jnp.exp2(s - top), axis=0, keepdims=True))

    @pl.when(k == 0)
    def _():
        m_scr[...] = jnp.full_like(m_scr, -jnp.inf)
        l_scr[...] = jnp.zeros_like(l_scr)

    before = m_scr[...]
    m = jnp.maximum(before, jnp.max(s, axis=1, keepdims=True))
    part = jnp.sum(jnp.exp2(s - m[:, :1]), axis=1, keepdims=True)
    total = l_scr[...] * jnp.exp2(before - m) + part
    m_scr[...] = m
    l_scr[...] = total

    @pl.when(k == 3)
    def _():
        row_ref[...] = jnp.transpose(m + jnp.log2(total))[:1, :]


def own_logits_kernel(order, scale, a, x, t, s_ref, row_ref, col_ref, diag_ref, m_scr, l_scr):
    k = pl.program_id(0)
    mult = scale[0] * LOG2E
    rows = a.shape[0]
    s_ref[:rows, :] = mult * lax.dot_general(a[...], t[...], NT, preferred_element_type=F32)
    s_ref[rows:, :] = mult * lax.dot_general(x[...], t[...], NT, preferred_element_type=F32)
    s = s_ref[...]

    @pl.when(k == 0)
    def _():
        sub = s[:rows, :]
        eye = lax.broadcasted_iota(jnp.int32, sub.shape, 0) == lax.broadcasted_iota(jnp.int32, sub.shape, 1)
        diag_ref[...] = jnp.sum(jnp.where(eye, sub, 0.0), axis=0, keepdims=True)

    stats_of(s, k, col_ref, row_ref, m_scr, l_scr)


def far_logits_kernel(even, scale, a, y, x, v0, v1, s_ref, row_ref, col_ref, m_scr, l_scr):
    k = pl.program_id(0)
    mult = scale[0] * LOG2E
    rows = a.shape[0]

    def run(img, v):
        return mult * lax.dot_general(img, v, NT, preferred_element_type=F32)

    ysel = jnp.where(even[0] == 1, y[...], a[...])
    v = jnp.where(k < 2, v0[...], v1[...])
    s_ref[:rows, :] = run(ysel, v)
    s_ref[rows:, :] = run(x[...], v)
    stats_of(s_ref[...], k, col_ref, row_ref, m_scr, l_scr)


def column(vec):
    return jnp.transpose(jnp.broadcast_to(vec, (128, vec.shape[1])))[:, :1]


def far_text_kernel(even, scale, a, y, x, s, row, col, w_ref, g23, g01, r_scr):
    k = pl.program_id(0)
    rows = a.shape[0]

    @pl.when(k == 0)
    def _():
        r_scr[...] = jnp.transpose(jnp.broadcast_to(row[...], (128, row.shape[1])))

    logits = s[...]
    w = (0.5 * (jnp.exp2(logits - r_scr[:, :1]) + jnp.exp2(logits - col[...]))).astype(BF16)
    w_ref[...] = w
    ysel = jnp.where(even[0] == 1, y[...], a[...])
    g = lax.dot_general(w[:rows], ysel, TN, preferred_element_type=F32)
    g = scale[0] * (g + lax.dot_general(w[rows:], x[...], TN, preferred_element_type=F32))

    @pl.when(k < 2)
    def _():
        g23[...] = g.astype(BF16)

    @pl.when(k >= 2)
    def _():
        g01[...] = g


def rest_kernel(order, scale, a, x, t, s, row, col, wv, v0, v1, g23, g01, gi_ref, gx_ref, gy_ref,
                r_scr, acc_i, acc_x, acc_y):
    k = pl.program_id(0)
    rows = a.shape[0]

    @pl.when(k == 0)
    def _():
        r_scr[...] = jnp.transpose(jnp.broadcast_to(row[...], (128, row.shape[1])))
        acc_i[...] = jnp.zeros_like(acc_i)
        acc_x[...] = jnp.zeros_like(acc_x)
        acc_y[...] = jnp.zeros_like(acc_y)

    logits = s[...]
    avg = 0.5 * (jnp.exp2(logits - r_scr[:, :1]) + jnp.exp2(logits - col[...]))
    ri = lax.broadcasted_iota(jnp.int32, avg.shape, 0)
    ci = lax.broadcasted_iota(jnp.int32, avg.shape, 1)
    avg = avg - jnp.where((ri == ci) & (k == 2), 1.0, 0.0)
    w = avg.astype(BF16)
    g = lax.dot_general(w[:rows], a[...], TN, preferred_element_type=F32)
    g = scale[0] * (g + lax.dot_general(w[rows:], x[...], TN, preferred_element_type=F32))

    @pl.when(k < 2)
    def _():
        g23[...] = g.astype(BF16)

    @pl.when(k >= 2)
    def _():
        g01[...] = g

    v = jnp.where(k >= 2, v0[...], v1[...])
    far = wv[...]
    acc_i[...] += jnp.dot(w[:rows], t[...], preferred_element_type=F32)
    acc_y[...] += jnp.dot(far[:rows], v, preferred_element_type=F32)
    acc_x[...] += (jnp.dot(w[rows:], t[...], preferred_element_type=F32)
                   + jnp.dot(far[rows:], v, preferred_element_type=F32))

    @pl.when(k == 3)
    def _():
        gi_ref[...] = scale[0] * acc_i[...]
        gx_ref[...] = (scale[0] * acc_x[...]).astype(BF16)
        gy_ref[...] = scale[0] * acc_y[...]


def whole(shape):
    return pl.BlockSpec(shape, lambda k, *_: (0,) * len(shape))


def lse2(*parts):
    top = parts[0]
    for p in parts[1:]:
        top = jnp.maximum(top, p)
    total = sum(jnp.exp2(p - top) for p in parts)
    return top + jnp.log2(total)


def per_device(image_emb, text_emb, logit_scale):
    rows, d = image_emb.shape
    blocks = lax.axis_size("blk")
    blk = lax.axis_index("blk")
    rep = lax.axis_index("rep")
    even = blk % 2 == 0
    evens = even.astype(jnp.int32).reshape(1)
    order = jnp.stack([rep ^ m for m in ORDER]).astype(jnp.int32)
    x_route = [(i, (i - 1) % blocks if i % 2 == 0 else (i - 3) % blocks) for i in range(blocks)]
    y_route = [(i, (i - 4) % blocks) for i in range(0, blocks, 2)]
    v_route = [(i, i ^ 1) for i in range(blocks)]
    x_back = [(b, a) for a, b in x_route]
    y_back = [(b, a) for a, b in y_route]

    def hop(value, route):
        return lax.ppermute(value, "blk", route)

    def swap(value, mask):
        return lax.ppermute(value, "rep", [(i, i ^ mask) for i in range(4)])

    first = lax.dynamic_slice_in_dim(text_emb, (rep) * rows, rows, 0)
    second = lax.dynamic_slice_in_dim(text_emb, (rep ^ 2) * rows, rows, 0)
    v0 = hop(jnp.concatenate([first, second]), v_route)
    x = hop(image_emb, x_route)
    y = hop(image_emb, y_route)
    v1 = swap(v0, 1)

    smem = pl.BlockSpec(memory_space=pltpu.SMEM)
    image_spec = whole((rows, d))
    vec = jax.ShapeDtypeStruct
    logits_shape = vec((2 * rows, 4 * rows), F32)
    stat_scratch = [pltpu.VMEM((2 * rows, 128), F32)] * 2
    tile = pl.BlockSpec((2 * rows, rows), lambda k, *_: (0, k))
    lane = pl.BlockSpec((1, rows), lambda k, *_: (0, k))
    logits_cost = pl.CostEstimate(flops=2 * 2 * rows * 4 * rows * d, bytes_accessed=6 << 20, transcendentals=4 << 20)
    s_t, row_t, col_t, diag = pl.pallas_call(
        own_logits_kernel,
        grid_spec=pltpu.PrefetchScalarGridSpec(
            num_scalar_prefetch=1,
            grid=(4,),
            in_specs=[smem, image_spec, image_spec, pl.BlockSpec((rows, d), lambda k, o: (o[k], 0))],
            out_specs=[tile, whole((1, 2 * rows)), lane, whole((1, rows))],
            scratch_shapes=stat_scratch,
        ),
        out_shape=[logits_shape, vec((1, 2 * rows), F32), vec((1, 4 * rows), F32), vec((1, rows), F32)],
        compiler_params=params(),
        cost_estimate=logits_cost,
        name="own_logits",
    )(order, logit_scale, image_emb, x, text_emb)
    s_v, row_v, col_v = pl.pallas_call(
        far_logits_kernel,
        grid=(4,),
        in_specs=[smem, smem, image_spec, image_spec, image_spec,
                  pl.BlockSpec((rows, d), lambda k: (jnp.minimum(k, 1), 0)),
                  pl.BlockSpec((rows, d), lambda k: (jnp.maximum(k - 2, 0), 0))],
        out_specs=[tile, whole((1, 2 * rows)), lane],
        scratch_shapes=stat_scratch,
        out_shape=[logits_shape, vec((1, 2 * rows), F32), vec((1, 4 * rows), F32)],
        compiler_params=params(),
        cost_estimate=logits_cost,
        name="far_logits",
    )(evens, logit_scale, image_emb, y, x, v0, v1)

    r_i, r_xt = row_t[:, :rows], row_t[:, rows:]
    r_y, r_xv = row_v[:, :rows], row_v[:, rows:]
    r_x = lse2(r_xt, r_xv)
    h_i = jnp.where(even, r_i, lse2(r_i, r_y))
    down = hop(jnp.concatenate([h_i, r_x], 1), x_route)
    up = hop(jnp.concatenate([r_x, r_y], 1), x_back)
    h_y = hop(r_i, y_route)
    y_i = hop(r_y, y_back)
    h_x, x_y = down[:, :rows], down[:, rows:]
    x_i, y_x = up[:, :rows], up[:, rows:]
    row_i = jnp.where(even, lse2(r_i, x_i, y_i), lse2(h_i, x_i))
    row_x = jnp.where(even, lse2(h_x, r_x), lse2(h_x, r_x, y_x))
    row_y = jnp.where(even, lse2(r_y, h_y, x_y), row_i)

    both = jnp.concatenate([col_t, col_v])
    quarters = [both[:, q * rows:(q + 1) * rows] for q in range(4)]
    parts = [both]
    for mask in (1, 2, 3):
        got = swap(both, mask)
        parts.append(jnp.concatenate(
            [got[:, q * rows:(q + 1) * rows] for q in (PLACE[ORDER[k] ^ mask] for k in range(4))], 1))
    group = lse2(*parts)
    other = hop(group, v_route)
    cols = lse2(group, other[::-1])
    c_t, c_v = cols[:1], cols[1:]

    late = pl.BlockSpec((2 * rows, rows), lambda k, *_: (0, (k + 2) % 4))
    late_lane = pl.BlockSpec((1, rows), lambda k, *_: (0, (k + 2) % 4))
    early_out = pl.BlockSpec((rows, d), lambda k, *_: (jnp.minimum(k, 1), 0))
    late_out = pl.BlockSpec((rows, d), lambda k, *_: (jnp.maximum(k - 2, 0), 0))
    row_spec = whole((1, 2 * rows))
    w_v, gv23, gv01 = pl.pallas_call(
        far_text_kernel,
        grid=(4,),
        in_specs=[smem, smem, image_spec, image_spec, image_spec, late, row_spec, late_lane],
        out_specs=[late, early_out, late_out],
        out_shape=[vec((2 * rows, 4 * rows), BF16), vec((2 * rows, d), BF16), vec((2 * rows, d), F32)],
        scratch_shapes=[pltpu.VMEM((2 * rows, 128), F32)],
        compiler_params=params(),
        cost_estimate=logits_cost,
        name="far_text",
    )(evens, logit_scale, image_emb, y, x, s_v, jnp.concatenate([row_y, row_x], 1), c_v)
    v_core = swap(gv23, 1)
    gt23, gt01, g_i, g_x, g_y = pl.pallas_call(
        rest_kernel,
        grid_spec=pltpu.PrefetchScalarGridSpec(
            num_scalar_prefetch=1,
            grid=(4,),
            in_specs=[smem, image_spec, image_spec,
                      pl.BlockSpec((rows, d), lambda k, o: (o[(k + 2) % 4], 0)),
                      late, row_spec, late_lane, late,
                      pl.BlockSpec((rows, d), lambda k, *_: (jnp.maximum(k - 2, 0), 0)),
                      pl.BlockSpec((rows, d), lambda k, *_: (jnp.minimum(k, 1), 0))],
            out_specs=[early_out, late_out, image_spec, image_spec, image_spec],
            scratch_shapes=[pltpu.VMEM((2 * rows, 128), F32)] + [pltpu.VMEM((rows, d), F32)] * 3,
        ),
        out_shape=[vec((2 * rows, d), BF16), vec((2 * rows, d), F32), vec((rows, d), F32), vec((rows, d), BF16),
                   vec((rows, d), F32)],
        compiler_params=params(),
        cost_estimate=pl.CostEstimate(flops=3 * 2 * 2 * rows * 4 * rows * d, bytes_accessed=12 << 20,
                                      transcendentals=2 << 20),
        name="rest",
    )(order, logit_scale, image_emb, x, text_emb, s_t, jnp.concatenate([row_i, row_x], 1), c_t, w_v, v0, v1)

    t_core = swap(gt23, 1)
    v_one = (gv01[rows:] + v_core[rows:].astype(F32)).astype(BF16)
    v_zero = (gv01[:rows] + v_core[:rows].astype(F32)).astype(BF16)
    home_one = hop(v_one, v_route)
    x_got = hop(g_x, x_back)
    y_got = hop(g_y.astype(BF16), y_back)
    home_zero = hop(v_zero, v_route)
    one = gt01[rows:] + t_core[rows:].astype(F32) + home_one.astype(F32)
    across = swap(one.astype(BF16), 2)
    grad_text = (gt01[:rows] + t_core[:rows].astype(F32)) + home_zero.astype(F32) + across.astype(F32)
    grad_image = g_i + x_got.astype(F32) + jnp.where(even, y_got.astype(F32), g_y)

    local = LN2 * (jnp.sum(row_i) + jnp.sum(c_t[:, :rows]) - 2.0 * jnp.sum(diag))
    total = jnp.broadcast_to(local, (1, 128))
    step = 1
    while step < blocks:
        total = total + hop(total, [(i, i ^ step) for i in range(blocks)])
        step *= 2
    for mask in (1, 2):
        total = total + swap(total, mask)
    pairs = rows * blocks * 4
    loss = total[0, :1] / (2.0 * pairs)
    return grad_image, grad_text, loss


def solution(mesh):
    placed = (P(("blk", "rep"), None), P("blk", None), P())
    return jax.shard_map(
        per_device,
        mesh=mesh,
        in_specs=placed,
        out_specs=(P(("blk", "rep"), None), P(("blk", "rep"), None), P()),
        check_vma=False,
    )
```

time: 677 us -> 162 us (0.24)
  waiting for transfers between devices: 488 us -> 73.7 us
  blocking collectives: 91.5 us -> 0 us
  Pallas kernels: 0 us -> 26.2 us
  matrix products: 23.6 us -> 0 us
  between operations: 18.7 us -> 4.66 us
    ppermute x17 -> x27, waiting for transfers between devices: 488 us -> 73.7 us  [the longest x18 64.4 us: hop(): return lax.ppermute(value, 'blk', route)]
    psum x1 -> x0, blocking collectives: 78.2 us -> none  [per_device(): loss_sum = lax.psum(local_loss, ('blk', 'rep'))]
    pallas_call x0 -> x4, Pallas kernels: none -> 26.2 us  [the longest x1 9.65 us: per_device(): pl.pallas_call(rest_kernel, grid_spec=pltpu.PrefetchScalarGridSpec(num_sc...]
    dot_general x12 -> x0, matrix products: 23.6 us -> none  [the longest x4 9.9 us: pair_logits(): lax.dot_general(images, captions, (((1,), (1,)), ((), ())), preferred_ele...]
    all_gather x2 -> x0, blocking collectives: 13.4 us -> none  [joined(): gathered = jax.tree.map(lambda a: lax.all_gather(a, axis), part)]
    ppermute x17 -> x27, starting transfers between devices: 46 us -> 42.5 us  [the longest x18 36.8 us: hop(): return lax.ppermute(value, 'blk', route)]
  transfers between devices with their start and end apart: 18 -> 27, of which waited for: 12 -> 13; matrix products, arithmetic and copies ran while one was open for 4% -> 4% of each run, Pallas kernels for 0% -> 10%
where the time goes in v1:
time: 162 us; the launch traced here: 161 us
  waiting for transfers between devices  73.7 us (45%)
  starting transfers between devices  42.5 us (26%)
  Pallas kernels  26.2 us (16%)
  other arithmetic  9.11 us (6%)
  local copies, waits for them, and re-layouts  4.98 us (3%)
  between operations  4.66 us (3%)
    ppermute x18, waiting for transfers between devices, hop(): return lax.ppermute(value, 'blk', route)  64.4 us
    ppermute x18, starting transfers between devices, hop(): return lax.ppermute(value, 'blk', route)  36.8 us
    pallas_call x1, Pallas kernels, per_device(): pl.pallas_call(rest_kernel, grid_spec=pltpu.PrefetchScalarGridSpec(num_sc...  9.65 us
    ppermute x9, waiting for transfers between devices, swap(): return lax.ppermute(value, 'rep', [(i, i ^ mask) for i in range(4)])  9.32 us
    pallas_call x1, Pallas kernels, per_device(): pl.pallas_call(own_logits_kernel, grid_spec=pltpu.PrefetchScalarGridSpec(...  5.91 us
    pallas_call x1, Pallas kernels, per_device(): pl.pallas_call(far_logits_kernel, grid=(4,), in_specs=[smem, smem, image_...  5.79 us
    ppermute x9, starting transfers between devices, swap(): return lax.ppermute(value, 'rep', [(i, i ^ mask) for i in range(4)])  5.73 us
    pallas_call x1, Pallas kernels, per_device(): pl.pallas_call(far_text_kernel, grid=(4,), in_specs=[smem, smem, image_sp...  4.83 us
  transfers between devices with their start and end apart: 27, of which 13 were waited for; matrix products, arithmetic and copies ran while one was open for 4% of the time, Pallas kernels for 10%

profile of v1, /device:TPU:16, one launch (start us, length us, event | category | flops | bytes accessed | tf_op | source)
XLA Modules:
  0.0 161.1 jit_solution(9493760177076402824)
XLA Ops:
  0.7 1.4 constant_dynamic-slice_fusion.1
  2.2 1.4 collective-permute-start.2
  3.5 23.6 %collective-permute-done.2.v0 = bf16[512,1024]{1,0:T(8,128)(2,1)S(1)} collective-permute-done((bf16[512,1024]{1,0:T(8,128)(2,1)S(1)}, bf16[512,1024]{1,0:T(8,128)(2,1)S(1)}, u32[]{:S(2)}, u32[]{:S(2)}) %collective-permute-start.2) | collective-permute-done | bytes 1048608 | tf_op jit(solution)/shard_map/ppermute | solution.py:176
  27.6 8.7 %collective-permute-start.1 = (bf16[256,1024]{1,0:T(8,128)(2,1)}, bf16[256,1024]{1,0:T(8,128)(2,1)}, u32[]{:S(2)}, u32[]{:S(2)}) collective-permute-start(bf16[256,1024]{1,0:T(8,128)(2,1)} %a.7), channel_id=1, source_target_pairs={{0,240},{8,248},{16,0},{24,8},{32,16},{40,24},{48,32},{56,40},{64,... | collective-permute-start | bytes 1572872 | tf_op jit(solution)/shard_map/ppermute | solution.py:176
  37.0 5.7 %collective-permute-done.x = bf16[256,1024]{1,0:T(8,128)(2,1)} collective-permute-done((bf16[256,1024]{1,0:T(8,128)(2,1)}, bf16[256,1024]{1,0:T(8,128)(2,1)}, u32[]{:S(2)}, u32[]{:S(2)}) %collective-permute-start) | collective-permute-done | bytes 524320 | tf_op jit(solution)/shard_map/ppermute | solution.py:176
  42.7 5.9 %own_logits.1 = (f32[512,1024]{1,0:T(8,128)S(1)}, f32[1,512]{1,0:T(1,128)S(1)}, f32[1,1024]{1,0:T(1,128)S(1)}, f32[1,256]{1,0:T(1,128)S(1)}) custom-call(s32[4]{0:T(128)S(1)} %pad_add_fusion.order, f32[1]{0:T(128)S(6)} %copy.6.scale, bf16[256,1024]{1,0:T(8,128)(2,1)} %a.7, bf16[256,1024]{1,0:T(8,128)(2,1)} %collective-permute-done.x, ...), custom_call_target="tpu_custom_call" | custom-call | flops 1073741824 | bytes 6291456 | tf_op jit(solution)/shard_map/own_logits/pallas_call | solution.py:196
  50.0 5.8 %far_logits.1 = (f32[512,1024]{1,0:T(8,128)S(1)}, f32[1,512]{1,0:T(1,128)S(1)}, f32[1,1024]{1,0:T(1,128)S(1)}) custom-call(s32[1]{0:T(128)} %bitcast.4.even, f32[1]{0:T(128)S(6)} %copy.6.scale, bf16[256,1024]{1,0:T(8,128)(2,1)} %a.7, bf16[256,1024]{1,0:T(8,128)(2,1)} %collective-permute-done.1.y, bf16[256,1024]{1,0:T(8,128)(2,1)} %collective-permute-done.x, ...), custom_call_target="tpu_custom_call" | custom-call | flops 1073741824 | bytes 6291456 | tf_op jit(solution)/shard_map/far_logits/pallas_call | solution.py:210
  55.8 1.4 copy-done.4
  58.1 3.8 %collective-permute-start.5 = (f32[1,256]{1,0:T(1,128)S(1)}, f32[1,256]{1,0:T(1,128)S(1)}, u32[]{:S(2)}, u32[]{:S(2)}) collective-permute-start(f32[1,256]{1,0:T(1,128)S(1)} %get-tuple-element.56), channel_id=1, source_target_pairs={{240,0},{248,8},{0,16},{8,24},{16,32},{24,40},{32,48},{40,56},{48,... | collective-permute-start | bytes 3080 | tf_op jit(solution)/shard_map/ppermute | solution.py:176
  62.0 7.6 %collective-permute-done.5 = f32[1,256]{1,0:T(1,128)S(1)} collective-permute-done((f32[1,256]{1,0:T(1,128)S(1)}, f32[1,256]{1,0:T(1,128)S(1)}, u32[]{:S(2)}, u32[]{:S(2)}) %collective-permute-start.5) | collective-permute-done | bytes 1056 | tf_op jit(solution)/shard_map/ppermute | solution.py:176
  70.3 3.9 %collective-permute-start.11 = (f32[1,256]{1,0:T(1,128)S(1)}, f32[1,256]{1,0:T(1,128)S(1)}, u32[]{:S(2)}, u32[]{:S(2)}) collective-permute-start(f32[1,256]{1,0:T(1,128)S(1)} %get-tuple-element.54), channel_id=1, source_target_pairs={{0,240},{8,248},{16,0},{24,8},{32,16},{40,24},{48,32},{56,40},{64,... | collective-permute-start | bytes 3080 | tf_op jit(solution)/shard_map/ppermute | solution.py:176
  74.3 2.8 %collective-permute-start.8 = (f32[2,1024]{1,0:T(2,128)S(1)}, f32[2,1024]{1,0:T(2,128)S(1)}, u32[]{:S(2)}, u32[]{:S(2)}) collective-permute-start(f32[2,1024]{1,0:T(2,128)S(1)} %pad_maximum_fusion.1), channel_id=1, source_target_pairs={{0,2},{1,3},{2,0},{3,1},{4,6},{5,7},{6,4},{7,5},{8,10},{9,11},{10,... | collective-permute-start | bytes 24584 | tf_op jit(solution)/shard_map/ppermute | solution.py:179
  77.7 1.8 %collective-permute-done.8 = f32[2,1024]{1,0:T(2,128)S(1)} collective-permute-done((f32[2,1024]{1,0:T(2,128)S(1)}, f32[2,1024]{1,0:T(2,128)S(1)}, u32[]{:S(2)}, u32[]{:S(2)}) %collective-permute-start.8) | collective-permute-done | bytes 8224 | tf_op jit(solution)/shard_map/ppermute | solution.py:179
  79.6 2.1 %collective-permute-done.9 = f32[2,1024]{1,0:T(2,128)S(1)} collective-permute-done((f32[2,1024]{1,0:T(2,128)S(1)}, f32[2,1024]{1,0:T(2,128)S(1)}, u32[]{:S(2)}, u32[]{:S(2)}) %collective-permute-start.9) | collective-permute-done | bytes 8224 | tf_op jit(solution)/shard_map/ppermute | solution.py:179
  81.8 3.8 %collective-permute-start.10 = (f32[2,1024]{1,0:T(2,128)S(1)}, f32[2,1024]{1,0:T(2,128)S(1)}, u32[]{:S(2)}, u32[]{:S(2)}) collective-permute-start(f32[2,1024]{1,0:T(2,128)S(1)} %multiply_add_fusion.1), channel_id=1, source_target_pairs={{0,4},{4,0},{8,12},{12,8},{16,20},{20,16},{24,28},{28,24},{32,36},... | collective-permute-start | bytes 24584 | tf_op jit(solution)/shard_map/ppermute | solution.py:176
  85.6 1.6 %collective-permute-done.10 = f32[2,1024]{1,0:T(2,128)S(1)} collective-permute-done((f32[2,1024]{1,0:T(2,128)S(1)}, f32[2,1024]{1,0:T(2,128)S(1)}, u32[]{:S(2)}, u32[]{:S(2)}) %collective-permute-start.10) | collective-permute-done | bytes 8224 | tf_op jit(solution)/shard_map/ppermute | solution.py:176
  87.5 4.8 %far_text.1 = (bf16[512,1024]{1,0:T(8,128)(2,1)S(1)}, bf16[512,1024]{1,0:T(8,128)(2,1)S(1)}, f32[512,1024]{1,0:T(8,128)S(1)}) custom-call(s32[1]{0:T(128)} %bitcast.4.even, f32[1]{0:T(128)S(6)} %copy.6.scale, bf16[256,1024]{1,0:T(8,128)(2,1)} %a.7, bf16[256,1024]{1,0:T(8,128)(2,1)} %collective-permute-done.1.y, bf16[256,1024]{1,0:T(8,128)(2,1)} %collective-permute-done.x, ...), custom_call_target="tpu_custom_call" | custom-call | flops 1073741824 | bytes 6291456 | tf_op jit(solution)/shard_map/far_text/pallas_call | solution.py:255
  92.4 9.7 %rest.1 = (bf16[512,1024]{1,0:T(8,128)(2,1)S(1)}, f32[512,1024]{1,0:T(8,128)}, f32[256,1024]{1,0:T(8,128)S(1)}, bf16[256,1024]{1,0:T(8,128)(2,1)S(1)}, f32[256,1024]{1,0:T(8,128)S(1)}) custom-call(s32[4]{0:T(128)S(1)} %pad_add_fusion.order, f32[1]{0:T(128)S(6)} %copy.6.scale, bf16[256,1024]{1,0:T(8,128)(2,1)} %a.7, ...), custom_call_target="tpu_custom_call" | custom-call | flops 3221225472 | bytes 12582912 | tf_op jit(solution)/shard_map/rest/pallas_call | solution.py:267
  102.6 1.4 add_convert_fusion.2
  103.9 2.0 %collective-permute-start.17 = (bf16[256,1024]{1,0:T(8,128)(2,1)}, bf16[256,1024]{1,0:T(8,128)(2,1)}, u32[]{:S(2)}, u32[]{:S(2)}) collective-permute-start(bf16[256,1024]{1,0:T(8,128)(2,1)} %get-tuple-element.37), channel_id=1, source_target_pairs={{0,4},{4,0},{8,12},{12,8},{16,20},{20,16},{24,28},{28,24},{32,36},... | collective-permute-start | bytes 1572872 | tf_op jit(solution)/shard_map/ppermute | solution.py:176
  109.4 1.9 %collective-permute-start.13 = (bf16[256,1024]{1,0:T(8,128)(2,1)S(1)}, bf16[256,1024]{1,0:T(8,128)(2,1)S(1)}, u32[]{:S(2)}, u32[]{:S(2)}) collective-permute-start(bf16[256,1024]{1,0:T(8,128)(2,1)S(1)} %convert_element_type.41), channel_id=1, source_target_pairs={{240,0},{248,8},{0,16},{8,24},{16,32},{24,40},{32,48},{40,56},{48,... | collective-permute-start | bytes 1572872 | tf_op jit(solution)/shard_map/ppermute | solution.py:176
  111.3 1.7 %collective-permute-start.12 = (bf16[256,1024]{1,0:T(8,128)(2,1)}, bf16[256,1024]{1,0:T(8,128)(2,1)S(1)}, u32[]{:S(2)}, u32[]{:S(2)}) collective-permute-start(bf16[256,1024]{1,0:T(8,128)(2,1)} %copy-done.2), channel_id=1, source_target_pairs={{252,0},{248,4},{4,8},{0,12},{12,16},{8,20},{20,24},{16,28},{28,32... | collective-permute-start | bytes 1572872 | tf_op jit(solution)/shard_map/ppermute | solution.py:176
  113.0 5.3 %collective-permute-done.19 = f32[1,128]{1,0:T(1,128)S(1)} collective-permute-done((f32[1,128]{1,0:T(1,128)S(1)}, f32[1,128]{1,0:T(1,128)S(1)}, u32[]{:S(2)}, u32[]{:S(2)}) %collective-permute-start.19) | collective-permute-done | bytes 544 | tf_op jit(solution)/shard_map/ppermute | solution.py:176
  118.4 4.1 %collective-permute-start.20 = (f32[1,128]{1,0:T(1,128)S(1)}, f32[1,128]{1,0:T(1,128)S(1)}, u32[]{:S(2)}, u32[]{:S(2)}) collective-permute-start(f32[1,128]{1,0:T(1,128)S(1)} %broadcast_add_fusion), channel_id=1, source_target_pairs={{0,8},{4,12},{8,0},{12,4},{16,24},{20,28},{24,16},{28,20},{32,40},... | collective-permute-start | bytes 1544 | tf_op jit(solution)/shard_map/ppermute | solution.py:176
  123.3 1.8 %add_convert_fusion = bf16[256,1024]{1,0:T(8,128)(2,1)S(1)} fusion(bf16[256,1024]{1,0:T(8,128)(2,1)} %collective-permute-done.17, f32[512,1024]{1,0:T(8,128)} %get-tuple-element.28, bf16[512,1024]{1,0:T(8,128)(2,1)} %collective-permute-done.14), kind=kLoop, calls=%fused_computation.2 | loop fusion | flops 1310720 | bytes 2621440 | tf_op jit(solution)/shard_map/convert_element_type | solution.py:296
  126.5 7.5 %collective-permute-done.21 = f32[1,128]{1,0:T(1,128)S(1)} collective-permute-done((f32[1,128]{1,0:T(1,128)S(1)}, f32[1,128]{1,0:T(1,128)S(1)}, u32[]{:S(2)}, u32[]{:S(2)}) %collective-permute-start.21) | collective-permute-done | bytes 544 | tf_op jit(solution)/shard_map/ppermute | solution.py:176
  134.0 4.4 %collective-permute-done.22 = f32[1,128]{1,0:T(1,128)S(1)} collective-permute-done((f32[1,128]{1,0:T(1,128)S(1)}, f32[1,128]{1,0:T(1,128)S(1)}, u32[]{:S(2)}, u32[]{:S(2)}) %collective-permute-start.22) | collective-permute-done | bytes 544 | tf_op jit(solution)/shard_map/ppermute | solution.py:176
  138.5 2.2 %collective-permute-start.23 = (f32[1,128]{1,0:T(1,128)S(1)}, f32[1,128]{1,0:T(1,128)S(1)}, u32[]{:S(2)}, u32[]{:S(2)}) collective-permute-start(f32[1,128]{1,0:T(1,128)S(1)} %add.172), channel_id=1, source_target_pairs={{0,64},{4,68},{8,72},{12,76},{16,80},{20,84},{24,88},{28,92},{32,9... | collective-permute-start | bytes 1544 | tf_op jit(solution)/shard_map/ppermute | solution.py:176
  140.7 5.3 %collective-permute-done.23 = f32[1,128]{1,0:T(1,128)S(1)} collective-permute-done((f32[1,128]{1,0:T(1,128)S(1)}, f32[1,128]{1,0:T(1,128)S(1)}, u32[]{:S(2)}, u32[]{:S(2)}) %collective-permute-start.23) | collective-permute-done | bytes 544 | tf_op jit(solution)/shard_map/ppermute | solution.py:176
  146.1 3.3 %collective-permute-done.24 = f32[1,128]{1,0:T(1,128)S(1)} collective-permute-done((f32[1,128]{1,0:T(1,128)S(1)}, f32[1,128]{1,0:T(1,128)S(1)}, u32[]{:S(2)}, u32[]{:S(2)}) %collective-permute-start.24) | collective-permute-done | bytes 544 | tf_op jit(solution)/shard_map/ppermute | solution.py:176
  151.4 4.2 %collective-permute-done.26 = f32[1,128]{1,0:T(1,128)S(1)} collective-permute-done((f32[1,128]{1,0:T(1,128)S(1)}, f32[1,128]{1,0:T(1,128)S(1)}, u32[]{:S(2)}, u32[]{:S(2)}) %collective-permute-start.26) | collective-permute-done | bytes 544 | tf_op jit(solution)/shard_map/ppermute | solution.py:179
  157.7 2.3 %convert_add_fusion = f32[256,1024]{1,0:T(8,128)} fusion(bf16[256,1024]{1,0:T(8,128)(2,1)S(1)} %collective-permute-done.18, bf16[256,1024]{1,0:T(8,128)(2,1)S(1)} %collective-permute-done.16, f32[512,1024]{1,0:T(8,128)S(1)} %copy-done.5, bf16[512,1024]{1,0:T(8,128)(2,1)} %collective-permute-done.14), kind=kLoop, calls=%fused_computation.1 | loop fusion | flops 1572864 | bytes 3670016 | tf_op jit(solution)/shard_map/add | solution.py:297
  (71 shorter events, 13.2 us)
Async XLA Ops:
  0.6 42.1 %copy-start = (bf16[1024,1024]{1,0:T(8,128)(2,1)S(1)}, bf16[1024,1024]{1,0:T(8,128)(2,1)}, u32[]{:S(2)}) copy-start(bf16[1024,1024]{1,0:T(8,128)(2,1)} %t.3) | copy-start | bytes 6291460
  2.2 25.0 %collective-permute-start.2 = (bf16[512,1024]{1,0:T(8,128)(2,1)S(1)}, bf16[512,1024]{1,0:T(8,128)(2,1)S(1)}, u32[]{:S(2)}, u32[]{:S(2)}) collective-permute-start(bf16[512,1024]{1,0:T(8,128)(2,1)S(1)} %pad_maximum_fusion), channel_id=1, source_target_pairs={{0,4},{4,0},{8,12},{12,8},{16,20},{20,16},{24,28},{28,24},{32,36},... | collective-permute-start | bytes 3145736 | tf_op jit(solution)/shard_map/ppermute | solution.py:176
  27.1 22.8 %copy-start.1 = (bf16[512,1024]{1,0:T(8,128)(2,1)}, bf16[512,1024]{1,0:T(8,128)(2,1)S(1)}, u32[]{:S(2)}) copy-start(bf16[512,1024]{1,0:T(8,128)(2,1)S(1)} %collective-permute-done.2.v0) | copy-start | bytes 3145732
  27.1 22.8 %collective-permute-start.3 = (bf16[512,1024]{1,0:T(8,128)(2,1)S(1)}, bf16[512,1024]{1,0:T(8,128)(2,1)}, u32[]{:S(2)}, u32[]{:S(2)}) collective-permute-start(bf16[512,1024]{1,0:T(8,128)(2,1)S(1)} %collective-permute-done.2.v0), channel_id=1, source_target_pairs={{0,1},{1,0},{2,3},{3,2},{4,5},{5,4},{6,7},{7,6},{8,9},{9,8},{10,11... | collective-permute-start | bytes 3145736 | tf_op jit(solution)/shard_map/ppermute | solution.py:179
  27.1 15.6 %collective-permute-start = (bf16[256,1024]{1,0:T(8,128)(2,1)}, bf16[256,1024]{1,0:T(8,128)(2,1)}, u32[]{:S(2)}, u32[]{:S(2)}) collective-permute-start(bf16[256,1024]{1,0:T(8,128)(2,1)} %a.7), channel_id=1, source_target_pairs={{0,252},{4,248},{8,4},{12,0},{16,12},{20,8},{24,20},{28,16},{32,28... | collective-permute-start | bytes 1572872 | tf_op jit(solution)/shard_map/ppermute | solution.py:176
  27.6 22.4 %collective-permute-start.1 = (bf16[256,1024]{1,0:T(8,128)(2,1)}, bf16[256,1024]{1,0:T(8,128)(2,1)}, u32[]{:S(2)}, u32[]{:S(2)}) collective-permute-start(bf16[256,1024]{1,0:T(8,128)(2,1)} %a.7), channel_id=1, source_target_pairs={{0,240},{8,248},{16,0},{24,8},{32,16},{40,24},{48,32},{56,40},{64,... | collective-permute-start | bytes 1572872 | tf_op jit(solution)/shard_map/ppermute | solution.py:176
  55.8 1.4 copy-start.4
  57.2 12.5 %collective-permute-start.4 = (f32[1,512]{1,0:T(1,128)S(1)}, f32[1,512]{1,0:T(1,128)S(1)}, u32[]{:S(2)}, u32[]{:S(2)}) collective-permute-start(f32[1,512]{1,0:T(1,128)S(1)} %pad_maximum_fusion.5), channel_id=1, source_target_pairs={{252,0},{248,4},{4,8},{0,12},{12,16},{8,20},{20,24},{16,28},{28,32... | collective-permute-start | bytes 6152 | tf_op jit(solution)/shard_map/ppermute | solution.py:176
  58.1 11.5 %collective-permute-start.5 = (f32[1,256]{1,0:T(1,128)S(1)}, f32[1,256]{1,0:T(1,128)S(1)}, u32[]{:S(2)}, u32[]{:S(2)}) collective-permute-start(f32[1,256]{1,0:T(1,128)S(1)} %get-tuple-element.56), channel_id=1, source_target_pairs={{240,0},{248,8},{0,16},{8,24},{16,32},{24,40},{32,48},{40,56},{48,... | collective-permute-start | bytes 3080 | tf_op jit(solution)/shard_map/ppermute | solution.py:176
  70.3 7.4 %collective-permute-start.6 = (f32[1,512]{1,0:T(1,128)S(1)}, f32[1,512]{1,0:T(1,128)S(1)}, u32[]{:S(2)}, u32[]{:S(2)}) collective-permute-start(f32[1,512]{1,0:T(1,128)S(1)} %pad_maximum_fusion.6), channel_id=1, source_target_pairs={{0,252},{4,248},{8,4},{12,0},{16,12},{20,8},{24,20},{28,16},{32,28... | collective-permute-start | bytes 6152 | tf_op jit(solution)/shard_map/ppermute | solution.py:176
  70.3 7.4 %collective-permute-start.11 = (f32[1,256]{1,0:T(1,128)S(1)}, f32[1,256]{1,0:T(1,128)S(1)}, u32[]{:S(2)}, u32[]{:S(2)}) collective-permute-start(f32[1,256]{1,0:T(1,128)S(1)} %get-tuple-element.54), channel_id=1, source_target_pairs={{0,240},{8,248},{16,0},{24,8},{32,16},{40,24},{48,32},{56,40},{64,... | collective-permute-start | bytes 3080 | tf_op jit(solution)/shard_map/ppermute | solution.py:176
  74.2 3.5 %collective-permute-start.7 = (f32[2,1024]{1,0:T(2,128)S(1)}, f32[2,1024]{1,0:T(2,128)S(1)}, u32[]{:S(2)}, u32[]{:S(2)}) collective-permute-start(f32[2,1024]{1,0:T(2,128)S(1)} %pad_maximum_fusion.1), channel_id=1, source_target_pairs={{0,1},{1,0},{2,3},{3,2},{4,5},{5,4},{6,7},{7,6},{8,9},{9,8},{10,11... | collective-permute-start | bytes 24584 | tf_op jit(solution)/shard_map/ppermute | solution.py:179
  74.3 5.2 %collective-permute-start.8 = (f32[2,1024]{1,0:T(2,128)S(1)}, f32[2,1024]{1,0:T(2,128)S(1)}, u32[]{:S(2)}, u32[]{:S(2)}) collective-permute-start(f32[2,1024]{1,0:T(2,128)S(1)} %pad_maximum_fusion.1), channel_id=1, source_target_pairs={{0,2},{1,3},{2,0},{3,1},{4,6},{5,7},{6,4},{7,5},{8,10},{9,11},{10,... | collective-permute-start | bytes 24584 | tf_op jit(solution)/shard_map/ppermute | solution.py:179
  77.1 4.6 %collective-permute-start.9 = (f32[2,1024]{1,0:T(2,128)S(1)}, f32[2,1024]{1,0:T(2,128)S(1)}, u32[]{:S(2)}, u32[]{:S(2)}) collective-permute-start(f32[2,1024]{1,0:T(2,128)S(1)} %pad_maximum_fusion.1), channel_id=1, source_target_pairs={{0,3},{1,2},{2,1},{3,0},{4,7},{5,6},{6,5},{7,4},{8,11},{9,10},{10,... | collective-permute-start | bytes 24584 | tf_op jit(solution)/shard_map/ppermute | solution.py:179
  81.8 5.5 %collective-permute-start.10 = (f32[2,1024]{1,0:T(2,128)S(1)}, f32[2,1024]{1,0:T(2,128)S(1)}, u32[]{:S(2)}, u32[]{:S(2)}) collective-permute-start(f32[2,1024]{1,0:T(2,128)S(1)} %multiply_add_fusion.1), channel_id=1, source_target_pairs={{0,4},{4,0},{8,12},{12,8},{16,20},{20,16},{24,28},{28,24},{32,36},... | collective-permute-start | bytes 24584 | tf_op jit(solution)/shard_map/ppermute | solution.py:176
  92.3 10.2 %collective-permute-start.15 = (bf16[512,1024]{1,0:T(8,128)(2,1)S(1)}, bf16[512,1024]{1,0:T(8,128)(2,1)S(1)}, u32[]{:S(2)}, u32[]{:S(2)}) collective-permute-start(bf16[512,1024]{1,0:T(8,128)(2,1)S(1)} %get-tuple-element.31), channel_id=1, source_target_pairs={{0,1},{1,0},{2,3},{3,2},{4,5},{5,4},{6,7},{7,6},{8,9},{9,8},{10,11... | collective-permute-start | bytes 3145736 | tf_op jit(solution)/shard_map/ppermute | solution.py:179
  102.1 1.8 %copy-start.2 = (bf16[256,1024]{1,0:T(8,128)(2,1)}, bf16[256,1024]{1,0:T(8,128)(2,1)S(1)}, u32[]{:S(2)}) copy-start(bf16[256,1024]{1,0:T(8,128)(2,1)S(1)} %get-tuple-element.26) | copy-start | bytes 1572868
  102.1 20.4 %collective-permute-start.14 = (bf16[512,1024]{1,0:T(8,128)(2,1)S(1)}, bf16[512,1024]{1,0:T(8,128)(2,1)}, u32[]{:S(2)}, u32[]{:S(2)}) collective-permute-start(bf16[512,1024]{1,0:T(8,128)(2,1)S(1)} %get-tuple-element.29), channel_id=1, source_target_pairs={{0,1},{1,0},{2,3},{3,2},{4,5},{5,4},{6,7},{7,6},{8,9},{9,8},{10,11... | collective-permute-start | bytes 3145736 | tf_op jit(solution)/shard_map/ppermute | solution.py:179
  103.9 19.4 %collective-permute-start.17 = (bf16[256,1024]{1,0:T(8,128)(2,1)}, bf16[256,1024]{1,0:T(8,128)(2,1)}, u32[]{:S(2)}, u32[]{:S(2)}) collective-permute-start(bf16[256,1024]{1,0:T(8,128)(2,1)} %get-tuple-element.37), channel_id=1, source_target_pairs={{0,4},{4,0},{8,12},{12,8},{16,20},{20,16},{24,28},{28,24},{32,36},... | collective-permute-start | bytes 1572872 | tf_op jit(solution)/shard_map/ppermute | solution.py:176
  109.2 9.2 %collective-permute-start.19 = (f32[1,128]{1,0:T(1,128)S(1)}, f32[1,128]{1,0:T(1,128)S(1)}, u32[]{:S(2)}, u32[]{:S(2)}) collective-permute-start(f32[1,128]{1,0:T(1,128)S(1)} %broadcast_in_dim.3), channel_id=1, source_target_pairs={{0,4},{4,0},{8,12},{12,8},{16,20},{20,16},{24,28},{28,24},{32,36},... | collective-permute-start | bytes 1544 | tf_op jit(solution)/shard_map/ppermute | solution.py:176
  109.4 46.3 %collective-permute-start.13 = (bf16[256,1024]{1,0:T(8,128)(2,1)S(1)}, bf16[256,1024]{1,0:T(8,128)(2,1)S(1)}, u32[]{:S(2)}, u32[]{:S(2)}) collective-permute-start(bf16[256,1024]{1,0:T(8,128)(2,1)S(1)} %convert_element_type.41), channel_id=1, source_target_pairs={{240,0},{248,8},{0,16},{8,24},{16,32},{24,40},{32,48},{40,56},{48,... | collective-permute-start | bytes 1572872 | tf_op jit(solution)/shard_map/ppermute | solution.py:176
  111.3 44.4 %collective-permute-start.12 = (bf16[256,1024]{1,0:T(8,128)(2,1)}, bf16[256,1024]{1,0:T(8,128)(2,1)S(1)}, u32[]{:S(2)}, u32[]{:S(2)}) collective-permute-start(bf16[256,1024]{1,0:T(8,128)(2,1)} %copy-done.2), channel_id=1, source_target_pairs={{252,0},{248,4},{4,8},{0,12},{12,16},{8,20},{20,24},{16,28},{28,32... | collective-permute-start | bytes 1572872 | tf_op jit(solution)/shard_map/ppermute | solution.py:176
  118.4 7.6 %collective-permute-start.20 = (f32[1,128]{1,0:T(1,128)S(1)}, f32[1,128]{1,0:T(1,128)S(1)}, u32[]{:S(2)}, u32[]{:S(2)}) collective-permute-start(f32[1,128]{1,0:T(1,128)S(1)} %broadcast_add_fusion), channel_id=1, source_target_pairs={{0,8},{4,12},{8,0},{12,4},{16,24},{20,28},{24,16},{28,20},{32,40},... | collective-permute-start | bytes 1544 | tf_op jit(solution)/shard_map/ppermute | solution.py:176
  122.4 34.6 %collective-permute-start.16 = (bf16[256,1024]{1,0:T(8,128)(2,1)}, bf16[256,1024]{1,0:T(8,128)(2,1)S(1)}, u32[]{:S(2)}, u32[]{:S(2)}) collective-permute-start(bf16[256,1024]{1,0:T(8,128)(2,1)} %get-tuple-element.36), channel_id=1, source_target_pairs={{0,4},{4,0},{8,12},{12,8},{16,20},{20,16},{24,28},{28,24},{32,36},... | collective-permute-start | bytes 1572872 | tf_op jit(solution)/shard_map/ppermute | solution.py:176
  125.1 31.9 %collective-permute-start.18 = (bf16[256,1024]{1,0:T(8,128)(2,1)S(1)}, bf16[256,1024]{1,0:T(8,128)(2,1)S(1)}, u32[]{:S(2)}, u32[]{:S(2)}) collective-permute-start(bf16[256,1024]{1,0:T(8,128)(2,1)S(1)} %add_convert_fusion), channel_id=1, source_target_pairs={{0,2},{1,3},{2,0},{3,1},{4,6},{5,7},{6,4},{7,5},{8,10},{9,11},{10,... | collective-permute-start | bytes 1572872 | tf_op jit(solution)/shard_map/ppermute | solution.py:179
  126.0 8.0 %collective-permute-start.21 = (f32[1,128]{1,0:T(1,128)S(1)}, f32[1,128]{1,0:T(1,128)S(1)}, u32[]{:S(2)}, u32[]{:S(2)}) collective-permute-start(f32[1,128]{1,0:T(1,128)S(1)} %fusion.12), channel_id=1, source_target_pairs={{0,16},{4,20},{8,24},{12,28},{16,0},{20,4},{24,8},{28,12},{32,48},... | collective-permute-start | bytes 1544 | tf_op jit(solution)/shard_map/ppermute | solution.py:176
  134.0 4.4 %collective-permute-start.22 = (f32[1,128]{1,0:T(1,128)S(1)}, f32[1,128]{1,0:T(1,128)S(1)}, u32[]{:S(2)}, u32[]{:S(2)}) collective-permute-start(f32[1,128]{1,0:T(1,128)S(1)} %add.171), channel_id=1, source_target_pairs={{0,32},{4,36},{8,40},{12,44},{16,48},{20,52},{24,56},{28,60},{32,0... | collective-permute-start | bytes 1544 | tf_op jit(solution)/shard_map/ppermute | solution.py:176
  138.5 7.4 %collective-permute-start.23 = (f32[1,128]{1,0:T(1,128)S(1)}, f32[1,128]{1,0:T(1,128)S(1)}, u32[]{:S(2)}, u32[]{:S(2)}) collective-permute-start(f32[1,128]{1,0:T(1,128)S(1)} %add.172), channel_id=1, source_target_pairs={{0,64},{4,68},{8,72},{12,76},{16,80},{20,84},{24,88},{28,92},{32,9... | collective-permute-start | bytes 1544 | tf_op jit(solution)/shard_map/ppermute | solution.py:176
  145.9 3.5 %collective-permute-start.24 = (f32[1,128]{1,0:T(1,128)S(1)}, f32[1,128]{1,0:T(1,128)S(1)}, u32[]{:S(2)}, u32[]{:S(2)}) collective-permute-start(f32[1,128]{1,0:T(1,128)S(1)} %add.173), channel_id=1, source_target_pairs={{0,128},{4,132},{8,136},{12,140},{16,144},{20,148},{24,152},{28,15... | collective-permute-start | bytes 1544 | tf_op jit(solution)/shard_map/ppermute | solution.py:176
  149.5 1.1 collective-permute-start.25
  150.6 5.0 %collective-permute-start.26 = (f32[1,128]{1,0:T(1,128)S(1)}, f32[1,128]{1,0:T(1,128)S(1)}, u32[]{:S(2)}, u32[]{:S(2)}) collective-permute-start(f32[1,128]{1,0:T(1,128)S(1)} %add.175), channel_id=1, source_target_pairs={{0,2},{1,3},{2,0},{3,1},{4,6},{5,7},{6,4},{7,5},{8,10},{9,11},{10,... | collective-permute-start | bytes 1544 | tf_op jit(solution)/shard_map/ppermute | solution.py:179
  155.7 2.0 %copy-start.5 = (f32[512,1024]{1,0:T(8,128)S(1)}, f32[512,1024]{1,0:T(8,128)}, u32[]{:S(2)}) copy-start(f32[512,1024]{1,0:T(8,128)} %get-tuple-element.28) | copy-start | bytes 6291460
  (1 other events, 1.3 us)

commit v2 on v0

v2 whole, which is shorter than its diff:
```python
import math

import jax
import jax.numpy as jnp
from jax import lax
from jax.experimental import pallas as pl
from jax.experimental.pallas import tpu as pltpu
from jax.sharding import PartitionSpec as P

LOG2E = math.log2(math.e)
LN2 = math.log(2.0)
ORDER = (0, 2, 1, 3)
PLACE = (0, 2, 1, 3)
NT = (((1,), (1,)), ((), ()))
TN = (((0,), (0,)), ((), ()))
F32 = jnp.float32
BF16 = jnp.bfloat16
CORE = jnp.bfloat16
CORE_V = jnp.float32
LANES = 128
VMEM = pl.BlockSpec(memory_space=pltpu.VMEM)
SMEM = pl.BlockSpec(memory_space=pltpu.SMEM)


ANY = pl.BlockSpec(memory_space=pl.ANY)
HBM = pl.BlockSpec(memory_space=pltpu.HBM)


def local_call(kernel, name, specs, shapes, flops, scratch=(), out_specs=None):
    return pl.pallas_call(
        kernel,
        in_specs=specs,
        out_specs=out_specs or [VMEM] * len(shapes),
        out_shape=[jax.ShapeDtypeStruct(*s) for s in shapes],
        scratch_shapes=list(scratch),
        compiler_params=pltpu.CompilerParams(vmem_limit_bytes=16 * 1024 * 1024),
        cost_estimate=pl.CostEstimate(flops=1, bytes_accessed=1, transcendentals=0),
        name=name,
    )


def fetch(sources, targets, sems):
    copies = [pltpu.make_async_copy(s, t, sems.at[i]) for i, (s, t) in enumerate(zip(sources, targets))]
    for copy in copies:
        copy.start()
    return copies


def fetch_y(even, a, y, target, sem):
    @pl.when(even[0] == 1)
    def _():
        pltpu.make_async_copy(y, target, sem).start()

    @pl.when(even[0] != 1)
    def _():
        pltpu.make_async_copy(a, target, sem).start()

    return pltpu.make_async_copy(y, target, sem)


def columns_of(s):
    top = jnp.max(s, axis=0, keepdims=True)
    return top + jnp.log2(jnp.sum(jnp.exp2(s - top), axis=0, keepdims=True))


def rows_of(s_ref, before):
    slabs = range(0, s_ref.shape[1], LANES)
    m = s_ref[:, :LANES]
    for o in slabs[1:]:
        m = jnp.maximum(m, s_ref[:, o:o + LANES])
    top = jnp.max(m, axis=1, keepdims=True)
    if before is not None:
        top = jnp.maximum(top, before)
    else:
        top = jnp.broadcast_to(top, m.shape)
    part = jnp.exp2(s_ref[:, :LANES] - top)
    for o in slabs[1:]:
        part = part + jnp.exp2(s_ref[:, o:o + LANES] - top)
    total = jnp.sum(part, axis=1, keepdims=True)
    if before is not None:
        total = total + jnp.exp2(before - top)
    return jnp.transpose(top + jnp.log2(total))[:1, :]


def spread(vec):
    return jnp.transpose(jnp.broadcast_to(vec, (LANES, vec.shape[1])))


def quarter(order, t, k, rows):
    return t.at[pl.ds(pl.multiple_of(order[k] * rows, rows), rows), :]


def halves(ref, rows):
    return [ref.at[k * rows:(k + 1) * rows, :] for k in range(2)]


def slice_kernel(order, t, half):
    half[...] = t[...]


def own_image_kernel(order, scale, a_in, t_in, s_out, row_ref, col_ref, diag_ref, a, t, s_ref, sems, out_sems):
    rows = a.shape[0]
    copies = fetch([a_in] + [quarter(order, t_in, k, rows) for k in range(4)], [a] + [t.at[k] for k in range(4)], sems)
    mult = scale[0] * LOG2E
    copies[0].wait()
    stores = []
    for k in range(4):
        copies[1 + k].wait()
        cols = slice(k * rows, (k + 1) * rows)
        s_ref[:, cols] = mult * lax.dot_general(a[...], t[k], NT, preferred_element_type=F32)
        stores.append(pltpu.make_async_copy(s_ref.at[:, cols], s_out.at[:, cols], out_sems.at[k]))
        stores[-1].start()
        col_ref[:, cols] = columns_of(s_ref[:, cols])
    sub = s_ref[:, :rows]
    eye = lax.broadcasted_iota(jnp.int32, sub.shape, 0) == lax.broadcasted_iota(jnp.int32, sub.shape, 1)
    diag_ref[...] = jnp.sum(jnp.where(eye, sub, 0.0), axis=0, keepdims=True)
    row_ref[...] = rows_of(s_ref, None)
    for store in stores:
        store.wait()


def x_logits_kernel(order, scale, x_in, t_in, s_out, row_ref, col_ref, x, t, s_ref, sems, out_sems):
    rows = x.shape[0]
    copies = fetch([x_in] + [quarter(order, t_in, k, rows) for k in range(4)], [x] + [t.at[k] for k in range(4)], sems)
    mult = scale[0] * LOG2E
    copies[0].wait()
    stores = []
    for k in range(4):
        copies[1 + k].wait()
        cols = slice(k * rows, (k + 1) * rows)
        s_ref[:, cols] = mult * lax.dot_general(x[...], t[k], NT, preferred_element_type=F32)
        stores.append(pltpu.make_async_copy(s_ref.at[:, cols], s_out.at[:, cols], out_sems.at[k]))
        stores[-1].start()
        col_ref[:, cols] = columns_of(s_ref[:, cols])
    row_ref[...] = rows_of(s_ref, None)
    for store in stores:
        store.wait()


def first_logits_kernel(even, scale, a_in, y_in, x_in, v_in, s_ref, row_ref, col_ref, yx_ref, v, sems):
    rows = a_in.shape[0]
    y_copy = fetch_y(even, a_in, y_in, yx_ref.at[:rows, :], sems.at[3])
    copies = fetch([x_in] + halves(v_in, rows), [yx_ref.at[rows:, :], v.at[0], v.at[1]], sems)
    mult = scale[0] * LOG2E
    y_copy.wait()
    copies[0].wait()
    for k in range(2):
        copies[1 + k].wait()
        cols = slice(k * rows, (k + 1) * rows)
        s_ref[:, cols] = mult * lax.dot_general(yx_ref[...], v[k], NT, preferred_element_type=F32)
        col_ref[:, cols] = columns_of(s_ref[:, cols])
    row_ref[...] = rows_of(s_ref, None)


def far_logits_kernel(scale, before, yx, v_in, s_ref, row_ref, col_ref, v, sems):
    rows = v.shape[1]
    copies = fetch(halves(v_in, rows), [v.at[k] for k in range(2)], sems)
    mult = scale[0] * LOG2E
    for k in range(2):
        copies[k].wait()
        cols = slice(k * rows, (k + 1) * rows)
        s_ref[:, cols] = mult * lax.dot_general(yx[...], v[k], NT, preferred_element_type=F32)
        col_ref[:, cols] = columns_of(s_ref[:, cols])
    row_ref[...] = rows_of(s_ref, spread(before[...]))


def weights_of(s_ref, r, c_ref, k, rows, diagonal=False):
    parts = []
    for o in range(k * rows, (k + 1) * rows, LANES):
        z = s_ref[:, o:o + LANES]
        avg = 0.5 * (jnp.exp2(z - r) + jnp.exp2(z - c_ref[:, o:o + LANES]))
        if diagonal:
            ri = lax.broadcasted_iota(jnp.int32, avg.shape, 0)
            ci = lax.broadcasted_iota(jnp.int32, avg.shape, 1) + o
            avg = avg - jnp.where(ri == ci, 1.0, 0.0)
        parts.append(avg.astype(BF16))
    return jnp.concatenate(parts, 1)


def far_text_kernel(scale, row, col, s, yx, w_ref, g_ref):
    rows = yx.shape[0] // 2
    r = spread(row[...])
    for k in (1, 0):
        w = weights_of(s, r, col, k, rows)
        w_ref[:, k * rows:(k + 1) * rows] = w
        g = lax.dot_general(w, yx[...], TN, preferred_element_type=F32)
        g_ref[k * rows:(k + 1) * rows, :] = (scale[0] * g).astype(g_ref.dtype)


def own_text_kernel(scale, row, col, si_in, sx_in, a_in, yx, w_ref, send_ref, keep_ref, s, a, sems):
    rows = a.shape[0]
    sources, targets = [a_in], [a]
    for k in (2, 3, 0, 1):
        cols = slice(k * rows, (k + 1) * rows)
        sources += [si_in.at[:, cols], sx_in.at[:, cols]]
        targets += [s.at[:rows, cols], s.at[rows:, cols]]
    copies = fetch(sources, targets, sems)
    r = spread(row[...])
    for i, k in enumerate((2, 3, 0, 1)):
        copies[1 + 2 * i].wait()
        copies[2 + 2 * i].wait()
        w = weights_of(s, r, col, k, rows, k == 0)
        w_ref[:, k * rows:(k + 1) * rows] = w
        if i == 0:
            copies[0].wait()
        g = lax.dot_general(w[:rows], a[...], TN, preferred_element_type=F32)
        g = scale[0] * (g + lax.dot_general(w[rows:], yx[rows:, :], TN, preferred_element_type=F32))
        if k >= 2:
            send_ref[(k - 2) * rows:(k - 1) * rows, :] = g.astype(send_ref.dtype)
        else:
            keep_ref[k * rows:(k + 1) * rows, :] = g


def y_grads_kernel(scale, wa, wb, va, vb, g_ref, send_ref, v, sems):
    rows = v.shape[1]
    copies = fetch(halves(va, rows) + halves(vb, rows), [v.at[k] for k in range(4)], sems)
    step = 512
    for o in range(0, g_ref.shape[1], step):
        cols = slice(o, o + step)
        g = 0.0
        for k in range(4):
            if o == 0:
                copies[k].wait()
            w = (wa, wb)[k // 2][:rows, (k % 2) * rows:(k % 2 + 1) * rows]
            g = g + jnp.dot(w, v[k, :, cols], preferred_element_type=F32)
        g_ref[:, cols] = scale[0] * g
        send_ref[:, cols] = (scale[0] * g).astype(BF16)


def image_kernel(order, even, scale, w, t_in, wa, wb, va, vb, gy, gi_ref, gx_ref, t, v, sems):
    rows = t.shape[1]
    sources = [quarter(order, t_in, k, rows) for k in range(4)] + halves(va, rows) + halves(vb, rows)
    copies = fetch(sources, [t.at[k] for k in range(4)] + [v.at[k] for k in range(4)], sems)
    step = 512
    for o in range(0, gi_ref.shape[1], step):
        cols = slice(o, o + step)
        gi = gx = 0.0
        for k in range(4):
            if o == 0:
                copies[k].wait()
                copies[4 + k].wait()
            tk = t[k, :, cols]
            wk = w[:, k * rows:(k + 1) * rows]
            gx = gx + jnp.dot(wk[rows:], tk, preferred_element_type=F32)
            gi = gi + jnp.dot(wk[:rows], tk, preferred_element_type=F32)
            far = (wa, wb)[k // 2][rows:, (k % 2) * rows:(k % 2 + 1) * rows]
            gx = gx + jnp.dot(far, v[k, :, cols], preferred_element_type=F32)
        gi_ref[:, cols] = scale[0] * gi + jnp.where(even[0] == 1, 0.0, gy[:, cols])
        gx_ref[:, cols] = (scale[0] * gx).astype(BF16)


def lse2(*parts):
    top = parts[0]
    for p in parts[1:]:
        top = jnp.maximum(top, p)
    total = sum(jnp.exp2(p - top) for p in parts)
    return top + jnp.log2(total)


def tie(*values):
    return lax.optimization_barrier(values)


def per_device(image_emb, text_emb, logit_scale):
    rows, d = image_emb.shape
    blocks = lax.axis_size("blk")
    rep = lax.axis_index("rep")
    even = lax.axis_index("blk") % 2 == 0
    evens = even.astype(jnp.int32).reshape(1)
    order = jnp.stack([rep ^ m for m in ORDER]).astype(jnp.int32)
    x_route = [(i, (i - 1) % blocks if i % 2 == 0 else (i - 3) % blocks) for i in range(blocks)]
    y_route = [(i, (i - 4) % blocks) for i in range(0, blocks, 2)]
    v_route = [(i, i ^ 1) for i in range(blocks)]
    x_back = [(b, a) for a, b in x_route]
    y_back = [(b, a) for a, b in y_route]
    tile = 2 * rows * rows * d

    def hop(value, route):
        return lax.ppermute(value, "blk", route)

    def swap(value, mask):
        return lax.ppermute(value, "rep", [(i, i ^ mask) for i in range(4)])

    def sems(n):
        return pltpu.SemaphoreType.DMA((n,))

    image_buf = pltpu.VMEM((rows, d), BF16)

    half = pl.pallas_call(
        slice_kernel,
        grid_spec=pltpu.PrefetchScalarGridSpec(
            num_scalar_prefetch=1, grid=(2,),
            in_specs=[pl.BlockSpec((rows, d), lambda k, o: (o[k], 0))],
            out_specs=pl.BlockSpec((rows, d), lambda k, o: (k, 0))),
        out_shape=jax.ShapeDtypeStruct((2 * rows, d), BF16),
        name="quarters",
    )(order, text_emb)
    half, images = tie(half, image_emb)
    va = hop(half, v_route)
    x = hop(images, x_route)
    y = hop(images, y_route)
    wide, narrow = (1, 4 * rows), (1, rows)
    text_buf = pltpu.VMEM((4, rows, d), BF16)
    half_buf = pltpu.VMEM((2, rows, d), BF16)
    logits_buf = pltpu.VMEM((rows, 4 * rows), F32)

    logits_i, r_i, col_i, diag = local_call(
        own_image_kernel, "own_image", [SMEM] * 2 + [HBM] * 2,
        [((rows, 4 * rows), F32), (narrow, F32), (wide, F32), (narrow, F32)], 4 * tile,
        [image_buf, text_buf, logits_buf, sems(5), sems(4)], [HBM, VMEM, VMEM, VMEM],
    )(order, logit_scale, image_emb, text_emb)
    x, logits_i = tie(x, logits_i)
    logits_x, r_xt, col_x = local_call(
        x_logits_kernel, "x_logits", [SMEM] * 2 + [HBM] * 2,
        [((rows, 4 * rows), F32), (narrow, F32), (wide, F32)], 4 * tile,
        [image_buf, text_buf, logits_buf, sems(5), sems(4)], [HBM, VMEM, VMEM],
    )(order, logit_scale, x, text_emb)
    h_y = hop(r_i, y_route)
    va, y, r_xt, logits_x, h_y = tie(va, y, r_xt, logits_x, h_y)
    vb = swap(va, 1)
    s_a, row_a, col_a, yx = local_call(
        first_logits_kernel, "first_logits", [SMEM] * 2 + [HBM] * 4,
        [((2 * rows, 2 * rows), F32), ((1, 2 * rows), F32), ((1, 2 * rows), F32), ((2 * rows, d), BF16)], 4 * tile,
        [half_buf, sems(4)],
    )(evens, logit_scale, image_emb, y, x, va)
    s_b, row_v, col_b = local_call(
        far_logits_kernel, "far_logits", [SMEM, VMEM, VMEM, HBM],
        [((2 * rows, 2 * rows), F32), ((1, 2 * rows), F32), ((1, 2 * rows), F32)], 4 * tile,
        [half_buf, sems(2)],
    )(logit_scale, row_a, yx, vb)

    r_y, r_xv = row_v[:, :rows], row_v[:, rows:]
    r_x = lse2(r_xt, r_xv)
    h_i = jnp.where(even, r_i, lse2(r_i, r_y))
    col_t = lse2(col_i, col_x)
    col_v = jnp.concatenate([col_a, col_b], 1)
    blank = jnp.zeros((1, 3 * rows), F32)
    peer = hop(jnp.concatenate([col_v, col_t, jnp.concatenate([diag, blank], 1)]), v_route)
    down = hop(jnp.concatenate([h_i, r_x], 1), x_route)
    up = hop(jnp.concatenate([r_x, r_y], 1), x_back)
    y_i = hop(r_y, y_back)
    peer, down, up, y_i = tie(peer, down, up, y_i)
    h_x, x_y = down[:, :rows], down[:, rows:]
    x_i, y_x = up[:, :rows], up[:, rows:]
    row_x = jnp.where(even, lse2(h_x, r_x), lse2(h_x, r_x, y_x))
    row_i = jnp.where(even, lse2(r_i, x_i, y_i), lse2(h_i, x_i))
    row_y = jnp.where(even, lse2(r_y, h_y, x_y), row_i)
    row_yx = jnp.concatenate([row_y, row_x], 1)
    row_ix = jnp.concatenate([row_i, row_x], 1)
    pair = row_i + row_x - 2.0 * (diag + peer[2:, :rows])
    columns = jnp.concatenate([lse2(col_t, peer[:1]), lse2(col_v, peer[1:2])])
    stats = jnp.concatenate([columns, jnp.concatenate([pair, blank], 1)])
    got = [swap(stats, mask) for mask in (1, 2, 3)]
    aligned = [columns]
    for mask, g in zip((1, 2, 3), got):
        places = [PLACE[ORDER[k] ^ mask] for k in range(4)]
        aligned.append(jnp.concatenate([g[:2, p * rows:(p + 1) * rows] for p in places], 1))
    columns = lse2(*aligned)
    c_t, c_v = columns[:1], columns[1:]
    pair = sum((g[2:, :rows] for g in got), pair)
    column_sum = c_t + c_v
    loss_part = LN2 * sum((column_sum[:, k * rows:(k + 1) * rows] for k in range(4)), pair)

    def far_text(s, cols, dtype):
        return local_call(
            far_text_kernel, "far_text", [SMEM] + [VMEM] * 4,
            [((2 * rows, 2 * rows), BF16), ((2 * rows, d), dtype)], 4 * tile,
        )(logit_scale, row_yx, cols, s, yx)

    def cross(value, mask):
        return hop(value, [(i, i ^ mask) for i in range(blocks)])

    def ring(value, distance):
        span = blocks // 2
        return hop(value, [((i + 4 * distance) % span + i // span * span, i) for i in range(blocks)])

    w_b, send_v = far_text(s_b, c_v[:, 2 * rows:], CORE_V)
    send_v, s_a = tie(send_v, s_a)
    got_v = swap(send_v, 1)
    got = cross(loss_part, 2)
    w_a, keep_v = far_text(s_a, c_v[:, :2 * rows], F32)
    keep_v, got_v, got = tie(keep_v, got_v, got)
    loss_part = loss_part + got
    v_one = (keep_v[rows:] + got_v[rows:].astype(F32)).astype(BF16)
    v_zero = (keep_v[:rows] + got_v[:rows].astype(F32)).astype(BF16)
    v_one, v_zero, logits_x, loss_part, w_a = tie(v_one, v_zero, logits_x, loss_part, w_a)
    home_1 = hop(v_one, v_route)
    home_0 = hop(v_zero, v_route)
    g_y, g_y_send = local_call(
        y_grads_kernel, "y_grads", [SMEM] + [VMEM] * 2 + [HBM] * 2,
        [((rows, d), F32), ((rows, d), BF16)], 4 * tile, [text_buf, sems(4)],
    )(logit_scale, w_a, w_b, va, vb)
    y_got = hop(g_y_send, y_back)
    logits_x, g_y, loss_part = tie(logits_x, g_y, loss_part)
    got = cross(loss_part, blocks // 2)
    w_t, send_t, keep_t = local_call(
        own_text_kernel, "own_text", [SMEM] + [VMEM] * 2 + [HBM] * 3 + [VMEM],
        [((2 * rows, 4 * rows), BF16), ((2 * rows, d), CORE), ((2 * rows, d), F32)], 8 * tile,
        [pltpu.VMEM((2 * rows, 4 * rows), F32), image_buf, sems(9)],
    )(logit_scale, row_ix, c_t, logits_i, logits_x, image_emb, yx)
    send_t, got = tie(send_t, got)
    loss_part = loss_part + got
    got_one = swap(send_t[rows:], 1)
    got_zero = swap(send_t[:rows], 1)
    got = ring(loss_part, 1)
    g_i, g_x = local_call(
        image_kernel, "image_grads", [SMEM] * 3 + [VMEM, HBM, VMEM, VMEM, HBM, HBM, VMEM],
        [((rows, d), F32), ((rows, d), BF16)], 16 * tile, [text_buf, text_buf, sems(8)],
    )(order, evens, logit_scale, w_t, text_emb, w_a, w_b, va, vb, g_y)
    g_x, got, got_one = tie(g_x, got, got_one)
    loss_part = loss_part + got
    x_got = hop(g_x, x_back)
    loss_part = loss_part + ring(loss_part, 2)
    part = keep_t[rows:] + got_one.astype(F32)
    part, home_1, loss_part = tie(part, home_1, loss_part)
    one = (part + home_1.astype(F32)).astype(BF16)
    one, loss_part = tie(one, loss_part)
    across = swap(one, 2)
    loss_part = loss_part + ring(loss_part, 4)
    loss = jnp.sum(loss_part, axis=1) / (2.0 * rows * blocks * 4)
    base = keep_t[:rows] + got_zero.astype(F32)
    grad_text = base + home_0.astype(F32) + across.astype(F32)
    grad_image = g_i + x_got.astype(F32) + jnp.where(even, y_got, jnp.zeros_like(y_got)).astype(F32)
    return grad_image, grad_text, loss


def solution(mesh):
    placed = (P(("blk", "rep"), None), P("blk", None), P())
    return jax.shard_map(
        per_device,
        mesh=mesh,
        in_specs=placed,
        out_specs=(P(("blk", "rep"), None), P(("blk", "rep"), None), P()),
        check_vma=False,
    )
```

time: 677 us -> 126 us (0.19)
  waiting for transfers between devices: 488 us -> 36.7 us
  blocking collectives: 91.5 us -> 0 us
  Pallas kernels: 0 us -> 26.5 us
  matrix products: 23.6 us -> 0 us
  between operations: 18.7 us -> 3.44 us
    ppermute x17 -> x25, waiting for transfers between devices: 488 us -> 36.7 us  [the longest x17 23.3 us: hop(): return lax.ppermute(value, 'blk', route)]
    psum x1 -> x0, blocking collectives: 78.2 us -> none  [per_device(): loss_sum = lax.psum(local_loss, ('blk', 'rep'))]
    pallas_call x0 -> x10, Pallas kernels: none -> 26.5 us  [the longest x1 4.14 us: per_device(): local_call(image_kernel, 'image_grads', [SMEM] * 3 + [VMEM, HBM, VMEM, VM...]
    dot_general x12 -> x0, matrix products: 23.6 us -> none  [the longest x4 9.9 us: pair_logits(): lax.dot_general(images, captions, (((1,), (1,)), ((), ())), preferred_ele...]
    all_gather x2 -> x0, blocking collectives: 13.4 us -> none  [joined(): gathered = jax.tree.map(lambda a: lax.all_gather(a, axis), part)]
    ppermute x17 -> x25, starting transfers between devices: 46 us -> 42.7 us  [the longest x17 37.4 us: hop(): return lax.ppermute(value, 'blk', route)]
  transfers between devices with their start and end apart: 18 -> 25, of which waited for: 12 -> 10; matrix products, arithmetic and copies ran while one was open for 4% -> 4% of each run, Pallas kernels for 0% -> 13%
where the time goes in v2:
time: 126 us
  starting transfers between devices  42.7 us (34%)
  waiting for transfers between devices  36.7 us (29%)
  Pallas kernels  26.5 us (21%)
  other arithmetic  8.72 us (7%)
  local copies, waits for them, and re-layouts  7.88 us (6%)
  between operations  3.44 us (3%)
    ppermute x17, starting transfers between devices, hop(): return lax.ppermute(value, 'blk', route)  37.4 us
    ppermute x17, waiting for transfers between devices, hop(): return lax.ppermute(value, 'blk', route)  23.3 us
    ppermute x8, waiting for transfers between devices, swap(): return lax.ppermute(value, 'rep', [(i, i ^ mask) for i in range(4)])  13.3 us
    unnamed x33, local copies, waits for them, and re-layouts  6.98 us
    ppermute x8, starting transfers between devices, swap(): return lax.ppermute(value, 'rep', [(i, i ^ mask) for i in range(4)])  5.24 us
    pallas_call x1, Pallas kernels, per_device(): local_call(image_kernel, 'image_grads', [SMEM] * 3 + [VMEM, HBM, VMEM, VM...  4.14 us
    pallas_call x1, Pallas kernels, per_device(): local_call(x_logits_kernel, 'x_logits', [SMEM] * 2 + [HBM] * 2, [((rows,...  3.4 us
    pallas_call x1, Pallas kernels, per_device(): local_call(own_image_kernel, 'own_image', [SMEM] * 2 + [HBM] * 2, [((rows...  3.4 us
  transfers between devices with their start and end apart: 25, of which 10 were waited for; matrix products, arithmetic and copies ran while one was open for 4% of the time, Pallas kernels for 13%

profile of v2, /device:TPU:16, one launch (start us, length us, event | category | flops | bytes accessed | tf_op | source)
XLA Modules:
  0.0 125.9 jit_solution(5008827321530465034)
XLA Ops:
  1.2 2.9 %quarters.1 = bf16[512,1024]{1,0:T(8,128)(2,1)} custom-call(s32[4]{0:T(128)} %pad_add_fusion.order, bf16[1024,1024]{1,0:T(8,128)(2,1)} %t_in.5), custom_call_target="tpu_custom_call" | custom-call | tf_op jit(solution)/shard_map/quarters/pallas_call | solution.py:289
  4.1 1.3 %collective-permute-start = (bf16[512,1024]{1,0:T(8,128)(2,1)}, bf16[512,1024]{1,0:T(8,128)(2,1)S(1)}, u32[]{:S(2)}, u32[]{:S(2)}) collective-permute-start(bf16[512,1024]{1,0:T(8,128)(2,1)} %quarters.1), channel_id=1, source_target_pairs={{0,4},{4,0},{8,12},{12,8},{16,20},{20,16},{24,28},{28,24},{32,36},... | collective-permute-start | bytes 3145736 | tf_op jit(solution)/shard_map/ppermute | solution.py:279
  5.3 1.4 %collective-permute-start.2 = (bf16[256,1024]{1,0:T(8,128)(2,1)}, bf16[256,1024]{1,0:T(8,128)(2,1)S(1)}, u32[]{:S(2)}, u32[]{:S(2)}) collective-permute-start(bf16[256,1024]{1,0:T(8,128)(2,1)} %a_in.5), channel_id=1, source_target_pairs={{0,252},{4,248},{8,4},{12,0},{16,12},{20,8},{24,20},{28,16},{32,28... | collective-permute-start | bytes 1572872 | tf_op jit(solution)/shard_map/ppermute | solution.py:279
  6.7 7.3 %collective-permute-start.1 = (bf16[256,1024]{1,0:T(8,128)(2,1)}, bf16[256,1024]{1,0:T(8,128)(2,1)S(1)}, u32[]{:S(2)}, u32[]{:S(2)}) collective-permute-start(bf16[256,1024]{1,0:T(8,128)(2,1)} %a_in.5), channel_id=1, source_target_pairs={{0,240},{8,248},{16,0},{24,8},{32,16},{40,24},{48,32},{56,40},{64,... | collective-permute-start | bytes 1572872 | tf_op jit(solution)/shard_map/ppermute | solution.py:279
  15.8 3.4 %own_image.1 = (f32[256,1024]{1,0:T(8,128)S(1)}, f32[1,256]{1,0:T(1,128)S(1)}, f32[1,1024]{1,0:T(1,128)S(1)}, f32[1,256]{1,0:T(1,128)S(1)}) custom-call(s32[4]{0:T(128)S(1)} %copy-done.15, f32[1]{0:T(128)S(6)} %copy.7.scale, bf16[256,1024]{1,0:T(8,128)(2,1)S(1)} %copy-done.1, bf16[1024,1024]{1,0:T(8,128)(2,1)S(1)} %copy-done), custom_call_target="tpu_custom_call" | custom-call | flops 1 | bytes 1 | tf_op jit(solution)/shard_map/own_image/pallas_call | solution.py:307
  20.1 2.9 %collective-permute-start.3 = (f32[1,256]{1,0:T(1,128)S(1)}, f32[1,256]{1,0:T(1,128)S(1)}, u32[]{:S(2)}, u32[]{:S(2)}) collective-permute-start(f32[1,256]{1,0:T(1,128)S(1)} %get-tuple-element.64), channel_id=1, source_target_pairs={{0,240},{8,248},{16,0},{24,8},{32,16},{40,24},{48,32},{56,40},{64,... | collective-permute-start | bytes 3080 | tf_op jit(solution)/shard_map/ppermute | solution.py:279
  23.1 3.4 %x_logits.1 = (f32[256,1024]{1,0:T(8,128)S(1)}, f32[1,256]{1,0:T(1,128)S(1)}, f32[1,1024]{1,0:T(1,128)S(1)}) custom-call(s32[4]{0:T(128)S(1)} %copy-done.15, f32[1]{0:T(128)S(6)} %copy.7.scale, bf16[256,1024]{1,0:T(8,128)(2,1)S(1)} %collective-permute-done.2.x_in, bf16[1024,1024]{1,0:T(8,128)(2,1)S(1)} %copy-done), custom_call_target="tpu_custom_call" | custom-call | flops 1 | bytes 1 | tf_op jit(solution)/shard_map/x_logits/pallas_call | solution.py:313
  32.3 2.1 %first_logits.1 = (f32[512,512]{1,0:T(8,128)S(1)}, f32[1,512]{1,0:T(1,128)S(1)}, f32[1,512]{1,0:T(1,128)S(1)}, bf16[512,1024]{1,0:T(8,128)(2,1)S(1)}) custom-call(s32[1]{0:T(128)} %bitcast.4.even, f32[1]{0:T(128)S(6)} %copy.7.scale, bf16[256,1024]{1,0:T(8,128)(2,1)S(1)} %copy-done.2, bf16[256,1024]{1,0:T(8,128)(2,1)S(1)} %copy-done.14, ...), custom_call_target="tpu_custom_call" | custom-call | flops 1 | bytes 1 | tf_op jit(solution)/shard_map/first_logits/pallas_call | solution.py:321
  34.5 3.0 %far_logits.1 = (f32[512,512]{1,0:T(8,128)S(1)}, f32[1,512]{1,0:T(1,128)S(1)}, f32[1,512]{1,0:T(1,128)S(1)}) custom-call(f32[1]{0:T(128)S(6)} %copy.7.scale, f32[1,512]{1,0:T(1,128)S(1)} %get-tuple-element.74.before, bf16[512,1024]{1,0:T(8,128)(2,1)S(1)} %get-tuple-element.75.yx, bf16[512,1024]{1,0:T(8,128)(2,1)} %collective-permute-done.4.v_in.vb), custom_call_target="tpu_custom_call" | custom-call | flops 1 | bytes 1 | tf_op jit(solution)/shard_map/far_logits/pallas_call | solution.py:326
  37.6 1.4 %collective-permute-start.5 = (f32[3,1024]{1,0:T(4,128)S(1)}, f32[3,1024]{1,0:T(4,128)S(1)}, u32[]{:S(2)}, u32[]{:S(2)}) collective-permute-start(f32[3,1024]{1,0:T(4,128)S(1)} %select_maximum_fusion.1), channel_id=1, source_target_pairs={{0,4},{4,0},{8,12},{12,8},{16,20},{20,16},{24,28},{28,24},{32,36},... | collective-permute-start | bytes 36872 | tf_op jit(solution)/shard_map/ppermute | solution.py:279
  39.0 7.9 %collective-permute-start.6 = (f32[1,512]{1,0:T(1,128)S(1)}, f32[1,512]{1,0:T(1,128)S(1)}, u32[]{:S(2)}, u32[]{:S(2)}) collective-permute-start(f32[1,512]{1,0:T(1,128)S(1)} %get-tuple-element.155), channel_id=1, source_target_pairs={{0,252},{4,248},{8,4},{12,0},{16,12},{20,8},{24,20},{28,16},{32,28... | collective-permute-start | bytes 6152 | tf_op jit(solution)/shard_map/ppermute | solution.py:279
  46.9 1.9 %collective-permute-start.8 = (f32[1,256]{1,0:T(1,128)S(1)}, f32[1,256]{1,0:T(1,128)S(1)}, u32[]{:S(2)}, u32[]{:S(2)}) collective-permute-start(f32[1,256]{1,0:T(1,128)S(1)} %get-tuple-element.149), channel_id=1, source_target_pairs={{240,0},{248,8},{0,16},{8,24},{16,32},{24,40},{32,48},{40,56},{48,... | collective-permute-start | bytes 3080 | tf_op jit(solution)/shard_map/ppermute | solution.py:279
  48.8 6.1 %collective-permute-done.8 = f32[1,256]{1,0:T(1,128)S(1)} collective-permute-done((f32[1,256]{1,0:T(1,128)S(1)}, f32[1,256]{1,0:T(1,128)S(1)}, u32[]{:S(2)}, u32[]{:S(2)}) %collective-permute-start.8) | collective-permute-done | bytes 1056 | tf_op jit(solution)/shard_map/ppermute | solution.py:279
  55.1 2.8 %collective-permute-start.10 = (f32[3,1024]{1,0:T(4,128)S(1)}, f32[3,1024]{1,0:T(4,128)S(1)}, u32[]{:S(2)}, u32[]{:S(2)}) collective-permute-start(f32[3,1024]{1,0:T(4,128)S(1)} %select_maximum_fusion), channel_id=1, source_target_pairs={{0,2},{1,3},{2,0},{3,1},{4,6},{5,7},{6,4},{7,5},{8,10},{9,11},{10,... | collective-permute-start | bytes 36872 | tf_op jit(solution)/shard_map/ppermute | solution.py:282
  58.5 2.0 %collective-permute-done.10 = f32[3,1024]{1,0:T(4,128)S(1)} collective-permute-done((f32[3,1024]{1,0:T(4,128)S(1)}, f32[3,1024]{1,0:T(4,128)S(1)}, u32[]{:S(2)}, u32[]{:S(2)}) %collective-permute-start.10) | collective-permute-done | bytes 12320 | tf_op jit(solution)/shard_map/ppermute | solution.py:282
  60.4 2.2 %collective-permute-done.11 = f32[3,1024]{1,0:T(4,128)S(1)} collective-permute-done((f32[3,1024]{1,0:T(4,128)S(1)}, f32[3,1024]{1,0:T(4,128)S(1)}, u32[]{:S(2)}, u32[]{:S(2)}) %collective-permute-start.11) | collective-permute-done | bytes 12320 | tf_op jit(solution)/shard_map/ppermute | solution.py:282
  64.0 2.8 %collective-permute-start.13 = (f32[1,256]{1,0:T(1,128)S(1)}, f32[1,256]{1,0:T(1,128)S(1)}, u32[]{:S(2)}, u32[]{:S(2)}) collective-permute-start(f32[1,256]{1,0:T(1,128)S(1)} %fusion.3), channel_id=1, source_target_pairs={{0,8},{4,12},{8,0},{12,4},{16,24},{20,28},{24,16},{28,20},{32,40},... | collective-permute-start | bytes 3080 | tf_op jit(solution)/shard_map/ppermute | solution.py:279
  67.8 1.3 %collective-permute-done.13 = f32[1,256]{1,0:T(1,128)S(1)} collective-permute-done((f32[1,256]{1,0:T(1,128)S(1)}, f32[1,256]{1,0:T(1,128)S(1)}, u32[]{:S(2)}, u32[]{:S(2)}) %collective-permute-start.13) | collective-permute-done | bytes 1056 | tf_op jit(solution)/shard_map/ppermute | solution.py:279
  69.2 1.1 add_convert_fusion.1
  70.3 2.8 %y_grads.1 = (f32[256,1024]{1,0:T(8,128)S(1)}, bf16[256,1024]{1,0:T(8,128)(2,1)}) custom-call(f32[1]{0:T(128)S(6)} %copy.7.scale, bf16[512,512]{1,0:T(8,128)(2,1)S(1)} %get-tuple-element.100.wa, bf16[512,512]{1,0:T(8,128)(2,1)S(1)} %get-tuple-element.101.wb, bf16[512,1024]{1,0:T(8,128)(2,1)S(1)} %collective-permute-done.v_in.va, ...), custom_call_target="tpu_custom_call" | custom-call | flops 1 | bytes 1 | tf_op jit(solution)/shard_map/y_grads/pallas_call | solution.py:389
  73.4 2.7 %own_text.1 = (bf16[512,1024]{1,0:T(8,128)(2,1)S(1)}, bf16[512,1024]{1,0:T(8,128)(2,1)S(1)}, f32[512,1024]{1,0:T(8,128)S(1)}) custom-call(f32[1]{0:T(128)S(6)} %copy.7.scale, f32[1,512]{1,0:T(1,128)S(1)} %get-tuple-element.153.row, f32[1,1024]{1,0:T(1,128)S(1)} %get-tuple-element.146.col, f32[256,1024]{1,0:T(8,128)S(1)} %copy-done.10, ...), custom_call_target="tpu_custom_call" | custom-call | flops 1 | bytes 1 | tf_op jit(solution)/shard_map/own_text/pallas_call | solution.py:396
  77.6 1.8 %collective-permute-start.15 = (f32[1,256]{1,0:T(1,128)S(1)}, f32[1,256]{1,0:T(1,128)S(1)}, u32[]{:S(2)}, u32[]{:S(2)}) collective-permute-start(f32[1,256]{1,0:T(1,128)S(1)} %add.202), channel_id=1, source_target_pairs={{16,0},{20,4},{24,8},{28,12},{32,16},{36,20},{40,24},{44,28},{48,3... | collective-permute-start | bytes 3080 | tf_op jit(solution)/shard_map/ppermute | solution.py:279
  79.4 2.2 %collective-permute-start.18 = (bf16[256,1024]{1,0:T(8,128)(2,1)}, bf16[256,1024]{1,0:T(8,128)(2,1)}, u32[]{:S(2)}, u32[]{:S(2)}) collective-permute-start(bf16[256,1024]{1,0:T(8,128)(2,1)} %get-tuple-element.114), channel_id=1, source_target_pairs={{240,0},{248,8},{0,16},{8,24},{16,32},{24,40},{32,48},{40,56},{48,... | collective-permute-start | bytes 1572872 | tf_op jit(solution)/shard_map/ppermute | solution.py:279
  81.6 4.1 %image_grads.1 = (f32[256,1024]{1,0:T(8,128)S(1)}, bf16[256,1024]{1,0:T(8,128)(2,1)}) custom-call(s32[4]{0:T(128)S(1)} %copy-done.15, s32[1]{0:T(128)} %bitcast.4.even, f32[1]{0:T(128)S(6)} %copy.7.scale, bf16[512,1024]{1,0:T(8,128)(2,1)S(1)} %get-tuple-element.105.w, bf16[1024,1024]{1,0:T(8,128)(2,1)S(1)} %copy-done, ...), custom_call_target="tpu_custom_call" | custom-call | flops 1 | bytes 1 | tf_op jit(solution)/shard_map/image_grads/pallas_call | solution.py:406
  85.8 2.7 %collective-permute-start.22 = (f32[1,256]{1,0:T(1,128)S(1)}, f32[1,256]{1,0:T(1,128)S(1)}, u32[]{:S(2)}, u32[]{:S(2)}) collective-permute-start(f32[1,256]{1,0:T(1,128)S(1)} %add.208), channel_id=1, source_target_pairs={{32,0},{36,4},{40,8},{44,12},{48,16},{52,20},{56,24},{60,28},{64,3... | collective-permute-start | bytes 3080 | tf_op jit(solution)/shard_map/ppermute | solution.py:279
  90.4 1.6 %collective-permute-done.21 = bf16[256,1024]{1,0:T(8,128)(2,1)S(1)} collective-permute-done((bf16[256,1024]{1,0:T(8,128)(2,1)S(1)}, bf16[256,1024]{1,0:T(8,128)(2,1)S(1)}, u32[]{:S(2)}, u32[]{:S(2)}) %collective-permute-start.21) | collective-permute-done | bytes 524320 | tf_op jit(solution)/shard_map/ppermute | solution.py:279
  92.9 2.7 %collective-permute-start.24 = (f32[1,256]{1,0:T(1,128)S(1)}, f32[1,256]{1,0:T(1,128)S(1)}, u32[]{:S(2)}, u32[]{:S(2)}) collective-permute-start(f32[1,256]{1,0:T(1,128)S(1)} %add.209), channel_id=1, source_target_pairs={{64,0},{68,4},{72,8},{76,12},{80,16},{84,20},{88,24},{92,28},{96,3... | collective-permute-start | bytes 3080 | tf_op jit(solution)/shard_map/ppermute | solution.py:279
  95.9 11.8 %collective-permute-done.24 = f32[1,256]{1,0:T(1,128)S(1)} collective-permute-done((f32[1,256]{1,0:T(1,128)S(1)}, f32[1,256]{1,0:T(1,128)S(1)}, u32[]{:S(2)}, u32[]{:S(2)}) %collective-permute-start.24) | collective-permute-done | bytes 1056 | tf_op jit(solution)/shard_map/ppermute | solution.py:279
  107.7 1.5 %collective-permute-start.23 = (bf16[256,1024]{1,0:T(8,128)(2,1)}, bf16[256,1024]{1,0:T(8,128)(2,1)}, u32[]{:S(2)}, u32[]{:S(2)}) collective-permute-start(bf16[256,1024]{1,0:T(8,128)(2,1)} %add_convert_fusion), channel_id=1, source_target_pairs={{0,2},{1,3},{2,0},{3,1},{4,6},{5,7},{6,4},{7,5},{8,10},{9,11},{10,... | collective-permute-start | bytes 1572872 | tf_op jit(solution)/shard_map/ppermute | solution.py:282
  110.5 2.7 %convert_add_fusion.2 = f32[256,1024]{1,0:T(8,128)} fusion(f32[256,1024]{1,0:T(8,128)} %copy-done.8, bf16[256,1024]{1,0:T(8,128)(2,1)} %collective-permute-done.17, bf16[256,1024]{1,0:T(8,128)(2,1)} %collective-permute-done.18, pred[]{:T(512)S(6)} %eq.5), kind=kLoop, calls=%fused_computation.3 | loop fusion | flops 1310720 | bytes 3145729 | tf_op jit(solution)/shard_map/add | solution.py:423
  113.3 9.2 %collective-permute-done.23 = bf16[256,1024]{1,0:T(8,128)(2,1)} collective-permute-done((bf16[256,1024]{1,0:T(8,128)(2,1)}, bf16[256,1024]{1,0:T(8,128)(2,1)}, u32[]{:S(2)}, u32[]{:S(2)}) %collective-permute-start.23) | collective-permute-done | bytes 524320 | tf_op jit(solution)/shard_map/ppermute | solution.py:282
  122.5 2.3 %convert_add_fusion = f32[256,1024]{1,0:T(8,128)} fusion(bf16[256,1024]{1,0:T(8,128)(2,1)} %collective-permute-done.23, bf16[256,1024]{1,0:T(8,128)(2,1)S(1)} %collective-permute-done.20, bf16[256,1024]{1,0:T(8,128)(2,1)S(1)} %collective-permute-done.19, f32[512,1024]{1,0:T(8,128)S(1)} %copy-done.7), kind=kLoop, calls=%fused_computation | loop fusion | flops 1572864 | bytes 3670016 | tf_op jit(solution)/shard_map/add | solution.py:422
  (89 shorter events, 17.2 us)
Async XLA Ops:
  0.6 14.1 %copy-start = (bf16[1024,1024]{1,0:T(8,128)(2,1)S(1)}, bf16[1024,1024]{1,0:T(8,128)(2,1)}, u32[]{:S(2)}) copy-start(bf16[1024,1024]{1,0:T(8,128)(2,1)} %t_in.5) | copy-start | bytes 6291460
  1.2 13.5 %copy-start.15 = (s32[4]{0:T(128)S(1)}, s32[4]{0:T(128)}, u32[]{:S(2)}) copy-start(s32[4]{0:T(128)} %pad_add_fusion.order) | copy-start | bytes 52
  4.1 25.1 %collective-permute-start = (bf16[512,1024]{1,0:T(8,128)(2,1)}, bf16[512,1024]{1,0:T(8,128)(2,1)S(1)}, u32[]{:S(2)}, u32[]{:S(2)}) collective-permute-start(bf16[512,1024]{1,0:T(8,128)(2,1)} %quarters.1), channel_id=1, source_target_pairs={{0,4},{4,0},{8,12},{12,8},{16,20},{20,16},{24,28},{28,24},{32,36},... | collective-permute-start | bytes 3145736 | tf_op jit(solution)/shard_map/ppermute | solution.py:279
  5.3 17.7 %collective-permute-start.2 = (bf16[256,1024]{1,0:T(8,128)(2,1)}, bf16[256,1024]{1,0:T(8,128)(2,1)S(1)}, u32[]{:S(2)}, u32[]{:S(2)}) collective-permute-start(bf16[256,1024]{1,0:T(8,128)(2,1)} %a_in.5), channel_id=1, source_target_pairs={{0,252},{4,248},{8,4},{12,0},{16,12},{20,8},{24,20},{28,16},{32,28... | collective-permute-start | bytes 1572872 | tf_op jit(solution)/shard_map/ppermute | solution.py:279
  6.7 20.8 %collective-permute-start.1 = (bf16[256,1024]{1,0:T(8,128)(2,1)}, bf16[256,1024]{1,0:T(8,128)(2,1)S(1)}, u32[]{:S(2)}, u32[]{:S(2)}) collective-permute-start(bf16[256,1024]{1,0:T(8,128)(2,1)} %a_in.5), channel_id=1, source_target_pairs={{0,240},{8,248},{16,0},{24,8},{32,16},{40,24},{48,32},{56,40},{64,... | collective-permute-start | bytes 1572872 | tf_op jit(solution)/shard_map/ppermute | solution.py:279
  20.1 7.4 %collective-permute-start.3 = (f32[1,256]{1,0:T(1,128)S(1)}, f32[1,256]{1,0:T(1,128)S(1)}, u32[]{:S(2)}, u32[]{:S(2)}) collective-permute-start(f32[1,256]{1,0:T(1,128)S(1)} %get-tuple-element.64), channel_id=1, source_target_pairs={{0,240},{8,248},{16,0},{24,8},{32,16},{40,24},{48,32},{56,40},{64,... | collective-permute-start | bytes 3080 | tf_op jit(solution)/shard_map/ppermute | solution.py:279
  23.1 6.1 %copy-start.4 = (bf16[256,1024]{1,0:T(8,128)(2,1)}, bf16[256,1024]{1,0:T(8,128)(2,1)S(1)}, u32[]{:S(2)}) copy-start(bf16[256,1024]{1,0:T(8,128)(2,1)S(1)} %collective-permute-done.2.x_in) | copy-start | bytes 1572868
  29.2 5.3 %collective-permute-start.4 = (bf16[512,1024]{1,0:T(8,128)(2,1)S(1)}, bf16[512,1024]{1,0:T(8,128)(2,1)}, u32[]{:S(2)}, u32[]{:S(2)}) collective-permute-start(bf16[512,1024]{1,0:T(8,128)(2,1)S(1)} %collective-permute-done.v_in.va), channel_id=1, source_target_pairs={{0,1},{1,0},{2,3},{3,2},{4,5},{5,4},{6,7},{7,6},{8,9},{9,8},{10,11... | collective-permute-start | bytes 3145736 | tf_op jit(solution)/shard_map/ppermute | solution.py:282
  37.6 17.3 %collective-permute-start.5 = (f32[3,1024]{1,0:T(4,128)S(1)}, f32[3,1024]{1,0:T(4,128)S(1)}, u32[]{:S(2)}, u32[]{:S(2)}) collective-permute-start(f32[3,1024]{1,0:T(4,128)S(1)} %select_maximum_fusion.1), channel_id=1, source_target_pairs={{0,4},{4,0},{8,12},{12,8},{16,20},{20,16},{24,28},{28,24},{32,36},... | collective-permute-start | bytes 36872 | tf_op jit(solution)/shard_map/ppermute | solution.py:279
  39.0 15.8 %collective-permute-start.6 = (f32[1,512]{1,0:T(1,128)S(1)}, f32[1,512]{1,0:T(1,128)S(1)}, u32[]{:S(2)}, u32[]{:S(2)}) collective-permute-start(f32[1,512]{1,0:T(1,128)S(1)} %get-tuple-element.155), channel_id=1, source_target_pairs={{0,252},{4,248},{8,4},{12,0},{16,12},{20,8},{24,20},{28,16},{32,28... | collective-permute-start | bytes 6152 | tf_op jit(solution)/shard_map/ppermute | solution.py:279
  46.9 8.0 %collective-permute-start.7 = (f32[1,512]{1,0:T(1,128)S(1)}, f32[1,512]{1,0:T(1,128)S(1)}, u32[]{:S(2)}, u32[]{:S(2)}) collective-permute-start(f32[1,512]{1,0:T(1,128)S(1)} %get-tuple-element.154), channel_id=1, source_target_pairs={{252,0},{248,4},{4,8},{0,12},{12,16},{8,20},{20,24},{16,28},{28,32... | collective-permute-start | bytes 6152 | tf_op jit(solution)/shard_map/ppermute | solution.py:279
  46.9 8.0 %collective-permute-start.8 = (f32[1,256]{1,0:T(1,128)S(1)}, f32[1,256]{1,0:T(1,128)S(1)}, u32[]{:S(2)}, u32[]{:S(2)}) collective-permute-start(f32[1,256]{1,0:T(1,128)S(1)} %get-tuple-element.149), channel_id=1, source_target_pairs={{240,0},{248,8},{0,16},{8,24},{16,32},{24,40},{32,48},{40,56},{48,... | collective-permute-start | bytes 3080 | tf_op jit(solution)/shard_map/ppermute | solution.py:279
  55.0 3.5 %collective-permute-start.9 = (f32[3,1024]{1,0:T(4,128)S(1)}, f32[3,1024]{1,0:T(4,128)S(1)}, u32[]{:S(2)}, u32[]{:S(2)}) collective-permute-start(f32[3,1024]{1,0:T(4,128)S(1)} %select_maximum_fusion), channel_id=1, source_target_pairs={{0,1},{1,0},{2,3},{3,2},{4,5},{5,4},{6,7},{7,6},{8,9},{9,8},{10,11... | collective-permute-start | bytes 36872 | tf_op jit(solution)/shard_map/ppermute | solution.py:282
  55.1 5.3 %collective-permute-start.10 = (f32[3,1024]{1,0:T(4,128)S(1)}, f32[3,1024]{1,0:T(4,128)S(1)}, u32[]{:S(2)}, u32[]{:S(2)}) collective-permute-start(f32[3,1024]{1,0:T(4,128)S(1)} %select_maximum_fusion), channel_id=1, source_target_pairs={{0,2},{1,3},{2,0},{3,1},{4,6},{5,7},{6,4},{7,5},{8,10},{9,11},{10,... | collective-permute-start | bytes 36872 | tf_op jit(solution)/shard_map/ppermute | solution.py:282
  57.9 4.7 %collective-permute-start.11 = (f32[3,1024]{1,0:T(4,128)S(1)}, f32[3,1024]{1,0:T(4,128)S(1)}, u32[]{:S(2)}, u32[]{:S(2)}) collective-permute-start(f32[3,1024]{1,0:T(4,128)S(1)} %select_maximum_fusion), channel_id=1, source_target_pairs={{0,3},{1,2},{2,1},{3,0},{4,7},{5,6},{6,5},{7,4},{8,11},{9,10},{10,... | collective-permute-start | bytes 36872 | tf_op jit(solution)/shard_map/ppermute | solution.py:282
  63.7 5.4 %collective-permute-start.12 = (f32[512,1024]{1,0:T(8,128)S(1)}, f32[512,1024]{1,0:T(8,128)S(1)}, u32[]{:S(2)}, u32[]{:S(2)}) collective-permute-start(f32[512,1024]{1,0:T(8,128)S(1)} %get-tuple-element.93), channel_id=1, source_target_pairs={{0,1},{1,0},{2,3},{3,2},{4,5},{5,4},{6,7},{7,6},{8,9},{9,8},{10,11... | collective-permute-start | bytes 6291464 | tf_op jit(solution)/shard_map/ppermute | solution.py:282
  64.0 5.2 %collective-permute-start.13 = (f32[1,256]{1,0:T(1,128)S(1)}, f32[1,256]{1,0:T(1,128)S(1)}, u32[]{:S(2)}, u32[]{:S(2)}) collective-permute-start(f32[1,256]{1,0:T(1,128)S(1)} %fusion.3), channel_id=1, source_target_pairs={{0,8},{4,12},{8,0},{12,4},{16,24},{20,28},{24,16},{28,20},{32,40},... | collective-permute-start | bytes 3080 | tf_op jit(solution)/shard_map/ppermute | solution.py:279
  70.3 3.1 %copy-start.12 = (f32[256,1024]{1,0:T(8,128)S(1)}, f32[256,1024]{1,0:T(8,128)}, u32[]{:S(2)}) copy-start(f32[256,1024]{1,0:T(8,128)} %copy-done.11) | copy-start | bytes 3145732
  73.0 3.7 %collective-permute-start.14 = (f32[1,256]{1,0:T(1,128)S(1)}, f32[1,256]{1,0:T(1,128)S(1)}, u32[]{:S(2)}, u32[]{:S(2)}) collective-permute-start(f32[1,256]{1,0:T(1,128)S(1)} %add.201), channel_id=1, source_target_pairs={{0,128},{4,132},{8,136},{12,140},{16,144},{20,148},{24,152},{28,15... | collective-permute-start | bytes 3080 | tf_op jit(solution)/shard_map/ppermute | solution.py:279
  76.1 13.1 %copy-start.6 = (f32[512,1024]{1,0:T(8,128)}, f32[512,1024]{1,0:T(8,128)S(1)}, u32[]{:S(2)}) copy-start(f32[512,1024]{1,0:T(8,128)S(1)} %get-tuple-element.115) | copy-start | bytes 6291460
  77.6 8.2 %collective-permute-start.16 = (bf16[256,1024]{1,0:T(8,128)(2,1)S(1)}, bf16[256,1024]{1,0:T(8,128)(2,1)S(1)}, u32[]{:S(2)}, u32[]{:S(2)}) collective-permute-start(bf16[256,1024]{1,0:T(8,128)(2,1)S(1)} %get-tuple-element.132), channel_id=1, source_target_pairs={{0,1},{1,0},{2,3},{3,2},{4,5},{5,4},{6,7},{7,6},{8,9},{9,8},{10,11... | collective-permute-start | bytes 1572872 | tf_op jit(solution)/shard_map/ppermute | solution.py:282
  77.6 14.3 %collective-permute-start.21 = (bf16[256,1024]{1,0:T(8,128)(2,1)S(1)}, bf16[256,1024]{1,0:T(8,128)(2,1)S(1)}, u32[]{:S(2)}, u32[]{:S(2)}) collective-permute-start(bf16[256,1024]{1,0:T(8,128)(2,1)S(1)} %get-tuple-element.118), channel_id=1, source_target_pairs={{0,4},{4,0},{8,12},{12,8},{16,20},{20,16},{24,28},{28,24},{32,36},... | collective-permute-start | bytes 1572872 | tf_op jit(solution)/shard_map/ppermute | solution.py:279
  77.6 8.2 %collective-permute-start.15 = (f32[1,256]{1,0:T(1,128)S(1)}, f32[1,256]{1,0:T(1,128)S(1)}, u32[]{:S(2)}, u32[]{:S(2)}) collective-permute-start(f32[1,256]{1,0:T(1,128)S(1)} %add.202), channel_id=1, source_target_pairs={{16,0},{20,4},{24,8},{28,12},{32,16},{36,20},{40,24},{44,28},{48,3... | collective-permute-start | bytes 3080 | tf_op jit(solution)/shard_map/ppermute | solution.py:279
  79.4 31.1 %collective-permute-start.18 = (bf16[256,1024]{1,0:T(8,128)(2,1)}, bf16[256,1024]{1,0:T(8,128)(2,1)}, u32[]{:S(2)}, u32[]{:S(2)}) collective-permute-start(bf16[256,1024]{1,0:T(8,128)(2,1)} %get-tuple-element.114), channel_id=1, source_target_pairs={{240,0},{248,8},{0,16},{8,24},{16,32},{24,40},{32,48},{40,56},{48,... | collective-permute-start | bytes 1572872 | tf_op jit(solution)/shard_map/ppermute | solution.py:279
  85.8 7.1 %copy-start.8 = (f32[256,1024]{1,0:T(8,128)}, f32[256,1024]{1,0:T(8,128)S(1)}, u32[]{:S(2)}) copy-start(f32[256,1024]{1,0:T(8,128)S(1)} %get-tuple-element.107) | copy-start | bytes 3145732
  85.8 4.5 %collective-permute-start.22 = (f32[1,256]{1,0:T(1,128)S(1)}, f32[1,256]{1,0:T(1,128)S(1)}, u32[]{:S(2)}, u32[]{:S(2)}) collective-permute-start(f32[1,256]{1,0:T(1,128)S(1)} %add.208), channel_id=1, source_target_pairs={{32,0},{36,4},{40,8},{44,12},{48,16},{52,20},{56,24},{60,28},{64,3... | collective-permute-start | bytes 3080 | tf_op jit(solution)/shard_map/ppermute | solution.py:279
  88.6 22.0 %collective-permute-start.17 = (bf16[256,1024]{1,0:T(8,128)(2,1)}, bf16[256,1024]{1,0:T(8,128)(2,1)}, u32[]{:S(2)}, u32[]{:S(2)}) collective-permute-start(bf16[256,1024]{1,0:T(8,128)(2,1)} %get-tuple-element.113), channel_id=1, source_target_pairs={{252,0},{248,4},{4,8},{0,12},{12,16},{8,20},{20,24},{16,28},{28,32... | collective-permute-start | bytes 1572872 | tf_op jit(solution)/shard_map/ppermute | solution.py:279
  92.9 29.6 %copy-start.7 = (f32[512,1024]{1,0:T(8,128)S(1)}, f32[512,1024]{1,0:T(8,128)}, u32[]{:S(2)}) copy-start(f32[512,1024]{1,0:T(8,128)} %copy-done.6) | copy-start | bytes 6291460
  92.9 14.8 %collective-permute-start.24 = (f32[1,256]{1,0:T(1,128)S(1)}, f32[1,256]{1,0:T(1,128)S(1)}, u32[]{:S(2)}, u32[]{:S(2)}) collective-permute-start(f32[1,256]{1,0:T(1,128)S(1)} %add.209), channel_id=1, source_target_pairs={{64,0},{68,4},{72,8},{76,12},{80,16},{84,20},{88,24},{92,28},{96,3... | collective-permute-start | bytes 3080 | tf_op jit(solution)/shard_map/ppermute | solution.py:279
  95.6 17.7 %collective-permute-start.20 = (bf16[256,1024]{1,0:T(8,128)(2,1)}, bf16[256,1024]{1,0:T(8,128)(2,1)S(1)}, u32[]{:S(2)}, u32[]{:S(2)}) collective-permute-start(bf16[256,1024]{1,0:T(8,128)(2,1)} %get-tuple-element.116), channel_id=1, source_target_pairs={{0,4},{4,0},{8,12},{12,8},{16,20},{20,16},{24,28},{28,24},{32,36},... | collective-permute-start | bytes 1572872 | tf_op jit(solution)/shard_map/ppermute | solution.py:279
  95.8 17.4 %collective-permute-start.19 = (bf16[256,1024]{1,0:T(8,128)(2,1)}, bf16[256,1024]{1,0:T(8,128)(2,1)S(1)}, u32[]{:S(2)}, u32[]{:S(2)}) collective-permute-start(bf16[256,1024]{1,0:T(8,128)(2,1)} %get-tuple-element.131), channel_id=1, source_target_pairs={{0,1},{1,0},{2,3},{3,2},{4,5},{5,4},{6,7},{7,6},{8,9},{9,8},{10,11... | collective-permute-start | bytes 1572872 | tf_op jit(solution)/shard_map/ppermute | solution.py:282
  107.7 14.8 %collective-permute-start.23 = (bf16[256,1024]{1,0:T(8,128)(2,1)}, bf16[256,1024]{1,0:T(8,128)(2,1)}, u32[]{:S(2)}, u32[]{:S(2)}) collective-permute-start(bf16[256,1024]{1,0:T(8,128)(2,1)} %add_convert_fusion), channel_id=1, source_target_pairs={{0,2},{1,3},{2,0},{3,1},{4,6},{5,7},{6,4},{7,5},{8,10},{9,11},{10,... | collective-permute-start | bytes 1572872 | tf_op jit(solution)/shard_map/ppermute | solution.py:282
  (9 other events, 13.1 us)

commit v3 on v2

--- a/solution.py
+++ b/solution.py
@@ -92,10 +92,6 @@
 
 def halves(ref, rows):
     return [ref.at[k * rows:(k + 1) * rows, :] for k in range(2)]
-
-
-def slice_kernel(order, t, half):
-    half[...] = t[...]
 
 
 def own_image_kernel(order, scale, a_in, t_in, s_out, row_ref, col_ref, diag_ref, a, t, s_ref, sems, out_sems):
@@ -140,26 +136,26 @@
 def first_logits_kernel(even, scale, a_in, y_in, x_in, v_in, s_ref, row_ref, col_ref, yx_ref, v, sems):
     rows = a_in.shape[0]
     y_copy = fetch_y(even, a_in, y_in, yx_ref.at[:rows, :], sems.at[3])
-    copies = fetch([x_in] + halves(v_in, rows), [yx_ref.at[rows:, :], v.at[0], v.at[1]], sems)
+    copies = fetch([x_in] + halves(v_in, rows), [yx_ref.at[rows:, :]] + halves(v, rows), sems)
     mult = scale[0] * LOG2E
     y_copy.wait()
     copies[0].wait()
     for k in range(2):
         copies[1 + k].wait()
         cols = slice(k * rows, (k + 1) * rows)
-        s_ref[:, cols] = mult * lax.dot_general(yx_ref[...], v[k], NT, preferred_element_type=F32)
+        s_ref[:, cols] = mult * lax.dot_general(yx_ref[...], v[cols, :], NT, preferred_element_type=F32)
         col_ref[:, cols] = columns_of(s_ref[:, cols])
     row_ref[...] = rows_of(s_ref, None)
 
 
 def far_logits_kernel(scale, before, yx, v_in, s_ref, row_ref, col_ref, v, sems):
-    rows = v.shape[1]
-    copies = fetch(halves(v_in, rows), [v.at[k] for k in range(2)], sems)
+    rows = v.shape[0] // 2
+    copies = fetch(halves(v_in, rows), halves(v, rows), sems)
     mult = scale[0] * LOG2E
     for k in range(2):
         copies[k].wait()
         cols = slice(k * rows, (k + 1) * rows)
-        s_ref[:, cols] = mult * lax.dot_general(yx[...], v[k], NT, preferred_element_type=F32)
+        s_ref[:, cols] = mult * lax.dot_general(yx[...], v[cols, :], NT, preferred_element_type=F32)
         col_ref[:, cols] = columns_of(s_ref[:, cols])
     row_ref[...] = rows_of(s_ref, spread(before[...]))
 
@@ -211,42 +207,59 @@
             keep_ref[k * rows:(k + 1) * rows, :] = g
 
 
-def y_grads_kernel(scale, wa, wb, va, vb, g_ref, send_ref, v, sems):
-    rows = v.shape[1]
-    copies = fetch(halves(va, rows) + halves(vb, rows), [v.at[k] for k in range(4)], sems)
+def y_grads_kernel(scale, wa, wb, va, vb, g_ref, send_ref):
+    rows = wa.shape[0] // 2
+    g = jnp.dot(wa[:rows, :], va[...], preferred_element_type=F32)
+    g = scale[0] * (g + jnp.dot(wb[:rows, :], vb[...], preferred_element_type=F32))
+    g_ref[...] = g
+    send_ref[...] = g.astype(BF16)
+
+
+def image_kernel(order, even, scale, w, t_in, wa, wb, va, vb, gy, gi_ref, gx_ref, t, sems):
+    rows = t.shape[1]
+    copies = fetch([quarter(order, t_in, k, rows) for k in range(4)], [t.at[k] for k in range(4)], sems)
     step = 512
-    for o in range(0, g_ref.shape[1], step):
+    for o in range(0, gi_ref.shape[1], step):
         cols = slice(o, o + step)
-        g = 0.0
+        gx = jnp.dot(wa[rows:, :], va[:, cols], preferred_element_type=F32)
+        gx = gx + jnp.dot(wb[rows:, :], vb[:, cols], preferred_element_type=F32)
+        gi = 0.0
         for k in range(4):
             if o == 0:
                 copies[k].wait()
-            w = (wa, wb)[k // 2][:rows, (k % 2) * rows:(k % 2 + 1) * rows]
-            g = g + jnp.dot(w, v[k, :, cols], preferred_element_type=F32)
-        g_ref[:, cols] = scale[0] * g
-        send_ref[:, cols] = (scale[0] * g).astype(BF16)
-
-
-def image_kernel(order, even, scale, w, t_in, wa, wb, va, vb, gy, gi_ref, gx_ref, t, v, sems):
-    rows = t.shape[1]
-    sources = [quarter(order, t_in, k, rows) for k in range(4)] + halves(va, rows) + halves(vb, rows)
-    copies = fetch(sources, [t.at[k] for k in range(4)] + [v.at[k] for k in range(4)], sems)
-    step = 512
-    for o in range(0, gi_ref.shape[1], step):
-        cols = slice(o, o + step)
-        gi = gx = 0.0
-        for k in range(4):
-            if o == 0:
-                copies[k].wait()
-                copies[4 + k].wait()
             tk = t[k, :, cols]
             wk = w[:, k * rows:(k + 1) * rows]
             gx = gx + jnp.dot(wk[rows:], tk, preferred_element_type=F32)
             gi = gi + jnp.dot(wk[:rows], tk, preferred_element_type=F32)
-            far = (wa, wb)[k // 2][rows:, (k % 2) * rows:(k % 2 + 1) * rows]
-            gx = gx + jnp.dot(far, v[k, :, cols], preferred_element_type=F32)
         gi_ref[:, cols] = scale[0] * gi + jnp.where(even[0] == 1, 0.0, gy[:, cols])
         gx_ref[:, cols] = (scale[0] * gx).astype(BF16)
+
+
+def finish_kernel(keep, got_zero, home_0, across, g_i, x_got, y_got, loss_in, scale_in, text_out, image_out, loss_ref,
+                  b0, b1, b2, b3, b4, out, sems, out_sems):
+    rows, d = b0.shape
+    span = d // 2
+    parts = [slice(0, span), slice(span, d)]
+    texts = [fetch([r.at[:, c] for r in (got_zero, home_0, across)], [b.at[:, c] for b in (b0, b1, b2)], sems.at[i])
+             for i, c in enumerate(parts)]
+    images = [fetch([r.at[:, c] for r in (x_got, y_got)], [b.at[:, c] for b in (b3, b4)], sems.at[2 + i])
+              for i, c in enumerate(parts)]
+    loss_ref[...] = jnp.sum(loss_in[...], axis=1, keepdims=True) * scale_in[0]
+    stores = []
+    for i, c in enumerate(parts):
+        for copy in images[i]:
+            copy.wait()
+        out[0, :, c] = g_i[:, c] + b3[:, c].astype(F32) + b4[:, c].astype(F32)
+        stores.append(pltpu.make_async_copy(out.at[0, :, c], image_out.at[:, c], out_sems.at[2 * i]))
+        stores[-1].start()
+        for copy in texts[i]:
+            copy.wait()
+        total = keep[:rows, c] + b0[:, c].astype(F32) + b1[:, c].astype(F32) + b2[:, c].astype(F32)
+        out[1, :, c] = total
+        stores.append(pltpu.make_async_copy(out.at[1, :, c], text_out.at[:, c], out_sems.at[2 * i + 1]))
+        stores[-1].start()
+    for store in stores:
+        store.wait()
 
 
 def lse2(*parts):
@@ -286,22 +299,13 @@
 
     image_buf = pltpu.VMEM((rows, d), BF16)
 
-    half = pl.pallas_call(
-        slice_kernel,
-        grid_spec=pltpu.PrefetchScalarGridSpec(
-            num_scalar_prefetch=1, grid=(2,),
-            in_specs=[pl.BlockSpec((rows, d), lambda k, o: (o[k], 0))],
-            out_specs=pl.BlockSpec((rows, d), lambda k, o: (k, 0))),
-        out_shape=jax.ShapeDtypeStruct((2 * rows, d), BF16),
-        name="quarters",
-    )(order, text_emb)
+    half = jnp.concatenate([lax.dynamic_slice_in_dim(text_emb, (rep ^ m) * rows, rows, 0) for m in ORDER[:2]])
     half, images = tie(half, image_emb)
     va = hop(half, v_route)
     x = hop(images, x_route)
     y = hop(images, y_route)
     wide, narrow = (1, 4 * rows), (1, rows)
     text_buf = pltpu.VMEM((4, rows, d), BF16)
-    half_buf = pltpu.VMEM((2, rows, d), BF16)
     logits_buf = pltpu.VMEM((rows, 4 * rows), F32)
 
     logits_i, r_i, col_i, diag = local_call(
@@ -318,15 +322,15 @@
     h_y = hop(r_i, y_route)
     va, y, r_xt, logits_x, h_y = tie(va, y, r_xt, logits_x, h_y)
     vb = swap(va, 1)
-    s_a, row_a, col_a, yx = local_call(
+    s_a, row_a, col_a, yx, near_a = local_call(
         first_logits_kernel, "first_logits", [SMEM] * 2 + [HBM] * 4,
+        [((2 * rows, 2 * rows), F32), ((1, 2 * rows), F32), ((1, 2 * rows), F32)] + [((2 * rows, d), BF16)] * 2, 4 * tile,
+        [sems(4)],
+    )(evens, logit_scale, image_emb, y, x, va)
+    s_b, row_v, col_b, near_b = local_call(
+        far_logits_kernel, "far_logits", [SMEM, VMEM, VMEM, HBM],
         [((2 * rows, 2 * rows), F32), ((1, 2 * rows), F32), ((1, 2 * rows), F32), ((2 * rows, d), BF16)], 4 * tile,
-        [half_buf, sems(4)],
-    )(evens, logit_scale, image_emb, y, x, va)
-    s_b, row_v, col_b = local_call(
-        far_logits_kernel, "far_logits", [SMEM, VMEM, VMEM, HBM],
-        [((2 * rows, 2 * rows), F32), ((1, 2 * rows), F32), ((1, 2 * rows), F32)], 4 * tile,
-        [half_buf, sems(2)],
+        [sems(2)],
     )(logit_scale, row_a, yx, vb)
 
     r_y, r_xv = row_v[:, :rows], row_v[:, rows:]
@@ -367,61 +371,60 @@
             [((2 * rows, 2 * rows), BF16), ((2 * rows, d), dtype)], 4 * tile,
         )(logit_scale, row_yx, cols, s, yx)
 
-    def cross(value, mask):
-        return hop(value, [(i, i ^ mask) for i in range(blocks)])
-
-    def ring(value, distance):
+    def shifted(value, xor, distance):
         span = blocks // 2
-        return hop(value, [((i + 4 * distance) % span + i // span * span, i) for i in range(blocks)])
-
-    w_b, send_v = far_text(s_b, c_v[:, 2 * rows:], CORE_V)
-    send_v, s_a = tie(send_v, s_a)
-    got_v = swap(send_v, 1)
-    got = cross(loss_part, 2)
-    w_a, keep_v = far_text(s_a, c_v[:, :2 * rows], F32)
-    keep_v, got_v, got = tie(keep_v, got_v, got)
-    loss_part = loss_part + got
-    v_one = (keep_v[rows:] + got_v[rows:].astype(F32)).astype(BF16)
-    v_zero = (keep_v[:rows] + got_v[:rows].astype(F32)).astype(BF16)
-    v_one, v_zero, logits_x, loss_part, w_a = tie(v_one, v_zero, logits_x, loss_part, w_a)
-    home_1 = hop(v_one, v_route)
-    home_0 = hop(v_zero, v_route)
-    g_y, g_y_send = local_call(
-        y_grads_kernel, "y_grads", [SMEM] + [VMEM] * 2 + [HBM] * 2,
-        [((rows, d), F32), ((rows, d), BF16)], 4 * tile, [text_buf, sems(4)],
-    )(logit_scale, w_a, w_b, va, vb)
-    y_got = hop(g_y_send, y_back)
-    logits_x, g_y, loss_part = tie(logits_x, g_y, loss_part)
-    got = cross(loss_part, blocks // 2)
+
+        def source(i):
+            i = i ^ xor
+            return (i + 4 * distance) % span + i // span * span
+        return hop(value, [(source(i), i) for i in range(blocks)])
+
     w_t, send_t, keep_t = local_call(
         own_text_kernel, "own_text", [SMEM] + [VMEM] * 2 + [HBM] * 3 + [VMEM],
         [((2 * rows, 4 * rows), BF16), ((2 * rows, d), CORE), ((2 * rows, d), F32)], 8 * tile,
         [pltpu.VMEM((2 * rows, 4 * rows), F32), image_buf, sems(9)],
     )(logit_scale, row_ix, c_t, logits_i, logits_x, image_emb, yx)
-    send_t, got = tie(send_t, got)
+    got_t = swap(send_t, 1)
+    send_t, s_b = tie(send_t, s_b)
+    w_b, send_v = far_text(s_b, c_v[:, 2 * rows:], CORE_V)
+    send_v, s_a = tie(send_v, s_a)
+    got_v = swap(send_v, 1)
+    got = shifted(loss_part, 2, 0)
+    w_a, keep_v = far_text(s_a, c_v[:, :2 * rows], F32)
+    keep_v, got_v, got, got_t = tie(keep_v, got_v, got, got_t)
     loss_part = loss_part + got
-    got_one = swap(send_t[rows:], 1)
-    got_zero = swap(send_t[:rows], 1)
-    got = ring(loss_part, 1)
+    v_one = (keep_v[rows:] + got_v[rows:].astype(F32)).astype(BF16)
+    v_zero = (keep_v[:rows] + got_v[:rows].astype(F32)).astype(BF16)
+    v_one, v_zero, loss_part, w_a = tie(v_one, v_zero, loss_part, w_a)
+    home_1 = hop(v_one, v_route)
+    home_0 = hop(v_zero, v_route)
+    g_y, g_y_send = local_call(
+        y_grads_kernel, "y_grads", [SMEM] + [VMEM] * 4, [((rows, d), F32), ((rows, d), BF16)], 4 * tile,
+    )(logit_scale, w_a, w_b, near_a, near_b)
+    y_got = hop(g_y_send, y_back)
     g_i, g_x = local_call(
-        image_kernel, "image_grads", [SMEM] * 3 + [VMEM, HBM, VMEM, VMEM, HBM, HBM, VMEM],
-        [((rows, d), F32), ((rows, d), BF16)], 16 * tile, [text_buf, text_buf, sems(8)],
-    )(order, evens, logit_scale, w_t, text_emb, w_a, w_b, va, vb, g_y)
-    g_x, got, got_one = tie(g_x, got, got_one)
-    loss_part = loss_part + got
+        image_kernel, "image_grads", [SMEM] * 3 + [VMEM, HBM] + [VMEM] * 5,
+        [((rows, d), F32), ((rows, d), BF16)], 16 * tile, [text_buf, sems(4)],
+    )(order, evens, logit_scale, w_t, text_emb, w_a, w_b, near_a, near_b, g_y)
+    g_x, loss_part = tie(g_x, loss_part)
+    got = [shifted(loss_part, x, z) for x, z in ((blocks // 2, 0), (0, 4), (blocks // 2, 4))]
+    got_zero = got_t[:rows]
+    part = keep_t[rows:] + got_t[rows:].astype(F32)
+    part, home_1, g_i, y_got, *got = tie(part, home_1, g_i, y_got, *got)
+    loss_part = sum(got, loss_part)
+    one = (part + home_1.astype(F32)).astype(BF16)
+    one, loss_part, g_x = tie(one, loss_part, g_x)
+    across = swap(one, 2)
     x_got = hop(g_x, x_back)
-    loss_part = loss_part + ring(loss_part, 2)
-    part = keep_t[rows:] + got_one.astype(F32)
-    part, home_1, loss_part = tie(part, home_1, loss_part)
-    one = (part + home_1.astype(F32)).astype(BF16)
-    one, loss_part = tie(one, loss_part)
-    across = swap(one, 2)
-    loss_part = loss_part + ring(loss_part, 4)
-    loss = jnp.sum(loss_part, axis=1) / (2.0 * rows * blocks * 4)
-    base = keep_t[:rows] + got_zero.astype(F32)
-    grad_text = base + home_0.astype(F32) + across.astype(F32)
-    grad_image = g_i + x_got.astype(F32) + jnp.where(even, y_got, jnp.zeros_like(y_got)).astype(F32)
-    return grad_image, grad_text, loss
+    got = [shifted(loss_part, 0, z) for z in (1, 2, 3)]
+    across, home_0, x_got, *got = tie(across, home_0, x_got, *got)
+    grad_text, grad_image, loss = local_call(
+        finish_kernel, "finish", [VMEM, ANY, ANY, ANY, VMEM, ANY, ANY, VMEM, SMEM],
+        [((rows, d), F32), ((rows, d), F32), ((1, 1), F32)], tile,
+        [image_buf] * 5 + [pltpu.VMEM((2, rows, d), F32), pltpu.SemaphoreType.DMA((4, 3)), sems(4)], [ANY, ANY, VMEM],
+    )(keep_t, got_zero, home_0, across, g_i, x_got, y_got, sum(got, loss_part),
+      jnp.full((1,), 1.0 / (2.0 * rows * blocks * 4), F32))
+    return grad_image, grad_text, loss.reshape(1)
 
 
 def solution(mesh):

time: 126 us -> 116 us (0.921)
  starting transfers between devices: 42.7 us -> 52.8 us
  other arithmetic: 8.72 us -> 2.23 us
  local copies, waits for them, and re-layouts: 7.88 us -> 2.48 us
  waiting for transfers between devices: 36.7 us -> 33.2 us
  Pallas kernels: 26.5 us -> 23.7 us
  between operations: 3.44 us -> 1.84 us
    ppermute x17 -> x19, starting transfers between devices: 37.4 us -> 47.4 us  [hop(): return lax.ppermute(value, 'blk', route)]
    unnamed x33 -> x13, local copies, waits for them, and re-layouts: 6.98 us -> 1 us
    add x4 -> x3, other arithmetic: 5.18 us -> 0.16 us  [the longest x1 0.15 us: per_device(): part = keep_t[rows:] + got_t[rows:].astype(F32)]
    ppermute x17 -> x19, waiting for transfers between devices: 23.3 us -> 19.2 us  [hop(): return lax.ppermute(value, 'blk', route)]
    pallas_call x3, Pallas kernels: 9.76 us -> 5.8 us  [the longest x1 2.77 us: per_device(): local_call(image_kernel, 'image_grads', [SMEM] * 3 + [VMEM, HBM] + [VMEM]...]
    dynamic_slice x0 -> x1, local copies, waits for them, and re-layouts: none -> 1.42 us  [per_device(): lax.dynamic_slice_in_dim(text_emb, (rep ^ m) * rows, rows, 0)]
    ppermute x8 -> x7, waiting for transfers between devices: 13.3 us -> 14 us  [swap(): return lax.ppermute(value, 'rep', [(i, i ^ mask) for i in range(4)])]
    ppermute x8 -> x7, starting transfers between devices: 5.24 us -> 5.35 us  [swap(): return lax.ppermute(value, 'rep', [(i, i ^ mask) for i in range(4)])]
  transfers between devices with their start and end apart: 25 -> 26, of which waited for: 10 -> 11; matrix products, arithmetic and copies ran while one was open for 4% -> 0% of each run, Pallas kernels for 13% -> 13%
where the time goes in v3:
time: 116 us
  starting transfers between devices  52.8 us (46%)
  waiting for transfers between devices  33.2 us (29%)
  Pallas kernels  23.7 us (20%)
  local copies, waits for them, and re-layouts  2.48 us (2%)
  other arithmetic  2.23 us (2%)
  between operations  1.84 us (2%)
    ppermute x19, starting transfers between devices, hop(): return lax.ppermute(value, 'blk', route)  47.4 us
    ppermute x19, waiting for transfers between devices, hop(): return lax.ppermute(value, 'blk', route)  19.2 us
    ppermute x7, waiting for transfers between devices, swap(): return lax.ppermute(value, 'rep', [(i, i ^ mask) for i in range(4)])  14 us
    ppermute x7, starting transfers between devices, swap(): return lax.ppermute(value, 'rep', [(i, i ^ mask) for i in range(4)])  5.35 us
    pallas_call x1, Pallas kernels, per_device(): local_call(own_image_kernel, 'own_image', [SMEM] * 2 + [HBM] * 2, [((rows...  3.4 us
    pallas_call x1, Pallas kernels, per_device(): local_call(x_logits_kernel, 'x_logits', [SMEM] * 2 + [HBM] * 2, [((rows,...  3.4 us
    pallas_call x1, Pallas kernels, per_device(): local_call(first_logits_kernel, 'first_logits', [SMEM] * 2 + [HBM] * 4, [...  3.33 us
    pallas_call x1, Pallas kernels, per_device(): local_call(far_logits_kernel, 'far_logits', [SMEM, VMEM, VMEM, HBM], [((2...  3.03 us
  transfers between devices with their start and end apart: 26, of which 11 were waited for; matrix products, arithmetic and copies ran while one was open for 0% of the time, Pallas kernels for 13%

profile of v3, /device:TPU:16, one launch (start us, length us, event | category | flops | bytes accessed | tf_op | source)
XLA Modules:
  0.0 116.2 jit_solution(11703583537219617305)
XLA Ops:
  0.7 1.4 %constant_dynamic-slice_fusion.1 = (bf16[256,1024]{1,0:T(8,128)(2,1)S(1)}, bf16[256,1024]{1,0:T(8,128)(2,1)S(1)}) fusion(bf16[1024,1024]{1,0:T(8,128)(2,1)} %t_in.5, s32[]{:T(128)S(6)} %select_n.35, s32[]{:T(128)S(6)} %select_n.36), kind=kLoop, calls=%fused_computation.57 | loop fusion | bytes 2097160 | tf_op jit(solution)/shard_map/dynamic_slice | solution.py:302
  4.4 1.4 %collective-permute-start.2 = (bf16[256,1024]{1,0:T(8,128)(2,1)S(1)}, bf16[256,1024]{1,0:T(8,128)(2,1)S(1)}, u32[]{:S(2)}, u32[]{:S(2)}) collective-permute-start(bf16[256,1024]{1,0:T(8,128)(2,1)S(1)} %copy-done.1), channel_id=1, source_target_pairs={{0,252},{4,248},{8,4},{12,0},{16,12},{20,8},{24,20},{28,16},{32,28... | collective-permute-start | bytes 1572872 | tf_op jit(solution)/shard_map/ppermute | solution.py:292
  5.8 7.3 %collective-permute-start.1 = (bf16[256,1024]{1,0:T(8,128)(2,1)S(1)}, bf16[256,1024]{1,0:T(8,128)(2,1)}, u32[]{:S(2)}, u32[]{:S(2)}) collective-permute-start(bf16[256,1024]{1,0:T(8,128)(2,1)S(1)} %copy-done.1), channel_id=1, source_target_pairs={{0,240},{8,248},{16,0},{24,8},{32,16},{40,24},{48,32},{56,40},{64,... | collective-permute-start | bytes 1572872 | tf_op jit(solution)/shard_map/ppermute | solution.py:292
  13.9 3.4 %own_image.1 = (f32[256,1024]{1,0:T(8,128)S(1)}, f32[1,256]{1,0:T(1,128)S(1)}, f32[1,1024]{1,0:T(1,128)S(1)}, f32[1,256]{1,0:T(1,128)S(1)}) custom-call(s32[4]{0:T(128)S(1)} %pad_add_fusion.order, f32[1]{0:T(128)S(6)} %copy.7.scale, bf16[256,1024]{1,0:T(8,128)(2,1)S(1)} %copy-done.1, bf16[1024,1024]{1,0:T(8,128)(2,1)S(1)} %copy-done), custom_call_target="tpu_custom_call" | custom-call | flops 1 | bytes 1 | tf_op jit(solution)/shard_map/own_image/pallas_call | solution.py:311
  17.3 2.9 %collective-permute-start.3 = (f32[1,256]{1,0:T(1,128)S(1)}, f32[1,256]{1,0:T(1,128)S(1)}, u32[]{:S(2)}, u32[]{:S(2)}) collective-permute-start(f32[1,256]{1,0:T(1,128)S(1)} %get-tuple-element.75), channel_id=1, source_target_pairs={{0,240},{8,248},{16,0},{24,8},{32,16},{40,24},{48,32},{56,40},{64,... | collective-permute-start | bytes 3080 | tf_op jit(solution)/shard_map/ppermute | solution.py:292
  20.2 3.4 %x_logits.1 = (f32[256,1024]{1,0:T(8,128)S(1)}, f32[1,256]{1,0:T(1,128)S(1)}, f32[1,1024]{1,0:T(1,128)S(1)}) custom-call(s32[4]{0:T(128)S(1)} %pad_add_fusion.order, f32[1]{0:T(128)S(6)} %copy.7.scale, bf16[256,1024]{1,0:T(8,128)(2,1)S(1)} %collective-permute-done.2.x_in, bf16[1024,1024]{1,0:T(8,128)(2,1)S(1)} %copy-done), custom_call_target="tpu_custom_call" | custom-call | flops 1 | bytes 1 | tf_op jit(solution)/shard_map/x_logits/pallas_call | solution.py:317
  24.6 3.7 %collective-permute-done.v_in = bf16[512,1024]{1,0:T(8,128)(2,1)} collective-permute-done((bf16[512,1024]{1,0:T(8,128)(2,1)}, bf16[512,1024]{1,0:T(8,128)(2,1)}, u32[]{:S(2)}, u32[]{:S(2)}) %collective-permute-start) | collective-permute-done | bytes 1048608 | tf_op jit(solution)/shard_map/ppermute | solution.py:292
  28.4 3.3 %first_logits.1 = (f32[512,512]{1,0:T(8,128)S(1)}, f32[1,512]{1,0:T(1,128)S(1)}, f32[1,512]{1,0:T(1,128)S(1)}, bf16[512,1024]{1,0:T(8,128)(2,1)S(1)}, bf16[512,1024]{1,0:T(8,128)(2,1)S(1)}) custom-call(s32[1]{0:T(128)} %bitcast.4.even, f32[1]{0:T(128)S(6)} %copy.7.scale, bf16[256,1024]{1,0:T(8,128)(2,1)S(1)} %copy-done.1, ...), custom_call_target="tpu_custom_call" | custom-call | flops 1 | bytes 1 | tf_op jit(solution)/shard_map/first_logits/pallas_call | solution.py:325
  31.8 3.0 %far_logits.1 = (f32[512,512]{1,0:T(8,128)S(1)}, f32[1,512]{1,0:T(1,128)S(1)}, f32[1,512]{1,0:T(1,128)S(1)}, bf16[512,1024]{1,0:T(8,128)(2,1)S(1)}) custom-call(f32[1]{0:T(128)S(6)} %copy.7.scale, f32[1,512]{1,0:T(1,128)S(1)} %get-tuple-element.85.before, bf16[512,1024]{1,0:T(8,128)(2,1)S(1)} %get-tuple-element.86.yx, ...), custom_call_target="tpu_custom_call" | custom-call | flops 1 | bytes 1 | tf_op jit(solution)/shard_map/far_logits/pallas_call | solution.py:330
  36.2 4.0 %collective-permute-start.7 = (f32[1,512]{1,0:T(1,128)S(1)}, f32[1,512]{1,0:T(1,128)S(1)}, u32[]{:S(2)}, u32[]{:S(2)}) collective-permute-start(f32[1,512]{1,0:T(1,128)S(1)} %get-tuple-element.176), channel_id=1, source_target_pairs={{252,0},{248,4},{4,8},{0,12},{12,16},{8,20},{20,24},{16,28},{28,32... | collective-permute-start | bytes 6152 | tf_op jit(solution)/shard_map/ppermute | solution.py:292
  40.1 3.0 %collective-permute-start.6 = (f32[1,512]{1,0:T(1,128)S(1)}, f32[1,512]{1,0:T(1,128)S(1)}, u32[]{:S(2)}, u32[]{:S(2)}) collective-permute-start(f32[1,512]{1,0:T(1,128)S(1)} %get-tuple-element.177), channel_id=1, source_target_pairs={{0,252},{4,248},{8,4},{12,0},{16,12},{20,8},{24,20},{28,16},{32,28... | collective-permute-start | bytes 6152 | tf_op jit(solution)/shard_map/ppermute | solution.py:292
  43.1 1.9 %collective-permute-start.8 = (f32[1,256]{1,0:T(1,128)S(1)}, f32[1,256]{1,0:T(1,128)S(1)}, u32[]{:S(2)}, u32[]{:S(2)}) collective-permute-start(f32[1,256]{1,0:T(1,128)S(1)} %get-tuple-element.171), channel_id=1, source_target_pairs={{240,0},{248,8},{0,16},{8,24},{16,32},{24,40},{32,48},{40,56},{48,... | collective-permute-start | bytes 3080 | tf_op jit(solution)/shard_map/ppermute | solution.py:292
  45.0 6.2 %collective-permute-done.8 = f32[1,256]{1,0:T(1,128)S(1)} collective-permute-done((f32[1,256]{1,0:T(1,128)S(1)}, f32[1,256]{1,0:T(1,128)S(1)}, u32[]{:S(2)}, u32[]{:S(2)}) %collective-permute-start.8) | collective-permute-done | bytes 1056 | tf_op jit(solution)/shard_map/ppermute | solution.py:292
  51.4 1.5 %collective-permute-start.11 = (f32[3,1024]{1,0:T(4,128)S(1)}, f32[3,1024]{1,0:T(4,128)S(1)}, u32[]{:S(2)}, u32[]{:S(2)}) collective-permute-start(f32[3,1024]{1,0:T(4,128)S(1)} %select_maximum_fusion), channel_id=1, source_target_pairs={{0,3},{1,2},{2,1},{3,0},{4,7},{5,6},{6,5},{7,4},{8,11},{9,10},{10,... | collective-permute-start | bytes 36872 | tf_op jit(solution)/shard_map/ppermute | solution.py:295
  52.8 1.4 %collective-permute-start.10 = (f32[3,1024]{1,0:T(4,128)S(1)}, f32[3,1024]{1,0:T(4,128)S(1)}, u32[]{:S(2)}, u32[]{:S(2)}) collective-permute-start(f32[3,1024]{1,0:T(4,128)S(1)} %select_maximum_fusion), channel_id=1, source_target_pairs={{0,2},{1,3},{2,0},{3,1},{4,6},{5,7},{6,4},{7,5},{8,10},{9,11},{10,... | collective-permute-start | bytes 36872 | tf_op jit(solution)/shard_map/ppermute | solution.py:295
  54.8 1.3 %collective-permute-done.11 = f32[3,1024]{1,0:T(4,128)S(1)} collective-permute-done((f32[3,1024]{1,0:T(4,128)S(1)}, f32[3,1024]{1,0:T(4,128)S(1)}, u32[]{:S(2)}, u32[]{:S(2)}) %collective-permute-start.11) | collective-permute-done | bytes 12320 | tf_op jit(solution)/shard_map/ppermute | solution.py:295
  56.1 2.0 %collective-permute-done.10 = f32[3,1024]{1,0:T(4,128)S(1)} collective-permute-done((f32[3,1024]{1,0:T(4,128)S(1)}, f32[3,1024]{1,0:T(4,128)S(1)}, u32[]{:S(2)}, u32[]{:S(2)}) %collective-permute-start.10) | collective-permute-done | bytes 12320 | tf_op jit(solution)/shard_map/ppermute | solution.py:295
  58.2 2.7 %own_text.1 = (bf16[512,1024]{1,0:T(8,128)(2,1)S(1)}, bf16[512,1024]{1,0:T(8,128)(2,1)S(1)}, f32[512,1024]{1,0:T(8,128)S(1)}) custom-call(f32[1]{0:T(128)S(6)} %copy.7.scale, f32[1,512]{1,0:T(1,128)S(1)} %get-tuple-element.175.row, f32[1,1024]{1,0:T(1,128)S(1)} %get-tuple-element.168.col, f32[256,1024]{1,0:T(8,128)S(1)} %copy-done.3, ...), custom_call_target="tpu_custom_call" | custom-call | flops 1 | bytes 1 | tf_op jit(solution)/shard_map/own_text/pallas_call | solution.py:382
  62.6 5.1 %collective-permute-start.13 = (f32[1,256]{1,0:T(1,128)S(1)}, f32[1,256]{1,0:T(1,128)S(1)}, u32[]{:S(2)}, u32[]{:S(2)}) collective-permute-start(f32[1,256]{1,0:T(1,128)S(1)} %fusion.3), channel_id=1, source_target_pairs={{8,0},{12,4},{0,8},{4,12},{24,16},{28,20},{16,24},{20,28},{40,32},... | collective-permute-start | bytes 3080 | tf_op jit(solution)/shard_map/ppermute | solution.py:292
  70.5 1.9 %collective-permute-start.16 = (bf16[256,1024]{1,0:T(8,128)(2,1)S(1)}, bf16[256,1024]{1,0:T(8,128)(2,1)S(1)}, u32[]{:S(2)}, u32[]{:S(2)}) collective-permute-start(bf16[256,1024]{1,0:T(8,128)(2,1)S(1)} %get-tuple-element.122), channel_id=1, source_target_pairs={{240,0},{248,8},{0,16},{8,24},{16,32},{24,40},{32,48},{40,56},{48,... | collective-permute-start | bytes 1572872 | tf_op jit(solution)/shard_map/ppermute | solution.py:292
  72.4 2.8 %image_grads.1 = (f32[256,1024]{1,0:T(8,128)S(1)}, bf16[256,1024]{1,0:T(8,128)(2,1)S(1)}) custom-call(s32[4]{0:T(128)S(1)} %pad_add_fusion.order, s32[1]{0:T(128)} %bitcast.4.even, f32[1]{0:T(128)S(6)} %copy.7.scale, bf16[512,1024]{1,0:T(8,128)(2,1)S(1)} %get-tuple-element.115.w, bf16[1024,1024]{1,0:T(8,128)(2,1)S(1)} %copy-done, ...), custom_call_target="tpu_custom_call" | custom-call | flops 1 | bytes 1 | tf_op jit(solution)/shard_map/image_grads/pallas_call | solution.py:405
  75.2 1.6 %collective-permute-start.19 = (f32[1,256]{1,0:T(1,128)S(1)}, f32[1,256]{1,0:T(1,128)S(1)}, u32[]{:S(2)}, u32[]{:S(2)}) collective-permute-start(f32[1,256]{1,0:T(1,128)S(1)} %add.201), channel_id=1, source_target_pairs={{192,0},{196,4},{200,8},{204,12},{208,16},{212,20},{216,24},{220,2... | collective-permute-start | bytes 3080 | tf_op jit(solution)/shard_map/ppermute | solution.py:292
  76.8 4.1 %collective-permute-start.18 = (f32[1,256]{1,0:T(1,128)S(1)}, f32[1,256]{1,0:T(1,128)S(1)}, u32[]{:S(2)}, u32[]{:S(2)}) collective-permute-start(f32[1,256]{1,0:T(1,128)S(1)} %add.201), channel_id=1, source_target_pairs={{64,0},{68,4},{72,8},{76,12},{80,16},{84,20},{88,24},{92,28},{96,3... | collective-permute-start | bytes 3080 | tf_op jit(solution)/shard_map/ppermute | solution.py:292
  80.9 1.8 %collective-permute-start.17 = (f32[1,256]{1,0:T(1,128)S(1)}, f32[1,256]{1,0:T(1,128)S(1)}, u32[]{:S(2)}, u32[]{:S(2)}) collective-permute-start(f32[1,256]{1,0:T(1,128)S(1)} %add.201), channel_id=1, source_target_pairs={{128,0},{132,4},{136,8},{140,12},{144,16},{148,20},{152,24},{156,2... | collective-permute-start | bytes 3080 | tf_op jit(solution)/shard_map/ppermute | solution.py:292
  82.8 3.1 %collective-permute-done.19 = f32[1,256]{1,0:T(1,128)S(1)} collective-permute-done((f32[1,256]{1,0:T(1,128)S(1)}, f32[1,256]{1,0:T(1,128)S(1)}, u32[]{:S(2)}, u32[]{:S(2)}) %collective-permute-start.19) | collective-permute-done | bytes 1056 | tf_op jit(solution)/shard_map/ppermute | solution.py:292
  86.0 2.1 %collective-permute-done.16.y_got = bf16[256,1024]{1,0:T(8,128)(2,1)S(1)} collective-permute-done((bf16[256,1024]{1,0:T(8,128)(2,1)S(1)}, bf16[256,1024]{1,0:T(8,128)(2,1)S(1)}, u32[]{:S(2)}, u32[]{:S(2)}) %collective-permute-start.16) | collective-permute-done | bytes 524320 | tf_op jit(solution)/shard_map/ppermute | solution.py:292
  88.3 1.3 %collective-permute-start.20 = (bf16[256,1024]{1,0:T(8,128)(2,1)S(1)}, bf16[256,1024]{1,0:T(8,128)(2,1)S(1)}, u32[]{:S(2)}, u32[]{:S(2)}) collective-permute-start(bf16[256,1024]{1,0:T(8,128)(2,1)S(1)} %add_convert_fusion), channel_id=1, source_target_pairs={{0,2},{1,3},{2,0},{3,1},{4,6},{5,7},{6,4},{7,5},{8,10},{9,11},{10,... | collective-permute-start | bytes 1572872 | tf_op jit(solution)/shard_map/ppermute | solution.py:295
  89.6 5.0 %collective-permute-start.25 = (f32[1,256]{1,0:T(1,128)S(1)}, f32[1,256]{1,0:T(1,128)S(1)}, u32[]{:S(2)}, u32[]{:S(2)}) collective-permute-start(f32[1,256]{1,0:T(1,128)S(1)} %add_add_fusion.1), channel_id=1, source_target_pairs={{48,0},{52,4},{56,8},{60,12},{64,16},{68,20},{72,24},{76,28},{80,3... | collective-permute-start | bytes 3080 | tf_op jit(solution)/shard_map/ppermute | solution.py:292
  94.6 4.8 %collective-permute-start.24 = (f32[1,256]{1,0:T(1,128)S(1)}, f32[1,256]{1,0:T(1,128)S(1)}, u32[]{:S(2)}, u32[]{:S(2)}) collective-permute-start(f32[1,256]{1,0:T(1,128)S(1)} %add_add_fusion.1), channel_id=1, source_target_pairs={{32,0},{36,4},{40,8},{44,12},{48,16},{52,20},{56,24},{60,28},{64,3... | collective-permute-start | bytes 3080 | tf_op jit(solution)/shard_map/ppermute | solution.py:292
  100.7 2.3 %collective-permute-done.23 = f32[1,256]{1,0:T(1,128)S(1)} collective-permute-done((f32[1,256]{1,0:T(1,128)S(1)}, f32[1,256]{1,0:T(1,128)S(1)}, u32[]{:S(2)}, u32[]{:S(2)}) %collective-permute-start.23) | collective-permute-done | bytes 1056 | tf_op jit(solution)/shard_map/ppermute | solution.py:292
  103.0 10.7 %collective-permute-done.20.across = bf16[256,1024]{1,0:T(8,128)(2,1)S(1)} collective-permute-done((bf16[256,1024]{1,0:T(8,128)(2,1)S(1)}, bf16[256,1024]{1,0:T(8,128)(2,1)S(1)}, u32[]{:S(2)}, u32[]{:S(2)}) %collective-permute-start.20) | collective-permute-done | bytes 524320 | tf_op jit(solution)/shard_map/ppermute | solution.py:295
  113.7 2.3 %finish.1 = (f32[256,1024]{1,0:T(8,128)}, f32[256,1024]{1,0:T(8,128)}, f32[1,1]{1,0:T(1,128)}) custom-call(f32[512,1024]{1,0:T(8,128)S(1)} %get-tuple-element.99.keep, bf16[256,1024]{1,0:T(8,128)(2,1)S(1)} %slice.147.got_zero, bf16[256,1024]{1,0:T(8,128)(2,1)S(1)} %collective-permute-done.21.home_0, bf16[256,1024]{1,0:T(8,128)(2,1)S(1)} %collective-permute-done.20.across, ...), custom_call_target="tpu_custom_call" | custom-call | flops 1 | bytes 1 | tf_op jit(solution)/shard_map/finish/pallas_call | solution.py:421
  (69 shorter events, 11.7 us)
Async XLA Ops:
  0.6 3.8 %copy-start.1 = (bf16[256,1024]{1,0:T(8,128)(2,1)S(1)}, bf16[256,1024]{1,0:T(8,128)(2,1)}, u32[]{:S(2)}) copy-start(bf16[256,1024]{1,0:T(8,128)(2,1)} %a_in.5) | copy-start | bytes 1572868
  0.7 13.2 %copy-start = (bf16[1024,1024]{1,0:T(8,128)(2,1)S(1)}, bf16[1024,1024]{1,0:T(8,128)(2,1)}, u32[]{:S(2)}) copy-start(bf16[1024,1024]{1,0:T(8,128)(2,1)} %t_in.5) | copy-start | bytes 6291460
  3.1 25.2 %collective-permute-start = (bf16[512,1024]{1,0:T(8,128)(2,1)}, bf16[512,1024]{1,0:T(8,128)(2,1)}, u32[]{:S(2)}, u32[]{:S(2)}) collective-permute-start(bf16[512,1024]{1,0:T(8,128)(2,1)} %pad_maximum_fusion), channel_id=1, source_target_pairs={{0,4},{4,0},{8,12},{12,8},{16,20},{20,16},{24,28},{28,24},{32,36},... | collective-permute-start | bytes 3145736 | tf_op jit(solution)/shard_map/ppermute | solution.py:292
  4.4 15.8 %collective-permute-start.2 = (bf16[256,1024]{1,0:T(8,128)(2,1)S(1)}, bf16[256,1024]{1,0:T(8,128)(2,1)S(1)}, u32[]{:S(2)}, u32[]{:S(2)}) collective-permute-start(bf16[256,1024]{1,0:T(8,128)(2,1)S(1)} %copy-done.1), channel_id=1, source_target_pairs={{0,252},{4,248},{8,4},{12,0},{16,12},{20,8},{24,20},{28,16},{32,28... | collective-permute-start | bytes 1572872 | tf_op jit(solution)/shard_map/ppermute | solution.py:292
  5.8 18.8 %collective-permute-start.1 = (bf16[256,1024]{1,0:T(8,128)(2,1)S(1)}, bf16[256,1024]{1,0:T(8,128)(2,1)}, u32[]{:S(2)}, u32[]{:S(2)}) collective-permute-start(bf16[256,1024]{1,0:T(8,128)(2,1)S(1)} %copy-done.1), channel_id=1, source_target_pairs={{0,240},{8,248},{16,0},{24,8},{32,16},{40,24},{48,32},{56,40},{64,... | collective-permute-start | bytes 1572872 | tf_op jit(solution)/shard_map/ppermute | solution.py:292
  17.3 7.3 %copy-start.2 = (f32[256,1024]{1,0:T(8,128)}, f32[256,1024]{1,0:T(8,128)S(1)}, u32[]{:S(2)}) copy-start(f32[256,1024]{1,0:T(8,128)S(1)} %get-tuple-element.97.si_in) | copy-start | bytes 3145732
  17.3 7.3 %collective-permute-start.3 = (f32[1,256]{1,0:T(1,128)S(1)}, f32[1,256]{1,0:T(1,128)S(1)}, u32[]{:S(2)}, u32[]{:S(2)}) collective-permute-start(f32[1,256]{1,0:T(1,128)S(1)} %get-tuple-element.75), channel_id=1, source_target_pairs={{0,240},{8,248},{16,0},{24,8},{32,16},{40,24},{48,32},{56,40},{64,... | collective-permute-start | bytes 3080 | tf_op jit(solution)/shard_map/ppermute | solution.py:292
  23.6 1.0 copy-start.4
  28.3 3.4 %collective-permute-start.4 = (bf16[512,1024]{1,0:T(8,128)(2,1)}, bf16[512,1024]{1,0:T(8,128)(2,1)}, u32[]{:S(2)}, u32[]{:S(2)}) collective-permute-start(bf16[512,1024]{1,0:T(8,128)(2,1)} %collective-permute-done.v_in), channel_id=1, source_target_pairs={{0,1},{1,0},{2,3},{3,2},{4,5},{5,4},{6,7},{7,6},{8,9},{9,8},{10,11... | collective-permute-start | bytes 3145736 | tf_op jit(solution)/shard_map/ppermute | solution.py:295
  28.4 29.8 %copy-start.3 = (f32[256,1024]{1,0:T(8,128)S(1)}, f32[256,1024]{1,0:T(8,128)}, u32[]{:S(2)}) copy-start(f32[256,1024]{1,0:T(8,128)} %copy-done.2) | copy-start | bytes 3145732
  28.4 29.8 %copy-start.5 = (f32[256,1024]{1,0:T(8,128)S(1)}, f32[256,1024]{1,0:T(8,128)}, u32[]{:S(2)}) copy-start(f32[256,1024]{1,0:T(8,128)} %copy-done.4) | copy-start | bytes 3145732
  34.8 16.4 %collective-permute-start.5 = (f32[3,1024]{1,0:T(4,128)S(1)}, f32[3,1024]{1,0:T(4,128)S(1)}, u32[]{:S(2)}, u32[]{:S(2)}) collective-permute-start(f32[3,1024]{1,0:T(4,128)S(1)} %select_maximum_fusion.1), channel_id=1, source_target_pairs={{0,4},{4,0},{8,12},{12,8},{16,20},{20,16},{24,28},{28,24},{32,36},... | collective-permute-start | bytes 36872 | tf_op jit(solution)/shard_map/ppermute | solution.py:292
  36.2 15.1 %collective-permute-start.7 = (f32[1,512]{1,0:T(1,128)S(1)}, f32[1,512]{1,0:T(1,128)S(1)}, u32[]{:S(2)}, u32[]{:S(2)}) collective-permute-start(f32[1,512]{1,0:T(1,128)S(1)} %get-tuple-element.176), channel_id=1, source_target_pairs={{252,0},{248,4},{4,8},{0,12},{12,16},{8,20},{20,24},{16,28},{28,32... | collective-permute-start | bytes 6152 | tf_op jit(solution)/shard_map/ppermute | solution.py:292
  40.1 11.1 %collective-permute-start.6 = (f32[1,512]{1,0:T(1,128)S(1)}, f32[1,512]{1,0:T(1,128)S(1)}, u32[]{:S(2)}, u32[]{:S(2)}) collective-permute-start(f32[1,512]{1,0:T(1,128)S(1)} %get-tuple-element.177), channel_id=1, source_target_pairs={{0,252},{4,248},{8,4},{12,0},{16,12},{20,8},{24,20},{28,16},{32,28... | collective-permute-start | bytes 6152 | tf_op jit(solution)/shard_map/ppermute | solution.py:292
  43.1 8.1 %collective-permute-start.8 = (f32[1,256]{1,0:T(1,128)S(1)}, f32[1,256]{1,0:T(1,128)S(1)}, u32[]{:S(2)}, u32[]{:S(2)}) collective-permute-start(f32[1,256]{1,0:T(1,128)S(1)} %get-tuple-element.171), channel_id=1, source_target_pairs={{240,0},{248,8},{0,16},{8,24},{16,32},{24,40},{32,48},{40,56},{48,... | collective-permute-start | bytes 3080 | tf_op jit(solution)/shard_map/ppermute | solution.py:292
  51.4 4.8 %collective-permute-start.11 = (f32[3,1024]{1,0:T(4,128)S(1)}, f32[3,1024]{1,0:T(4,128)S(1)}, u32[]{:S(2)}, u32[]{:S(2)}) collective-permute-start(f32[3,1024]{1,0:T(4,128)S(1)} %select_maximum_fusion), channel_id=1, source_target_pairs={{0,3},{1,2},{2,1},{3,0},{4,7},{5,6},{6,5},{7,4},{8,11},{9,10},{10,... | collective-permute-start | bytes 36872 | tf_op jit(solution)/shard_map/ppermute | solution.py:295
  52.8 5.2 %collective-permute-start.10 = (f32[3,1024]{1,0:T(4,128)S(1)}, f32[3,1024]{1,0:T(4,128)S(1)}, u32[]{:S(2)}, u32[]{:S(2)}) collective-permute-start(f32[3,1024]{1,0:T(4,128)S(1)} %select_maximum_fusion), channel_id=1, source_target_pairs={{0,2},{1,3},{2,0},{3,1},{4,6},{5,7},{6,4},{7,5},{8,10},{9,11},{10,... | collective-permute-start | bytes 36872 | tf_op jit(solution)/shard_map/ppermute | solution.py:295
  54.3 3.8 %collective-permute-start.9 = (f32[3,1024]{1,0:T(4,128)S(1)}, f32[3,1024]{1,0:T(4,128)S(1)}, u32[]{:S(2)}, u32[]{:S(2)}) collective-permute-start(f32[3,1024]{1,0:T(4,128)S(1)} %select_maximum_fusion), channel_id=1, source_target_pairs={{0,1},{1,0},{2,3},{3,2},{4,5},{5,4},{6,7},{7,6},{8,9},{9,8},{10,11... | collective-permute-start | bytes 36872 | tf_op jit(solution)/shard_map/ppermute | solution.py:295
  61.9 7.2 %collective-permute-start.12 = (f32[512,1024]{1,0:T(8,128)S(1)}, f32[512,1024]{1,0:T(8,128)S(1)}, u32[]{:S(2)}, u32[]{:S(2)}) collective-permute-start(f32[512,1024]{1,0:T(8,128)S(1)} %get-tuple-element.108), channel_id=1, source_target_pairs={{0,1},{1,0},{2,3},{3,2},{4,5},{5,4},{6,7},{7,6},{8,9},{9,8},{10,11... | collective-permute-start | bytes 6291464 | tf_op jit(solution)/shard_map/ppermute | solution.py:295
  62.3 6.8 %collective-permute-start.14 = (bf16[512,1024]{1,0:T(8,128)(2,1)S(1)}, bf16[512,1024]{1,0:T(8,128)(2,1)S(1)}, u32[]{:S(2)}, u32[]{:S(2)}) collective-permute-start(bf16[512,1024]{1,0:T(8,128)(2,1)S(1)} %get-tuple-element.101), channel_id=1, source_target_pairs={{0,1},{1,0},{2,3},{3,2},{4,5},{5,4},{6,7},{7,6},{8,9},{9,8},{10,11... | collective-permute-start | bytes 3145736 | tf_op jit(solution)/shard_map/ppermute | solution.py:295
  62.6 6.6 %collective-permute-start.13 = (f32[1,256]{1,0:T(1,128)S(1)}, f32[1,256]{1,0:T(1,128)S(1)}, u32[]{:S(2)}, u32[]{:S(2)}) collective-permute-start(f32[1,256]{1,0:T(1,128)S(1)} %fusion.3), channel_id=1, source_target_pairs={{8,0},{12,4},{0,8},{4,12},{24,16},{28,20},{16,24},{20,28},{40,32},... | collective-permute-start | bytes 3080 | tf_op jit(solution)/shard_map/ppermute | solution.py:292
  69.7 16.3 %collective-permute-start.15 = (bf16[256,1024]{1,0:T(8,128)(2,1)S(1)}, bf16[256,1024]{1,0:T(8,128)(2,1)S(1)}, u32[]{:S(2)}, u32[]{:S(2)}) collective-permute-start(bf16[256,1024]{1,0:T(8,128)(2,1)S(1)} %get-tuple-element.114), channel_id=1, source_target_pairs={{0,4},{4,0},{8,12},{12,8},{16,20},{20,16},{24,28},{28,24},{32,36},... | collective-permute-start | bytes 1572872 | tf_op jit(solution)/shard_map/ppermute | solution.py:292
  70.5 17.6 %collective-permute-start.16 = (bf16[256,1024]{1,0:T(8,128)(2,1)S(1)}, bf16[256,1024]{1,0:T(8,128)(2,1)S(1)}, u32[]{:S(2)}, u32[]{:S(2)}) collective-permute-start(bf16[256,1024]{1,0:T(8,128)(2,1)S(1)} %get-tuple-element.122), channel_id=1, source_target_pairs={{240,0},{248,8},{0,16},{8,24},{16,32},{24,40},{32,48},{40,56},{48,... | collective-permute-start | bytes 1572872 | tf_op jit(solution)/shard_map/ppermute | solution.py:292
  75.2 10.7 %collective-permute-start.19 = (f32[1,256]{1,0:T(1,128)S(1)}, f32[1,256]{1,0:T(1,128)S(1)}, u32[]{:S(2)}, u32[]{:S(2)}) collective-permute-start(f32[1,256]{1,0:T(1,128)S(1)} %add.201), channel_id=1, source_target_pairs={{192,0},{196,4},{200,8},{204,12},{208,16},{212,20},{216,24},{220,2... | collective-permute-start | bytes 3080 | tf_op jit(solution)/shard_map/ppermute | solution.py:292
  76.8 9.2 %collective-permute-start.18 = (f32[1,256]{1,0:T(1,128)S(1)}, f32[1,256]{1,0:T(1,128)S(1)}, u32[]{:S(2)}, u32[]{:S(2)}) collective-permute-start(f32[1,256]{1,0:T(1,128)S(1)} %add.201), channel_id=1, source_target_pairs={{64,0},{68,4},{72,8},{76,12},{80,16},{84,20},{88,24},{92,28},{96,3... | collective-permute-start | bytes 3080 | tf_op jit(solution)/shard_map/ppermute | solution.py:292
  80.9 5.2 %collective-permute-start.17 = (f32[1,256]{1,0:T(1,128)S(1)}, f32[1,256]{1,0:T(1,128)S(1)}, u32[]{:S(2)}, u32[]{:S(2)}) collective-permute-start(f32[1,256]{1,0:T(1,128)S(1)} %add.201), channel_id=1, source_target_pairs={{128,0},{132,4},{136,8},{140,12},{144,16},{148,20},{152,24},{156,2... | collective-permute-start | bytes 3080 | tf_op jit(solution)/shard_map/ppermute | solution.py:292
  86.0 13.5 %collective-permute-start.21 = (bf16[256,1024]{1,0:T(8,128)(2,1)S(1)}, bf16[256,1024]{1,0:T(8,128)(2,1)S(1)}, u32[]{:S(2)}, u32[]{:S(2)}) collective-permute-start(bf16[256,1024]{1,0:T(8,128)(2,1)S(1)} %get-tuple-element.133), channel_id=1, source_target_pairs={{0,4},{4,0},{8,12},{12,8},{16,20},{20,16},{24,28},{28,24},{32,36},... | collective-permute-start | bytes 1572872 | tf_op jit(solution)/shard_map/ppermute | solution.py:292
  88.3 25.4 %collective-permute-start.20 = (bf16[256,1024]{1,0:T(8,128)(2,1)S(1)}, bf16[256,1024]{1,0:T(8,128)(2,1)S(1)}, u32[]{:S(2)}, u32[]{:S(2)}) collective-permute-start(bf16[256,1024]{1,0:T(8,128)(2,1)S(1)} %add_convert_fusion), channel_id=1, source_target_pairs={{0,2},{1,3},{2,0},{3,1},{4,6},{5,7},{6,4},{7,5},{8,10},{9,11},{10,... | collective-permute-start | bytes 1572872 | tf_op jit(solution)/shard_map/ppermute | solution.py:295
  89.6 24.1 %collective-permute-start.22 = (bf16[256,1024]{1,0:T(8,128)(2,1)S(1)}, bf16[256,1024]{1,0:T(8,128)(2,1)S(1)}, u32[]{:S(2)}, u32[]{:S(2)}) collective-permute-start(bf16[256,1024]{1,0:T(8,128)(2,1)S(1)} %get-tuple-element.134), channel_id=1, source_target_pairs={{252,0},{248,4},{4,8},{0,12},{12,16},{8,20},{20,24},{16,28},{28,32... | collective-permute-start | bytes 1572872 | tf_op jit(solution)/shard_map/ppermute | solution.py:292
  89.6 9.9 %collective-permute-start.25 = (f32[1,256]{1,0:T(1,128)S(1)}, f32[1,256]{1,0:T(1,128)S(1)}, u32[]{:S(2)}, u32[]{:S(2)}) collective-permute-start(f32[1,256]{1,0:T(1,128)S(1)} %add_add_fusion.1), channel_id=1, source_target_pairs={{48,0},{52,4},{56,8},{60,12},{64,16},{68,20},{72,24},{76,28},{80,3... | collective-permute-start | bytes 3080 | tf_op jit(solution)/shard_map/ppermute | solution.py:292
  94.6 6.1 %collective-permute-start.24 = (f32[1,256]{1,0:T(1,128)S(1)}, f32[1,256]{1,0:T(1,128)S(1)}, u32[]{:S(2)}, u32[]{:S(2)}) collective-permute-start(f32[1,256]{1,0:T(1,128)S(1)} %add_add_fusion.1), channel_id=1, source_target_pairs={{32,0},{36,4},{40,8},{44,12},{48,16},{52,20},{56,24},{60,28},{64,3... | collective-permute-start | bytes 3080 | tf_op jit(solution)/shard_map/ppermute | solution.py:292
  99.4 3.6 %collective-permute-start.23 = (f32[1,256]{1,0:T(1,128)S(1)}, f32[1,256]{1,0:T(1,128)S(1)}, u32[]{:S(2)}, u32[]{:S(2)}) collective-permute-start(f32[1,256]{1,0:T(1,128)S(1)} %add_add_fusion.1), channel_id=1, source_target_pairs={{16,0},{20,4},{24,8},{28,12},{32,16},{36,20},{40,24},{44,28},{48,3... | collective-permute-start | bytes 3080 | tf_op jit(solution)/shard_map/ppermute | solution.py:292

commit v4 on v3

--- a/solution.py
+++ b/solution.py
@@ -407,7 +407,7 @@
         [((rows, d), F32), ((rows, d), BF16)], 16 * tile, [text_buf, sems(4)],
     )(order, evens, logit_scale, w_t, text_emb, w_a, w_b, near_a, near_b, g_y)
     g_x, loss_part = tie(g_x, loss_part)
-    got = [shifted(loss_part, x, z) for x, z in ((blocks // 2, 0), (0, 4), (blocks // 2, 4))]
+    got = [shifted(loss_part, 0, z) for z in (1, 2, 3)]
     got_zero = got_t[:rows]
     part = keep_t[rows:] + got_t[rows:].astype(F32)
     part, home_1, g_i, y_got, *got = tie(part, home_1, g_i, y_got, *got)
@@ -416,7 +416,7 @@
     one, loss_part, g_x = tie(one, loss_part, g_x)
     across = swap(one, 2)
     x_got = hop(g_x, x_back)
-    got = [shifted(loss_part, 0, z) for z in (1, 2, 3)]
+    got = [shifted(loss_part, x, z) for x, z in ((blocks // 2, 0), (0, 4), (blocks // 2, 4))]
     across, home_0, x_got, *got = tie(across, home_0, x_got, *got)
     grad_text, grad_image, loss = local_call(
         finish_kernel, "finish", [VMEM, ANY, ANY, ANY, VMEM, ANY, ANY, VMEM, SMEM],

time: 116 us -> 117 us (level)
  waiting for transfers between devices: 33.2 us -> 37 us
  starting transfers between devices: 52.8 us -> 49.1 us
    ppermute x19, waiting for transfers between devices: 19.2 us -> 31.3 us  [hop(): return lax.ppermute(value, 'blk', route)]
    ppermute x7, waiting for transfers between devices: 14 us -> 5.7 us  [swap(): return lax.ppermute(value, 'rep', [(i, i ^ mask) for i in range(4)])]
    ppermute x19, starting transfers between devices: 47.4 us -> 43.5 us  [hop(): return lax.ppermute(value, 'blk', route)]
  transfers between devices with their start and end apart: 26 -> 26, of which waited for: 11 -> 12; matrix products, arithmetic and copies ran while one was open for 0% -> 0% of each run, Pallas kernels for 13% -> 13%
where the time goes in v4:
time: 117 us; the launch traced here: 116 us
  starting transfers between devices  49.1 us (42%)
  waiting for transfers between devices  37 us (32%)
  Pallas kernels  23.7 us (20%)
  local copies, waits for them, and re-layouts  2.48 us (2%)
  other arithmetic  2.23 us (2%)
  between operations  1.84 us (2%)
    ppermute x19, starting transfers between devices, hop(): return lax.ppermute(value, 'blk', route)  43.5 us
    ppermute x19, waiting for transfers between devices, hop(): return lax.ppermute(value, 'blk', route)  31.3 us
    ppermute x7, waiting for transfers between devices, swap(): return lax.ppermute(value, 'rep', [(i, i ^ mask) for i in range(4)])  5.7 us
    ppermute x7, starting transfers between devices, swap(): return lax.ppermute(value, 'rep', [(i, i ^ mask) for i in range(4)])  5.59 us
    pallas_call x1, Pallas kernels, per_device(): local_call(own_image_kernel, 'own_image', [SMEM] * 2 + [HBM] * 2, [((rows...  3.4 us
    pallas_call x1, Pallas kernels, per_device(): local_call(x_logits_kernel, 'x_logits', [SMEM] * 2 + [HBM] * 2, [((rows,...  3.4 us
    pallas_call x1, Pallas kernels, per_device(): local_call(first_logits_kernel, 'first_logits', [SMEM] * 2 + [HBM] * 4, [...  3.33 us
    pallas_call x1, Pallas kernels, per_device(): local_call(far_logits_kernel, 'far_logits', [SMEM, VMEM, VMEM, HBM], [((2...  3.03 us
  transfers between devices with their start and end apart: 26, of which 12 were waited for; matrix products, arithmetic and copies ran while one was open for 0% of the time, Pallas kernels for 13%

profile of v4, /device:TPU:16, one launch (start us, length us, event | category | flops | bytes accessed | tf_op | source)
XLA Modules:
  0.0 116.4 jit_solution(34390027691267536)
XLA Ops:
  0.7 1.4 %constant_dynamic-slice_fusion.1 = (bf16[256,1024]{1,0:T(8,128)(2,1)S(1)}, bf16[256,1024]{1,0:T(8,128)(2,1)S(1)}) fusion(bf16[1024,1024]{1,0:T(8,128)(2,1)} %t_in.5, s32[]{:T(128)S(6)} %select_n.35, s32[]{:T(128)S(6)} %select_n.36), kind=kLoop, calls=%fused_computation.57 | loop fusion | bytes 2097160 | tf_op jit(solution)/shard_map/dynamic_slice | solution.py:302
  4.4 1.4 %collective-permute-start.2 = (bf16[256,1024]{1,0:T(8,128)(2,1)S(1)}, bf16[256,1024]{1,0:T(8,128)(2,1)S(1)}, u32[]{:S(2)}, u32[]{:S(2)}) collective-permute-start(bf16[256,1024]{1,0:T(8,128)(2,1)S(1)} %copy-done.1), channel_id=1, source_target_pairs={{0,252},{4,248},{8,4},{12,0},{16,12},{20,8},{24,20},{28,16},{32,28... | collective-permute-start | bytes 1572872 | tf_op jit(solution)/shard_map/ppermute | solution.py:292
  5.8 7.3 %collective-permute-start.1 = (bf16[256,1024]{1,0:T(8,128)(2,1)S(1)}, bf16[256,1024]{1,0:T(8,128)(2,1)}, u32[]{:S(2)}, u32[]{:S(2)}) collective-permute-start(bf16[256,1024]{1,0:T(8,128)(2,1)S(1)} %copy-done.1), channel_id=1, source_target_pairs={{0,240},{8,248},{16,0},{24,8},{32,16},{40,24},{48,32},{56,40},{64,... | collective-permute-start | bytes 1572872 | tf_op jit(solution)/shard_map/ppermute | solution.py:292
  13.9 3.4 %own_image.1 = (f32[256,1024]{1,0:T(8,128)S(1)}, f32[1,256]{1,0:T(1,128)S(1)}, f32[1,1024]{1,0:T(1,128)S(1)}, f32[1,256]{1,0:T(1,128)S(1)}) custom-call(s32[4]{0:T(128)S(1)} %pad_add_fusion.order, f32[1]{0:T(128)S(6)} %copy.7.scale, bf16[256,1024]{1,0:T(8,128)(2,1)S(1)} %copy-done.1, bf16[1024,1024]{1,0:T(8,128)(2,1)S(1)} %copy-done), custom_call_target="tpu_custom_call" | custom-call | flops 1 | bytes 1 | tf_op jit(solution)/shard_map/own_image/pallas_call | solution.py:311
  17.3 2.9 %collective-permute-start.3 = (f32[1,256]{1,0:T(1,128)S(1)}, f32[1,256]{1,0:T(1,128)S(1)}, u32[]{:S(2)}, u32[]{:S(2)}) collective-permute-start(f32[1,256]{1,0:T(1,128)S(1)} %get-tuple-element.75), channel_id=1, source_target_pairs={{0,240},{8,248},{16,0},{24,8},{32,16},{40,24},{48,32},{56,40},{64,... | collective-permute-start | bytes 3080 | tf_op jit(solution)/shard_map/ppermute | solution.py:292
  20.2 3.4 %x_logits.1 = (f32[256,1024]{1,0:T(8,128)S(1)}, f32[1,256]{1,0:T(1,128)S(1)}, f32[1,1024]{1,0:T(1,128)S(1)}) custom-call(s32[4]{0:T(128)S(1)} %pad_add_fusion.order, f32[1]{0:T(128)S(6)} %copy.7.scale, bf16[256,1024]{1,0:T(8,128)(2,1)S(1)} %collective-permute-done.2.x_in, bf16[1024,1024]{1,0:T(8,128)(2,1)S(1)} %copy-done), custom_call_target="tpu_custom_call" | custom-call | flops 1 | bytes 1 | tf_op jit(solution)/shard_map/x_logits/pallas_call | solution.py:317
  24.6 3.7 %collective-permute-done.v_in = bf16[512,1024]{1,0:T(8,128)(2,1)} collective-permute-done((bf16[512,1024]{1,0:T(8,128)(2,1)}, bf16[512,1024]{1,0:T(8,128)(2,1)}, u32[]{:S(2)}, u32[]{:S(2)}) %collective-permute-start) | collective-permute-done | bytes 1048608 | tf_op jit(solution)/shard_map/ppermute | solution.py:292
  28.4 3.3 %first_logits.1 = (f32[512,512]{1,0:T(8,128)S(1)}, f32[1,512]{1,0:T(1,128)S(1)}, f32[1,512]{1,0:T(1,128)S(1)}, bf16[512,1024]{1,0:T(8,128)(2,1)S(1)}, bf16[512,1024]{1,0:T(8,128)(2,1)S(1)}) custom-call(s32[1]{0:T(128)} %bitcast.4.even, f32[1]{0:T(128)S(6)} %copy.7.scale, bf16[256,1024]{1,0:T(8,128)(2,1)S(1)} %copy-done.1, ...), custom_call_target="tpu_custom_call" | custom-call | flops 1 | bytes 1 | tf_op jit(solution)/shard_map/first_logits/pallas_call | solution.py:325
  31.8 3.0 %far_logits.1 = (f32[512,512]{1,0:T(8,128)S(1)}, f32[1,512]{1,0:T(1,128)S(1)}, f32[1,512]{1,0:T(1,128)S(1)}, bf16[512,1024]{1,0:T(8,128)(2,1)S(1)}) custom-call(f32[1]{0:T(128)S(6)} %copy.7.scale, f32[1,512]{1,0:T(1,128)S(1)} %get-tuple-element.85.before, bf16[512,1024]{1,0:T(8,128)(2,1)S(1)} %get-tuple-element.86.yx, ...), custom_call_target="tpu_custom_call" | custom-call | flops 1 | bytes 1 | tf_op jit(solution)/shard_map/far_logits/pallas_call | solution.py:330
  36.2 4.0 %collective-permute-start.7 = (f32[1,512]{1,0:T(1,128)S(1)}, f32[1,512]{1,0:T(1,128)S(1)}, u32[]{:S(2)}, u32[]{:S(2)}) collective-permute-start(f32[1,512]{1,0:T(1,128)S(1)} %get-tuple-element.176), channel_id=1, source_target_pairs={{252,0},{248,4},{4,8},{0,12},{12,16},{8,20},{20,24},{16,28},{28,32... | collective-permute-start | bytes 6152 | tf_op jit(solution)/shard_map/ppermute | solution.py:292
  40.1 3.0 %collective-permute-start.6 = (f32[1,512]{1,0:T(1,128)S(1)}, f32[1,512]{1,0:T(1,128)S(1)}, u32[]{:S(2)}, u32[]{:S(2)}) collective-permute-start(f32[1,512]{1,0:T(1,128)S(1)} %get-tuple-element.177), channel_id=1, source_target_pairs={{0,252},{4,248},{8,4},{12,0},{16,12},{20,8},{24,20},{28,16},{32,28... | collective-permute-start | bytes 6152 | tf_op jit(solution)/shard_map/ppermute | solution.py:292
  43.1 1.9 %collective-permute-start.8 = (f32[1,256]{1,0:T(1,128)S(1)}, f32[1,256]{1,0:T(1,128)S(1)}, u32[]{:S(2)}, u32[]{:S(2)}) collective-permute-start(f32[1,256]{1,0:T(1,128)S(1)} %get-tuple-element.171), channel_id=1, source_target_pairs={{240,0},{248,8},{0,16},{8,24},{16,32},{24,40},{32,48},{40,56},{48,... | collective-permute-start | bytes 3080 | tf_op jit(solution)/shard_map/ppermute | solution.py:292
  45.0 6.2 %collective-permute-done.8 = f32[1,256]{1,0:T(1,128)S(1)} collective-permute-done((f32[1,256]{1,0:T(1,128)S(1)}, f32[1,256]{1,0:T(1,128)S(1)}, u32[]{:S(2)}, u32[]{:S(2)}) %collective-permute-start.8) | collective-permute-done | bytes 1056 | tf_op jit(solution)/shard_map/ppermute | solution.py:292
  51.4 1.5 %collective-permute-start.11 = (f32[3,1024]{1,0:T(4,128)S(1)}, f32[3,1024]{1,0:T(4,128)S(1)}, u32[]{:S(2)}, u32[]{:S(2)}) collective-permute-start(f32[3,1024]{1,0:T(4,128)S(1)} %select_maximum_fusion), channel_id=1, source_target_pairs={{0,3},{1,2},{2,1},{3,0},{4,7},{5,6},{6,5},{7,4},{8,11},{9,10},{10,... | collective-permute-start | bytes 36872 | tf_op jit(solution)/shard_map/ppermute | solution.py:295
  52.8 1.4 %collective-permute-start.10 = (f32[3,1024]{1,0:T(4,128)S(1)}, f32[3,1024]{1,0:T(4,128)S(1)}, u32[]{:S(2)}, u32[]{:S(2)}) collective-permute-start(f32[3,1024]{1,0:T(4,128)S(1)} %select_maximum_fusion), channel_id=1, source_target_pairs={{0,2},{1,3},{2,0},{3,1},{4,6},{5,7},{6,4},{7,5},{8,10},{9,11},{10,... | collective-permute-start | bytes 36872 | tf_op jit(solution)/shard_map/ppermute | solution.py:295
  56.1 2.0 %collective-permute-done.10 = f32[3,1024]{1,0:T(4,128)S(1)} collective-permute-done((f32[3,1024]{1,0:T(4,128)S(1)}, f32[3,1024]{1,0:T(4,128)S(1)}, u32[]{:S(2)}, u32[]{:S(2)}) %collective-permute-start.10) | collective-permute-done | bytes 12320 | tf_op jit(solution)/shard_map/ppermute | solution.py:295
  58.2 2.7 %own_text.1 = (bf16[512,1024]{1,0:T(8,128)(2,1)S(1)}, bf16[512,1024]{1,0:T(8,128)(2,1)S(1)}, f32[512,1024]{1,0:T(8,128)S(1)}) custom-call(f32[1]{0:T(128)S(6)} %copy.7.scale, f32[1,512]{1,0:T(1,128)S(1)} %get-tuple-element.175.row, f32[1,1024]{1,0:T(1,128)S(1)} %get-tuple-element.168.col, f32[256,1024]{1,0:T(8,128)S(1)} %copy-done.3, ...), custom_call_target="tpu_custom_call" | custom-call | flops 1 | bytes 1 | tf_op jit(solution)/shard_map/own_text/pallas_call | solution.py:382
  62.6 5.1 %collective-permute-start.13 = (f32[1,256]{1,0:T(1,128)S(1)}, f32[1,256]{1,0:T(1,128)S(1)}, u32[]{:S(2)}, u32[]{:S(2)}) collective-permute-start(f32[1,256]{1,0:T(1,128)S(1)} %fusion.3), channel_id=1, source_target_pairs={{8,0},{12,4},{0,8},{4,12},{24,16},{28,20},{16,24},{20,28},{40,32},... | collective-permute-start | bytes 3080 | tf_op jit(solution)/shard_map/ppermute | solution.py:292
  70.5 1.9 %collective-permute-start.16 = (bf16[256,1024]{1,0:T(8,128)(2,1)S(1)}, bf16[256,1024]{1,0:T(8,128)(2,1)S(1)}, u32[]{:S(2)}, u32[]{:S(2)}) collective-permute-start(bf16[256,1024]{1,0:T(8,128)(2,1)S(1)} %get-tuple-element.122), channel_id=1, source_target_pairs={{240,0},{248,8},{0,16},{8,24},{16,32},{24,40},{32,48},{40,56},{48,... | collective-permute-start | bytes 1572872 | tf_op jit(solution)/shard_map/ppermute | solution.py:292
  72.4 2.8 %image_grads.1 = (f32[256,1024]{1,0:T(8,128)S(1)}, bf16[256,1024]{1,0:T(8,128)(2,1)S(1)}) custom-call(s32[4]{0:T(128)S(1)} %pad_add_fusion.order, s32[1]{0:T(128)} %bitcast.4.even, f32[1]{0:T(128)S(6)} %copy.7.scale, bf16[512,1024]{1,0:T(8,128)(2,1)S(1)} %get-tuple-element.115.w, bf16[1024,1024]{1,0:T(8,128)(2,1)S(1)} %copy-done, ...), custom_call_target="tpu_custom_call" | custom-call | flops 1 | bytes 1 | tf_op jit(solution)/shard_map/image_grads/pallas_call | solution.py:405
  75.2 3.1 %collective-permute-start.19 = (f32[1,256]{1,0:T(1,128)S(1)}, f32[1,256]{1,0:T(1,128)S(1)}, u32[]{:S(2)}, u32[]{:S(2)}) collective-permute-start(f32[1,256]{1,0:T(1,128)S(1)} %add.201), channel_id=1, source_target_pairs={{48,0},{52,4},{56,8},{60,12},{64,16},{68,20},{72,24},{76,28},{80,3... | collective-permute-start | bytes 3080 | tf_op jit(solution)/shard_map/ppermute | solution.py:292
  78.3 1.7 %collective-permute-start.18 = (f32[1,256]{1,0:T(1,128)S(1)}, f32[1,256]{1,0:T(1,128)S(1)}, u32[]{:S(2)}, u32[]{:S(2)}) collective-permute-start(f32[1,256]{1,0:T(1,128)S(1)} %add.201), channel_id=1, source_target_pairs={{32,0},{36,4},{40,8},{44,12},{48,16},{52,20},{56,24},{60,28},{64,3... | collective-permute-start | bytes 3080 | tf_op jit(solution)/shard_map/ppermute | solution.py:292
  81.4 1.3 %collective-permute-done.18 = f32[1,256]{1,0:T(1,128)S(1)} collective-permute-done((f32[1,256]{1,0:T(1,128)S(1)}, f32[1,256]{1,0:T(1,128)S(1)}, u32[]{:S(2)}, u32[]{:S(2)}) %collective-permute-start.18) | collective-permute-done | bytes 1056 | tf_op jit(solution)/shard_map/ppermute | solution.py:292
  83.7 4.3 %collective-permute-done.16.y_got = bf16[256,1024]{1,0:T(8,128)(2,1)S(1)} collective-permute-done((bf16[256,1024]{1,0:T(8,128)(2,1)S(1)}, bf16[256,1024]{1,0:T(8,128)(2,1)S(1)}, u32[]{:S(2)}, u32[]{:S(2)}) %collective-permute-start.16) | collective-permute-done | bytes 524320 | tf_op jit(solution)/shard_map/ppermute | solution.py:292
  88.2 1.5 %collective-permute-start.20 = (bf16[256,1024]{1,0:T(8,128)(2,1)S(1)}, bf16[256,1024]{1,0:T(8,128)(2,1)S(1)}, u32[]{:S(2)}, u32[]{:S(2)}) collective-permute-start(bf16[256,1024]{1,0:T(8,128)(2,1)S(1)} %add_convert_fusion), channel_id=1, source_target_pairs={{0,2},{1,3},{2,0},{3,1},{4,6},{5,7},{6,4},{7,5},{8,10},{9,11},{10,... | collective-permute-start | bytes 1572872 | tf_op jit(solution)/shard_map/ppermute | solution.py:295
  89.7 2.9 %collective-permute-start.25 = (f32[1,256]{1,0:T(1,128)S(1)}, f32[1,256]{1,0:T(1,128)S(1)}, u32[]{:S(2)}, u32[]{:S(2)}) collective-permute-start(f32[1,256]{1,0:T(1,128)S(1)} %add_add_fusion.1), channel_id=1, source_target_pairs={{192,0},{196,4},{200,8},{204,12},{208,16},{212,20},{216,24},{220,2... | collective-permute-start | bytes 3080 | tf_op jit(solution)/shard_map/ppermute | solution.py:292
  92.6 2.7 %collective-permute-start.24 = (f32[1,256]{1,0:T(1,128)S(1)}, f32[1,256]{1,0:T(1,128)S(1)}, u32[]{:S(2)}, u32[]{:S(2)}) collective-permute-start(f32[1,256]{1,0:T(1,128)S(1)} %add_add_fusion.1), channel_id=1, source_target_pairs={{64,0},{68,4},{72,8},{76,12},{80,16},{84,20},{88,24},{92,28},{96,3... | collective-permute-start | bytes 3080 | tf_op jit(solution)/shard_map/ppermute | solution.py:292
  95.3 1.8 %collective-permute-start.23 = (f32[1,256]{1,0:T(1,128)S(1)}, f32[1,256]{1,0:T(1,128)S(1)}, u32[]{:S(2)}, u32[]{:S(2)}) collective-permute-start(f32[1,256]{1,0:T(1,128)S(1)} %add_add_fusion.1), channel_id=1, source_target_pairs={{128,0},{132,4},{136,8},{140,12},{144,16},{148,20},{152,24},{156,2... | collective-permute-start | bytes 3080 | tf_op jit(solution)/shard_map/ppermute | solution.py:292
  97.2 5.7 %collective-permute-done.25 = f32[1,256]{1,0:T(1,128)S(1)} collective-permute-done((f32[1,256]{1,0:T(1,128)S(1)}, f32[1,256]{1,0:T(1,128)S(1)}, u32[]{:S(2)}, u32[]{:S(2)}) %collective-permute-start.25) | collective-permute-done | bytes 1056 | tf_op jit(solution)/shard_map/ppermute | solution.py:292
  102.9 8.6 %collective-permute-done.23 = f32[1,256]{1,0:T(1,128)S(1)} collective-permute-done((f32[1,256]{1,0:T(1,128)S(1)}, f32[1,256]{1,0:T(1,128)S(1)}, u32[]{:S(2)}, u32[]{:S(2)}) %collective-permute-start.23) | collective-permute-done | bytes 1056 | tf_op jit(solution)/shard_map/ppermute | solution.py:292
  111.4 2.4 %collective-permute-done.20.across = bf16[256,1024]{1,0:T(8,128)(2,1)S(1)} collective-permute-done((bf16[256,1024]{1,0:T(8,128)(2,1)S(1)}, bf16[256,1024]{1,0:T(8,128)(2,1)S(1)}, u32[]{:S(2)}, u32[]{:S(2)}) %collective-permute-start.20) | collective-permute-done | bytes 524320 | tf_op jit(solution)/shard_map/ppermute | solution.py:295
  113.9 2.3 %finish.1 = (f32[256,1024]{1,0:T(8,128)}, f32[256,1024]{1,0:T(8,128)}, f32[1,1]{1,0:T(1,128)}) custom-call(f32[512,1024]{1,0:T(8,128)S(1)} %get-tuple-element.99.keep, bf16[256,1024]{1,0:T(8,128)(2,1)S(1)} %slice.147.got_zero, bf16[256,1024]{1,0:T(8,128)(2,1)S(1)} %collective-permute-done.21.home_0, bf16[256,1024]{1,0:T(8,128)(2,1)S(1)} %collective-permute-done.20.across, ...), custom_call_target="tpu_custom_call" | custom-call | flops 1 | bytes 1 | tf_op jit(solution)/shard_map/finish/pallas_call | solution.py:421
  (69 shorter events, 13.9 us)
Async XLA Ops:
  0.6 3.8 %copy-start.1 = (bf16[256,1024]{1,0:T(8,128)(2,1)S(1)}, bf16[256,1024]{1,0:T(8,128)(2,1)}, u32[]{:S(2)}) copy-start(bf16[256,1024]{1,0:T(8,128)(2,1)} %a_in.5) | copy-start | bytes 1572868
  0.7 13.2 %copy-start = (bf16[1024,1024]{1,0:T(8,128)(2,1)S(1)}, bf16[1024,1024]{1,0:T(8,128)(2,1)}, u32[]{:S(2)}) copy-start(bf16[1024,1024]{1,0:T(8,128)(2,1)} %t_in.5) | copy-start | bytes 6291460
  3.1 25.2 %collective-permute-start = (bf16[512,1024]{1,0:T(8,128)(2,1)}, bf16[512,1024]{1,0:T(8,128)(2,1)}, u32[]{:S(2)}, u32[]{:S(2)}) collective-permute-start(bf16[512,1024]{1,0:T(8,128)(2,1)} %pad_maximum_fusion), channel_id=1, source_target_pairs={{0,4},{4,0},{8,12},{12,8},{16,20},{20,16},{24,28},{28,24},{32,36},... | collective-permute-start | bytes 3145736 | tf_op jit(solution)/shard_map/ppermute | solution.py:292
  4.4 15.8 %collective-permute-start.2 = (bf16[256,1024]{1,0:T(8,128)(2,1)S(1)}, bf16[256,1024]{1,0:T(8,128)(2,1)S(1)}, u32[]{:S(2)}, u32[]{:S(2)}) collective-permute-start(bf16[256,1024]{1,0:T(8,128)(2,1)S(1)} %copy-done.1), channel_id=1, source_target_pairs={{0,252},{4,248},{8,4},{12,0},{16,12},{20,8},{24,20},{28,16},{32,28... | collective-permute-start | bytes 1572872 | tf_op jit(solution)/shard_map/ppermute | solution.py:292
  5.8 18.8 %collective-permute-start.1 = (bf16[256,1024]{1,0:T(8,128)(2,1)S(1)}, bf16[256,1024]{1,0:T(8,128)(2,1)}, u32[]{:S(2)}, u32[]{:S(2)}) collective-permute-start(bf16[256,1024]{1,0:T(8,128)(2,1)S(1)} %copy-done.1), channel_id=1, source_target_pairs={{0,240},{8,248},{16,0},{24,8},{32,16},{40,24},{48,32},{56,40},{64,... | collective-permute-start | bytes 1572872 | tf_op jit(solution)/shard_map/ppermute | solution.py:292
  17.3 7.3 %copy-start.2 = (f32[256,1024]{1,0:T(8,128)}, f32[256,1024]{1,0:T(8,128)S(1)}, u32[]{:S(2)}) copy-start(f32[256,1024]{1,0:T(8,128)S(1)} %get-tuple-element.97.si_in) | copy-start | bytes 3145732
  17.3 7.3 %collective-permute-start.3 = (f32[1,256]{1,0:T(1,128)S(1)}, f32[1,256]{1,0:T(1,128)S(1)}, u32[]{:S(2)}, u32[]{:S(2)}) collective-permute-start(f32[1,256]{1,0:T(1,128)S(1)} %get-tuple-element.75), channel_id=1, source_target_pairs={{0,240},{8,248},{16,0},{24,8},{32,16},{40,24},{48,32},{56,40},{64,... | collective-permute-start | bytes 3080 | tf_op jit(solution)/shard_map/ppermute | solution.py:292
  23.6 1.0 copy-start.4
  28.3 3.4 %collective-permute-start.4 = (bf16[512,1024]{1,0:T(8,128)(2,1)}, bf16[512,1024]{1,0:T(8,128)(2,1)}, u32[]{:S(2)}, u32[]{:S(2)}) collective-permute-start(bf16[512,1024]{1,0:T(8,128)(2,1)} %collective-permute-done.v_in), channel_id=1, source_target_pairs={{0,1},{1,0},{2,3},{3,2},{4,5},{5,4},{6,7},{7,6},{8,9},{9,8},{10,11... | collective-permute-start | bytes 3145736 | tf_op jit(solution)/shard_map/ppermute | solution.py:295
  28.4 29.8 %copy-start.3 = (f32[256,1024]{1,0:T(8,128)S(1)}, f32[256,1024]{1,0:T(8,128)}, u32[]{:S(2)}) copy-start(f32[256,1024]{1,0:T(8,128)} %copy-done.2) | copy-start | bytes 3145732
  28.4 29.8 %copy-start.5 = (f32[256,1024]{1,0:T(8,128)S(1)}, f32[256,1024]{1,0:T(8,128)}, u32[]{:S(2)}) copy-start(f32[256,1024]{1,0:T(8,128)} %copy-done.4) | copy-start | bytes 3145732
  34.8 16.4 %collective-permute-start.5 = (f32[3,1024]{1,0:T(4,128)S(1)}, f32[3,1024]{1,0:T(4,128)S(1)}, u32[]{:S(2)}, u32[]{:S(2)}) collective-permute-start(f32[3,1024]{1,0:T(4,128)S(1)} %select_maximum_fusion.1), channel_id=1, source_target_pairs={{0,4},{4,0},{8,12},{12,8},{16,20},{20,16},{24,28},{28,24},{32,36},... | collective-permute-start | bytes 36872 | tf_op jit(solution)/shard_map/ppermute | solution.py:292
  36.2 15.1 %collective-permute-start.7 = (f32[1,512]{1,0:T(1,128)S(1)}, f32[1,512]{1,0:T(1,128)S(1)}, u32[]{:S(2)}, u32[]{:S(2)}) collective-permute-start(f32[1,512]{1,0:T(1,128)S(1)} %get-tuple-element.176), channel_id=1, source_target_pairs={{252,0},{248,4},{4,8},{0,12},{12,16},{8,20},{20,24},{16,28},{28,32... | collective-permute-start | bytes 6152 | tf_op jit(solution)/shard_map/ppermute | solution.py:292
  40.1 11.1 %collective-permute-start.6 = (f32[1,512]{1,0:T(1,128)S(1)}, f32[1,512]{1,0:T(1,128)S(1)}, u32[]{:S(2)}, u32[]{:S(2)}) collective-permute-start(f32[1,512]{1,0:T(1,128)S(1)} %get-tuple-element.177), channel_id=1, source_target_pairs={{0,252},{4,248},{8,4},{12,0},{16,12},{20,8},{24,20},{28,16},{32,28... | collective-permute-start | bytes 6152 | tf_op jit(solution)/shard_map/ppermute | solution.py:292
  43.1 8.1 %collective-permute-start.8 = (f32[1,256]{1,0:T(1,128)S(1)}, f32[1,256]{1,0:T(1,128)S(1)}, u32[]{:S(2)}, u32[]{:S(2)}) collective-permute-start(f32[1,256]{1,0:T(1,128)S(1)} %get-tuple-element.171), channel_id=1, source_target_pairs={{240,0},{248,8},{0,16},{8,24},{16,32},{24,40},{32,48},{40,56},{48,... | collective-permute-start | bytes 3080 | tf_op jit(solution)/shard_map/ppermute | solution.py:292
  51.4 4.8 %collective-permute-start.11 = (f32[3,1024]{1,0:T(4,128)S(1)}, f32[3,1024]{1,0:T(4,128)S(1)}, u32[]{:S(2)}, u32[]{:S(2)}) collective-permute-start(f32[3,1024]{1,0:T(4,128)S(1)} %select_maximum_fusion), channel_id=1, source_target_pairs={{0,3},{1,2},{2,1},{3,0},{4,7},{5,6},{6,5},{7,4},{8,11},{9,10},{10,... | collective-permute-start | bytes 36872 | tf_op jit(solution)/shard_map/ppermute | solution.py:295
  52.8 5.2 %collective-permute-start.10 = (f32[3,1024]{1,0:T(4,128)S(1)}, f32[3,1024]{1,0:T(4,128)S(1)}, u32[]{:S(2)}, u32[]{:S(2)}) collective-permute-start(f32[3,1024]{1,0:T(4,128)S(1)} %select_maximum_fusion), channel_id=1, source_target_pairs={{0,2},{1,3},{2,0},{3,1},{4,6},{5,7},{6,4},{7,5},{8,10},{9,11},{10,... | collective-permute-start | bytes 36872 | tf_op jit(solution)/shard_map/ppermute | solution.py:295
  54.3 3.8 %collective-permute-start.9 = (f32[3,1024]{1,0:T(4,128)S(1)}, f32[3,1024]{1,0:T(4,128)S(1)}, u32[]{:S(2)}, u32[]{:S(2)}) collective-permute-start(f32[3,1024]{1,0:T(4,128)S(1)} %select_maximum_fusion), channel_id=1, source_target_pairs={{0,1},{1,0},{2,3},{3,2},{4,5},{5,4},{6,7},{7,6},{8,9},{9,8},{10,11... | collective-permute-start | bytes 36872 | tf_op jit(solution)/shard_map/ppermute | solution.py:295
  61.9 7.2 %collective-permute-start.12 = (f32[512,1024]{1,0:T(8,128)S(1)}, f32[512,1024]{1,0:T(8,128)S(1)}, u32[]{:S(2)}, u32[]{:S(2)}) collective-permute-start(f32[512,1024]{1,0:T(8,128)S(1)} %get-tuple-element.108), channel_id=1, source_target_pairs={{0,1},{1,0},{2,3},{3,2},{4,5},{5,4},{6,7},{7,6},{8,9},{9,8},{10,11... | collective-permute-start | bytes 6291464 | tf_op jit(solution)/shard_map/ppermute | solution.py:295
  62.3 6.8 %collective-permute-start.14 = (bf16[512,1024]{1,0:T(8,128)(2,1)S(1)}, bf16[512,1024]{1,0:T(8,128)(2,1)S(1)}, u32[]{:S(2)}, u32[]{:S(2)}) collective-permute-start(bf16[512,1024]{1,0:T(8,128)(2,1)S(1)} %get-tuple-element.101), channel_id=1, source_target_pairs={{0,1},{1,0},{2,3},{3,2},{4,5},{5,4},{6,7},{7,6},{8,9},{9,8},{10,11... | collective-permute-start | bytes 3145736 | tf_op jit(solution)/shard_map/ppermute | solution.py:295
  62.6 6.6 %collective-permute-start.13 = (f32[1,256]{1,0:T(1,128)S(1)}, f32[1,256]{1,0:T(1,128)S(1)}, u32[]{:S(2)}, u32[]{:S(2)}) collective-permute-start(f32[1,256]{1,0:T(1,128)S(1)} %fusion.3), channel_id=1, source_target_pairs={{8,0},{12,4},{0,8},{4,12},{24,16},{28,20},{16,24},{20,28},{40,32},... | collective-permute-start | bytes 3080 | tf_op jit(solution)/shard_map/ppermute | solution.py:292
  69.7 14.0 %collective-permute-start.15 = (bf16[256,1024]{1,0:T(8,128)(2,1)S(1)}, bf16[256,1024]{1,0:T(8,128)(2,1)S(1)}, u32[]{:S(2)}, u32[]{:S(2)}) collective-permute-start(bf16[256,1024]{1,0:T(8,128)(2,1)S(1)} %get-tuple-element.114), channel_id=1, source_target_pairs={{0,4},{4,0},{8,12},{12,8},{16,20},{20,16},{24,28},{28,24},{32,36},... | collective-permute-start | bytes 1572872 | tf_op jit(solution)/shard_map/ppermute | solution.py:292
  70.5 17.5 %collective-permute-start.16 = (bf16[256,1024]{1,0:T(8,128)(2,1)S(1)}, bf16[256,1024]{1,0:T(8,128)(2,1)S(1)}, u32[]{:S(2)}, u32[]{:S(2)}) collective-permute-start(bf16[256,1024]{1,0:T(8,128)(2,1)S(1)} %get-tuple-element.122), channel_id=1, source_target_pairs={{240,0},{248,8},{0,16},{8,24},{16,32},{24,40},{32,48},{40,56},{48,... | collective-permute-start | bytes 1572872 | tf_op jit(solution)/shard_map/ppermute | solution.py:292
  75.2 6.0 %collective-permute-start.19 = (f32[1,256]{1,0:T(1,128)S(1)}, f32[1,256]{1,0:T(1,128)S(1)}, u32[]{:S(2)}, u32[]{:S(2)}) collective-permute-start(f32[1,256]{1,0:T(1,128)S(1)} %add.201), channel_id=1, source_target_pairs={{48,0},{52,4},{56,8},{60,12},{64,16},{68,20},{72,24},{76,28},{80,3... | collective-permute-start | bytes 3080 | tf_op jit(solution)/shard_map/ppermute | solution.py:292
  78.3 4.5 %collective-permute-start.18 = (f32[1,256]{1,0:T(1,128)S(1)}, f32[1,256]{1,0:T(1,128)S(1)}, u32[]{:S(2)}, u32[]{:S(2)}) collective-permute-start(f32[1,256]{1,0:T(1,128)S(1)} %add.201), channel_id=1, source_target_pairs={{32,0},{36,4},{40,8},{44,12},{48,16},{52,20},{56,24},{60,28},{64,3... | collective-permute-start | bytes 3080 | tf_op jit(solution)/shard_map/ppermute | solution.py:292
  80.0 3.6 %collective-permute-start.17 = (f32[1,256]{1,0:T(1,128)S(1)}, f32[1,256]{1,0:T(1,128)S(1)}, u32[]{:S(2)}, u32[]{:S(2)}) collective-permute-start(f32[1,256]{1,0:T(1,128)S(1)} %add.201), channel_id=1, source_target_pairs={{16,0},{20,4},{24,8},{28,12},{32,16},{36,20},{40,24},{44,28},{48,3... | collective-permute-start | bytes 3080 | tf_op jit(solution)/shard_map/ppermute | solution.py:292
  81.2 14.1 %collective-permute-start.21 = (bf16[256,1024]{1,0:T(8,128)(2,1)S(1)}, bf16[256,1024]{1,0:T(8,128)(2,1)S(1)}, u32[]{:S(2)}, u32[]{:S(2)}) collective-permute-start(bf16[256,1024]{1,0:T(8,128)(2,1)S(1)} %get-tuple-element.133), channel_id=1, source_target_pairs={{0,4},{4,0},{8,12},{12,8},{16,20},{20,16},{24,28},{28,24},{32,36},... | collective-permute-start | bytes 1572872 | tf_op jit(solution)/shard_map/ppermute | solution.py:292
  88.2 25.7 %collective-permute-start.20 = (bf16[256,1024]{1,0:T(8,128)(2,1)S(1)}, bf16[256,1024]{1,0:T(8,128)(2,1)S(1)}, u32[]{:S(2)}, u32[]{:S(2)}) collective-permute-start(bf16[256,1024]{1,0:T(8,128)(2,1)S(1)} %add_convert_fusion), channel_id=1, source_target_pairs={{0,2},{1,3},{2,0},{3,1},{4,6},{5,7},{6,4},{7,5},{8,10},{9,11},{10,... | collective-permute-start | bytes 1572872 | tf_op jit(solution)/shard_map/ppermute | solution.py:295
  89.7 24.2 %collective-permute-start.22 = (bf16[256,1024]{1,0:T(8,128)(2,1)S(1)}, bf16[256,1024]{1,0:T(8,128)(2,1)S(1)}, u32[]{:S(2)}, u32[]{:S(2)}) collective-permute-start(bf16[256,1024]{1,0:T(8,128)(2,1)S(1)} %get-tuple-element.134), channel_id=1, source_target_pairs={{252,0},{248,4},{4,8},{0,12},{12,16},{8,20},{20,24},{16,28},{28,32... | collective-permute-start | bytes 1572872 | tf_op jit(solution)/shard_map/ppermute | solution.py:292
  89.7 13.2 %collective-permute-start.25 = (f32[1,256]{1,0:T(1,128)S(1)}, f32[1,256]{1,0:T(1,128)S(1)}, u32[]{:S(2)}, u32[]{:S(2)}) collective-permute-start(f32[1,256]{1,0:T(1,128)S(1)} %add_add_fusion.1), channel_id=1, source_target_pairs={{192,0},{196,4},{200,8},{204,12},{208,16},{212,20},{216,24},{220,2... | collective-permute-start | bytes 3080 | tf_op jit(solution)/shard_map/ppermute | solution.py:292
  92.6 10.3 %collective-permute-start.24 = (f32[1,256]{1,0:T(1,128)S(1)}, f32[1,256]{1,0:T(1,128)S(1)}, u32[]{:S(2)}, u32[]{:S(2)}) collective-permute-start(f32[1,256]{1,0:T(1,128)S(1)} %add_add_fusion.1), channel_id=1, source_target_pairs={{64,0},{68,4},{72,8},{76,12},{80,16},{84,20},{88,24},{92,28},{96,3... | collective-permute-start | bytes 3080 | tf_op jit(solution)/shard_map/ppermute | solution.py:292
  95.3 16.1 %collective-permute-start.23 = (f32[1,256]{1,0:T(1,128)S(1)}, f32[1,256]{1,0:T(1,128)S(1)}, u32[]{:S(2)}, u32[]{:S(2)}) collective-permute-start(f32[1,256]{1,0:T(1,128)S(1)} %add_add_fusion.1), channel_id=1, source_target_pairs={{128,0},{132,4},{136,8},{140,12},{144,16},{148,20},{152,24},{156,2... | collective-permute-start | bytes 3080 | tf_op jit(solution)/shard_map/ppermute | solution.py:292
